TPU v7x, 32 devices: a whole 2x2x4 slice. The times are simulated.
32 devices in a mesh: replica: 8 (over y, x, core), tensor: 4 (over z).
Axes of the slice: x: 2, y: 2, z: 4, core: 2. Of those that a mesh axis runs over, the one named last changes fastest.
Arguments:
- attention_output: bfloat16 [4, 128, 16384], P(None, 'replica', 'tensor'), may hold values from -6 to 6
- output_weight: bfloat16 [16384, 16384], P('tensor', 'replica'), may hold values from -0.0625 to 0.0625
- adapter_down_weight: bfloat16 [64, 16384, 64], P('replica', 'tensor'), may hold values from -0.046875 to 0.046875
- adapter_up_weight: bfloat16 [64, 64, 16384], P(None, None, ('replica', 'tensor')), may hold values from -0.75 to 0.75
- request_adapter: int32 [128], replicated, may hold values from 0 to 63, as said below
- adapter_storage_row: int32 [64], replicated, may hold values from 0 to 63, as said below
Outputs:
- mixed: bfloat16 [4, 128, 16384], P(None, None, ('replica', 'tensor'))
Inputs may be any that keep to these rules, and one draw needn't show every extreme that they name: `request_adapter`: adapter ids of requests; at most 48 requests use adapters whose storage rows lie on one index of replica (rows q * 8 to (q + 1) * 8 - 1), and one index has exactly 48. `adapter_storage_row`: a permutation: every storage row holds exactly one adapter.
All inputs are finite; a program needn't handle non-finite values.
Results may differ from a plain program's by a relative error of at most 0.0029.
Values may be sent and summed in bfloat16 or wider, within the bound.
No kernel may reach another device: no remote copies, remote signals or barrier semaphores. Data moves between devices by JAX's collectives and lax.ppermute only.
A program may use at most 128 MiB of HBM per device.

v0:
```python
import jax
import jax.numpy as jnp
from jax import lax
from jax.sharding import PartitionSpec as P

OWN_CAP = 48


adapter_scale = 0.5


def on_device(
    attention_output,
    output_weight,
    adapter_down_weight,
    adapter_up_weight,
    request_adapter,
    adapter_storage_row,
):
    replicas = lax.axis_size("replica")
    my_index = lax.axis_index("replica")
    owner_partial = adapter_down_weight.shape[0]
    requests = request_adapter.shape[0]
    everyone = lax.all_gather(attention_output, "replica", axis=1, tiled=True)
    partial_sums = jnp.einsum(
        "sif,fc->sic", everyone, output_weight, preferred_element_type=jnp.float32
    )
    base_output = lax.psum_scatter(partial_sums, "tensor", scatter_dimension=2, tiled=True)
    adapter_ids = jnp.arange(adapter_storage_row.shape[0], dtype=jnp.int32)
    storage_row_of = jnp.sum(
        jnp.where(
            request_adapter[:, None] == adapter_ids[None, :], adapter_storage_row[None, :], 0
        ),
        axis=1,
    )
    owner_of = storage_row_of // owner_partial
    owner_table = owner_of[:, None] == jnp.arange(replicas, dtype=jnp.int32)[None, :]
    running = jnp.cumsum(owner_table.astype(jnp.int32), axis=0) - 1
    rank_in = jnp.sum(jnp.where(owner_table, running, 0), axis=1)
    owned_here = owner_of == my_index
    target = jnp.where(owned_here, rank_in, OWN_CAP)
    chosen = (
        jnp.zeros((OWN_CAP,), jnp.int32)
        .at[target]
        .set(jnp.arange(requests, dtype=jnp.int32), mode="drop")
    )
    filled = jnp.zeros((OWN_CAP,), jnp.int32).at[target].set(1, mode="drop")
    local_slot = storage_row_of[chosen] - my_index * owner_partial
    slot_pick = jnp.where(
        local_slot[:, None] == jnp.arange(owner_partial, dtype=jnp.int32)[None, :],
        filled[:, None],
        0,
    ).astype(jnp.float32)
    selected_rows = everyone[:, chosen, :]
    reduced_input = jnp.einsum(
        "ldu,hun->ldhn", selected_rows, adapter_down_weight, preferred_element_type=jnp.float32
    )
    rank_part = jnp.sum(reduced_input * slot_pick[None, :, :, None], axis=2)
    spread = jnp.where(
        owned_here[None, :, None], rank_part[:, jnp.minimum(rank_in, OWN_CAP - 1), :], 0.0
    )
    rank_full = lax.psum(spread, ("replica", "tensor"))
    rank_values = rank_full.astype(jnp.bfloat16)
    selected_up_rows = adapter_up_weight[storage_row_of]
    adapter_delta = jnp.einsum(
        "ajz,jzt->ajt", rank_values, selected_up_rows, preferred_element_type=jnp.float32
    )
    return (base_output + adapter_scale * adapter_delta).astype(jnp.bfloat16)


def solution(mesh):
    in_specs = (
        P(None, "replica", "tensor"),
        P("tensor", "replica"),
        P("replica", "tensor", None),
        P(None, None, ("replica", "tensor")),
        P(),
        P(),
    )
    out_specs = P(None, None, ("replica", "tensor"))
    return jax.shard_map(
        on_device, mesh=mesh, in_specs=in_specs, out_specs=out_specs, check_vma=False
    )
```

profile of v0, /device:TPU:0, one launch (start us, length us, event | category | flops | bytes accessed | tf_op | source)
XLA Modules:
  0.0 154.8 jit_solution(10231729082682148293)
XLA Ops:
  6.5 0.0 all-gather.2.cloned.1.call-start
  6.5 0.7 all-gather.2.cloned.1.call-update
  7.3 0.0 reduce-scatter.2.cloned.1.call-start
  7.3 41.4 %all-gather.2.cloned.1.call-done = bf16[4,128,4096]{2,1,0:T(8,128)(2,1)} async-done(((bf16[4,16,4096]{2,1,0:T(8,128)(2,1)}), bf16[4,128,4096]{2,1,0:T(8,128)(2,1)}) %all-gather.2.cloned.1.call-update) | async-done | bytes 4194320 | tf_op jit(solution)/shard_map/all_gather | solution.py:24
  48.7 14.9 %fusion = f32[4,128,2048]{2,1,0:T(8,128)} fusion(bf16[4,128,4096]{2,1,0:T(8,128)(2,1)} %all-gather.2.cloned.1.call-done, bf16[4096,2048]{1,0:T(8,128)(2,1)} %param.7), kind=kOutput, calls=%fused_computation.6 | convolution fusion | flops 8589934592 | bytes 25165824 | tf_op jit(solution)/shard_map/sif,fc->sic/dot_general | solution.py:25
  63.6 0.0 reduce-scatter.2.cloned.1.call-update
  63.7 0.6 copy-done
  64.3 0.0 copy-done.1
  64.3 0.1 select_reduce_fusion.1
  64.4 0.1 fusion.18
  64.5 0.2 reduce_window_sum.11
  64.7 0.2 select_reduce_fusion
  64.9 1.0 scatter_custom_fusion.1
  65.9 1.2 scatter_custom_fusion
  67.1 0.8 gather_fusion.2
  67.8 9.1 %gather_fusion = bf16[128,64,512]{2,1,0:T(8,128)(2,1)} fusion(bf16[64,64,512]{2,1,0:T(8,128)(2,1)} %param.9, s32[1024]{0:T(1024)S(1)} %pad_clamp_fusion.2), kind=kCustom, calls=%fused_computation | custom fusion | bytes 16777728 | tf_op jit(solution)/shard_map/gather | solution.py:64
  77.0 7.4 %copy.10 = bf16[4,128,4096]{2,0,1:T(4,128)(2,1)} copy(bf16[4,128,4096]{2,1,0:T(8,128)(2,1)} %all-gather.2.cloned.1.call-done) | data formatting | bytes 8388608 | tf_op jit(solution)/shard_map/all_gather | solution.py:24
  84.3 4.1 %gather_fusion.1 = bf16[48,4,4096]{2,1,0:T(4,128)(2,1)S(1)} fusion(bf16[4,128,4096]{2,0,1:T(4,128)(2,1)} %copy.10, s32[1024]{0:T(1024)S(1)} %pad_clamp_fusion.1), kind=kCustom, calls=%fused_computation.1 | custom fusion | bytes 3145920 | tf_op jit(solution)/shard_map/gather | solution.py:54
  88.5 4.5 %fusion.10 = f32[4,48,64]{2,1,0:T(8,128)S(1)} fusion(bf16[8,4096,64]{1,2,0:T(8,128)(2,1)} %param.8, bf16[4,48,4096,1]{2,0,1,3:T(4,128)(2,1)S(1)} %bitcast.50, f32[48,8]{0,1:T(8,128)S(1)} %select_convert_fusion), kind=kOutput, calls=%fused_computation.12 | convolution fusion | flops 805490688 | bytes 5817856 | tf_op jit(solution)/shard_map/ldu,hun->ldhn/dot_general | solution.py:55
  93.0 0.8 gather_fusion.3
  93.8 0.2 select_bitcast_fusion
  94.0 46.9 %all-reduce.1 = bf16[4,128,64]{2,0,1:T(4,128)(2,1)S(1)} all-reduce(f32[4,128,64]{2,0,1:T(4,128)S(1)} %select_bitcast_fusion), channel_id=1, replica_groups=mesh['replica'=8,'tensor'=4] {'replica','tensor'}, use_global_device_ids=true, to_apply=%region_7.8 | all-reduce | flops 32768 | bytes 196608 | tf_op jit(solution)/shard_map/psum | solution.py:62
  140.9 4.6 %fusion.26 = f32[128,512,4]{1,2,0:T(4,128)S(1)} fusion(bf16[128,64,512]{2,1,0:T(8,128)(2,1)} %gather_fusion, bf16[4,128,64]{2,0,1:T(4,128)(2,1)S(1)} %all-reduce.1), kind=kOutput, calls=%fused_computation.53 | convolution fusion | flops 33554432 | bytes 9502720 | tf_op jit(solution)/shard_map/ajz,jzt->ajt/dot_general | solution.py:65
  145.6 2.4 %fusion.15 = bf16[4,128,512]{2,1,0:T(8,128)(2,1)} fusion(f32[4,128,512]{2,1,0:T(8,128)} %reduce-scatter.2.cloned.1.call-done, f32[128,512,4]{1,2,0:T(4,128)S(1)} %fusion.26), kind=kLoop, calls=%fused_computation.14 | loop fusion | flops 786432 | bytes 2621440 | tf_op jit(solution)/shard_map/convert_element_type | solution.py:68
  (14 shorter events, 0.1 us)
Async XLA Ops:
  6.5 42.2 %all-gather.2.cloned.1.call-start = ((), (), s32[]{:S(2)}) async-start(), calls=%async_computation.1 | async-start | bytes 4718592 | tf_op jit(solution)/shard_map/all_gather | solution.py:24
  7.3 138.3 %reduce-scatter.2.cloned.1.call-start = ((), (), s32[]{:S(2)}) async-start(), calls=%async_computation.2 | async-start | bytes 5242880 | tf_op jit(solution)/shard_map/reduce_scatter | solution.py:28
  63.6 0.7 copy-start
  63.6 0.7 copy-start.1
Sparse Core Ops, SparseCore 0:
  9.3 39.4 all-gather.1
  63.8 77.7 reduce-scatter.1
where the time goes:
time: 155 us
  blocking collectives  46.9 us (30%)
  waiting for transfers between devices  42.1 us (27%)
  local copies, waits for them, and re-layouts  24.9 us (16%)
  matrix products  24.1 us (16%)
  between operations  13.5 us (9%)
  other arithmetic  3.15 us (2%)
    psum x1, blocking collectives, on_device(): rank_full = lax.psum(spread, ('replica', 'tensor'))  46.9 us
    all_gather x1, waiting for transfers between devices, on_device(): everyone = lax.all_gather(attention_output, 'replica', axis=1, tiled=True)  41.4 us
    dot_general x1, matrix products, on_device(): jnp.einsum('sif,fc->sic', everyone, output_weight, preferred_element_type...  14.9 us
    gather x1, local copies, waits for them, and re-layouts, on_device(): selected_up_rows = adapter_up_weight[storage_row_of]  9.09 us
    all_gather x1, local copies, waits for them, and re-layouts, on_device(): everyone = lax.all_gather(attention_output, 'replica', axis=1, tiled=True)  7.35 us
    dot_general x1, matrix products, on_device(): jnp.einsum('ajz,jzt->ajt', rank_values, selected_up_rows, preferred_eleme...  4.62 us
    dot_general x1, matrix products, on_device(): jnp.einsum('ldu,hun->ldhn', selected_rows, adapter_down_weight, preferred...  4.53 us
    gather x1, local copies, waits for them, and re-layouts, on_device(): selected_rows = everyone[:, chosen, :]  4.13 us
  transfers between devices with their start and end apart: 2, of which 1 were waited for; matrix products, arithmetic and copies ran while one was open for 22% of the time, Pallas kernels for 0%

commit v1 on v0

--- a/solution.py
+++ b/solution.py
@@ -1,12 +1,284 @@
+import functools
+
 import jax
 import jax.numpy as jnp
 from jax import lax
+from jax.experimental import pallas as pl
+from jax.experimental.pallas import tpu as pltpu
 from jax.sharding import PartitionSpec as P
 
 OWN_CAP = 48
 
 
 adapter_scale = 0.5
+
+MIB = 2**20
+VMEM = pl.BlockSpec(memory_space=pltpu.VMEM)
+
+
+def params(mib):
+    return pltpu.CompilerParams(vmem_limit_bytes=mib * MIB)
+
+
+def stack_rows(parts, rows_ref):
+    at = 0
+    for part in parts:
+        steps, requests, feats = part.shape
+        rows_ref[pl.ds(at, steps * requests), :] = part[...].reshape(steps * requests, feats)
+        at += steps * requests
+
+
+def column_dot(rows_ref, weight_ref, chunk, store, cols, width):
+    for at in range(0, cols, width):
+        off = pl.multiple_of(chunk * cols + at, width)
+        store(
+            pl.ds(at, width),
+            jnp.dot(rows_ref[...], weight_ref[:, pl.ds(off, width)], preferred_element_type=jnp.float32),
+        )
+
+
+def base_out_kernel(n, *refs):
+    parts, weight, near, rows = refs[:n], refs[n], refs[n + 1], refs[n + 2]
+    cols = near.shape[-1]
+    mine = lax.axis_index("tensor")
+    stack_rows(parts, rows)
+    for slot, flip in enumerate((1, 3)):
+
+        def store(where, value, slot=slot):
+            near[slot, :, where] = value.astype(near.dtype)
+
+        column_dot(rows, weight, mine ^ flip, store, cols, 256)
+
+
+def base_in_kernel(n, *refs):
+    parts, weight, far, own, rows = refs[:n], refs[n], refs[n + 1], refs[n + 2], refs[n + 3]
+    cols = own.shape[-1]
+    mine = lax.axis_index("tensor")
+    stack_rows(parts, rows)
+    for flip, out in ((2, far), (0, own)):
+
+        def store(where, value, out=out):
+            out[:, where] = value
+
+        column_dot(rows, weight, mine ^ flip, store, cols, 256)
+
+
+def rank_kernel(order, n, *refs):
+    parts, down, slot, place = refs[:n], refs[n], refs[n + 1], refs[n + 2]
+    out, rows = refs[n + 3], refs[n + 4]
+    me = lax.axis_index("replica")
+    adapters, rank = down.shape[0], down.shape[1]
+    feats = down.shape[2]
+    steps = 4
+    for (k, first), part in zip(order, parts):
+        count = part.shape[0] * part.shape[1]
+        whole = steps * part.shape[1]
+        at = pl.multiple_of((me ^ k) * whole + first * part.shape[1], part.shape[1])
+        rows[pl.ds(at, count), :] = part[...].reshape(count, feats)
+    total = rows.shape[0]
+    reduced = lax.dot_general(
+        rows[...],
+        down[...].reshape(adapters * rank, feats),
+        (((1,), (1,)), ((), ())),
+        preferred_element_type=jnp.float32,
+    )
+    local = slot[...] - me * adapters
+    adapter_of = lax.broadcasted_iota(jnp.int32, (total, adapters * rank), 1) // rank
+    picked = jnp.where(adapter_of == local, reduced, 0.0)
+    width = adapters * rank
+    while width > rank:
+        width //= 2
+        picked = picked[:, :width] + picked[:, width:]
+    packed = steps * OWN_CAP
+    where = place[...] - me * packed
+    chosen = (lax.broadcasted_iota(jnp.int32, (packed, total), 0) == where).astype(jnp.float32)
+    packed_rank = jnp.dot(
+        chosen, picked, preferred_element_type=jnp.float32, precision=lax.Precision.HIGHEST
+    )
+    half = packed // 2
+    out[...] = jnp.concatenate([packed_rank[:half], packed_rank[half:]], axis=1)
+
+
+def up_kernel(packed_rank, up, slot, column, out):
+    total = slot.shape[0]
+    adapters, rank, cols = up.shape
+    owners, held, _ = packed_rank.shape
+    chosen = (
+        lax.broadcasted_iota(jnp.int32, (total, owners * held), 1) == column[...]
+    ).astype(jnp.bfloat16)
+    both = jnp.dot(
+        chosen, packed_rank[...].reshape(owners * held, 2 * rank), preferred_element_type=jnp.float32
+    )
+    late = (lax.broadcasted_iota(jnp.int32, (total, rank), 0) // 32) % 2
+    rank_rows = jnp.where(late == 1, both[:, rank:], both[:, :rank])
+    group = 8
+    wide = jnp.concatenate([rank_rows] * group, axis=1).astype(jnp.bfloat16)
+    adapter_of = lax.broadcasted_iota(jnp.int32, (total, group * rank), 1) // rank
+    local = slot[...] - adapter_of
+    out[...] = jnp.zeros_like(out)
+
+    def step(g, carry):
+        spread = jnp.where(local == g * group, wide, jnp.zeros_like(wide))
+        weight = up[pl.ds(g * group, group)].reshape(group * rank, cols)
+        out[...] += jnp.dot(spread, weight, preferred_element_type=jnp.float32)
+        return carry
+
+    lax.fori_loop(0, adapters // group, step, 0)
+    out[...] = adapter_scale * out[...]
+
+
+def finish_kernel(pieces, *refs):
+    out, delta = refs[-1], refs[-2]
+    steps, _, cols = out.shape
+    me = lax.axis_index("replica")
+    at = 0
+    for order in pieces:
+        own, near, far, mid = refs[at : at + 4]
+        at += 4
+        rows = own.shape[0] // len(order)
+        requests = rows // steps
+        for i, k in enumerate(order):
+            here = pl.ds(i * rows, rows)
+            who = me ^ k
+            total = own[here, :] + near[0, here, :].astype(jnp.float32)
+            total += far[here, :].astype(jnp.float32) + mid[here, :].astype(jnp.float32)
+            total += delta[pl.ds(pl.multiple_of(who * rows, rows), rows), :]
+            out[:, pl.ds(pl.multiple_of(who * requests, requests), requests), :] = total.astype(
+                out.dtype
+            ).reshape(steps, requests, cols)
+
+
+def flip(size, bits):
+    return [(i, i ^ bits) for i in range(size)]
+
+
+def on_device_blocks(
+    attention_output,
+    output_weight,
+    adapter_down_weight,
+    adapter_up_weight,
+    request_adapter,
+    adapter_storage_row,
+):
+    replicas = lax.axis_size("replica")
+    steps, own_requests, feats = attention_output.shape
+    tensors = lax.axis_size("tensor")
+    cols = output_weight.shape[1] // tensors
+    adapters_here = adapter_down_weight.shape[0]
+    requests = request_adapter.shape[0]
+    mine = lax.axis_index("tensor")
+    inner = (mine == 1) | (mine == 2)
+
+    def swap(value, bits):
+        return lax.ppermute(value, "replica", flip(replicas, bits))
+
+    half = steps // 2
+    x0 = attention_output
+    x1 = swap(x0, 1)
+    x2 = swap(x0, 2)
+    x4 = swap(x0, 4)
+    x3 = swap(x2, 1)
+    x5 = swap(x4, 1)
+    x6a = swap(x2[:half], 4)
+    x6b = swap(x4[half:], 2)
+    x7a = swap(x6a, 1)
+    x7b = swap(x6b, 1)
+
+    adapter_ids = jnp.arange(adapter_storage_row.shape[0], dtype=jnp.int32)
+    slot_of = jnp.sum(
+        jnp.where(request_adapter[:, None] == adapter_ids[None, :], adapter_storage_row[None, :], 0),
+        axis=1,
+    )
+    owner_of = slot_of // adapters_here
+    index = jnp.arange(requests, dtype=jnp.int32)
+    rank_in = jnp.sum(
+        ((owner_of[:, None] == owner_of[None, :]) & (index[None, :] < index[:, None])).astype(jnp.int32),
+        axis=1,
+    )
+
+    def by_row(per_request, per_step):
+        grid = per_request.reshape(replicas, 1, own_requests) + per_step.reshape(1, steps, 1)
+        return grid.reshape(replicas * steps * own_requests)
+
+    step = jnp.arange(steps, dtype=jnp.int32)
+    slot_rows = by_row(slot_of, 0 * step)[:, None]
+    place_rows = by_row(owner_of * (steps * OWN_CAP) + rank_in, step * OWN_CAP)[None, :]
+    column_rows = by_row(owner_of * (half * OWN_CAP) + rank_in, (step % half) * OWN_CAP)[:, None]
+
+    def base(parts):
+        rows = sum(p.shape[0] * p.shape[1] for p in parts)
+        n = len(parts)
+        scratch = [pltpu.VMEM((rows, feats), jnp.bfloat16)]
+        cost = pl.CostEstimate(flops=4 * rows * feats * cols, bytes_accessed=4 * rows * feats, transcendentals=0)
+        near = pl.pallas_call(
+            functools.partial(base_out_kernel, n),
+            out_shape=jax.ShapeDtypeStruct((2, rows, cols), jnp.bfloat16),
+            in_specs=[VMEM] * (n + 1),
+            out_specs=VMEM,
+            scratch_shapes=scratch,
+            compiler_params=params(16),
+            cost_estimate=cost,
+        )(*parts, output_weight)
+        near_in = lax.ppermute(near, "tensor", flip(tensors, 1))
+        mid_in = lax.ppermute(near[1], "tensor", [(1, 2), (2, 1)])
+        far, own = pl.pallas_call(
+            functools.partial(base_in_kernel, n),
+            out_shape=[jax.ShapeDtypeStruct((rows, cols), jnp.float32)] * 2,
+            in_specs=[VMEM] * (n + 1),
+            out_specs=[VMEM, VMEM],
+            scratch_shapes=scratch,
+            compiler_params=params(16),
+            cost_estimate=cost,
+        )(*parts, output_weight)
+        passed = (far + jnp.where(inner, near_in[1].astype(jnp.float32), 0.0)).astype(jnp.bfloat16)
+        far_in = lax.ppermute(passed, "tensor", flip(tensors, 2))
+        return own, near_in, far_in, mid_in
+
+    first = base([x0, x1])
+    second = base([x2, x3, x4, x5])
+
+    order = [(0, 0), (1, 0), (2, 0), (3, 0), (4, 0), (5, 0), (6, 0), (6, half), (7, 0), (7, half)]
+    parts = [x0, x1, x2, x3, x4, x5, x6a, x6b, x7a, x7b]
+    total_rows = replicas * steps * own_requests
+    down = jnp.transpose(adapter_down_weight, (0, 2, 1))
+    rank = down.shape[1]
+    packed = pl.pallas_call(
+        functools.partial(rank_kernel, order, len(parts)),
+        out_shape=jax.ShapeDtypeStruct((half * OWN_CAP, 2 * rank), jnp.float32),
+        in_specs=[VMEM] * (len(parts) + 3),
+        out_specs=VMEM,
+        scratch_shapes=[pltpu.VMEM((total_rows, feats), jnp.bfloat16)],
+        compiler_params=params(20),
+        cost_estimate=pl.CostEstimate(
+            flops=2 * total_rows * feats * adapters_here * rank, bytes_accessed=4 * MIB, transcendentals=0
+        ),
+    )(*parts, down, slot_rows, place_rows)
+    gathered = packed
+    for bits in (1, 2, 3):
+        gathered = gathered + lax.ppermute(packed, "tensor", flip(tensors, bits))
+    third = base([x6a, x6b, x7a, x7b])
+    ranks = lax.all_gather(gathered.astype(jnp.bfloat16), "replica", axis=0)
+    delta = pl.pallas_call(
+        up_kernel,
+        out_shape=jax.ShapeDtypeStruct((total_rows, cols), jnp.float32),
+        in_specs=[VMEM] * 4,
+        out_specs=VMEM,
+        compiler_params=params(20),
+        cost_estimate=pl.CostEstimate(
+            flops=2 * total_rows * cols * adapter_up_weight.shape[0] * rank,
+            bytes_accessed=4 * MIB,
+            transcendentals=0,
+        ),
+    )(ranks, adapter_up_weight, slot_rows, column_rows)
+
+    pieces = [(0, 1), (2, 3, 4, 5), (6, 7)]
+    return pl.pallas_call(
+        functools.partial(finish_kernel, pieces),
+        out_shape=jax.ShapeDtypeStruct((steps, requests, cols), jnp.bfloat16),
+        in_specs=[VMEM] * 13,
+        out_specs=VMEM,
+        compiler_params=params(16),
+    )(*first, *second, *third, delta)
 
 
 def on_device(
@@ -78,6 +350,11 @@
         P(),
     )
     out_specs = P(None, None, ("replica", "tensor"))
+    blocks = mesh.shape["replica"] == 8 and mesh.shape["tensor"] == 4
     return jax.shard_map(
-        on_device, mesh=mesh, in_specs=in_specs, out_specs=out_specs, check_vma=False
-    )
+        on_device_blocks if blocks else on_device,
+        mesh=mesh,
+        in_specs=in_specs,
+        out_specs=out_specs,
+        check_vma=False,
+    )

time: 155 us -> 97.1 us (0.63)
  blocking collectives: 46.9 us -> 9.28 us
  starting transfers between devices: 0.04 us -> 27.1 us
  matrix products: 24.1 us -> 0 us
  Pallas kernels: 0 us -> 19.1 us
  local copies, waits for them, and re-layouts: 24.9 us -> 7.5 us
  between operations: 13.5 us -> 0.38 us
  waiting for transfers between devices: 42.1 us -> 32.2 us
  other arithmetic: 3.15 us -> 1.29 us
    psum x1 -> x0, blocking collectives: 46.9 us -> none  [on_device(): rank_full = lax.psum(spread, ('replica', 'tensor'))]
    all_gather x1 -> x0, waiting for transfers between devices: 41.4 us -> none  [on_device(): everyone = lax.all_gather(attention_output, 'replica', axis=1, tiled=True)]
    ppermute x0 -> x21, waiting for transfers between devices: none -> 32.2 us  [the longest x3 18.8 us: base(): far_in = lax.ppermute(passed, 'tensor', flip(tensors, 2))]
    ppermute x0 -> x21, starting transfers between devices: none -> 27.1 us  [the longest x9 7.98 us: swap(): return lax.ppermute(value, 'replica', flip(replicas, bits))]
    dot_general x3 -> x0, matrix products: 24.1 us -> none  [the longest x1 14.9 us: on_device(): jnp.einsum('sif,fc->sic', everyone, output_weight, preferred_element_type...]
    pallas_call x0 -> x9, Pallas kernels: none -> 19.1 us  [the longest x3 5.12 us: base(): pl.pallas_call(functools.partial(base_out_kernel, n), out_shape=jax.Shape...]
    gather x4 -> x0, local copies, waits for them, and re-layouts: 14.7 us -> none  [the longest x1 9.09 us: on_device(): selected_up_rows = adapter_up_weight[storage_row_of]]
    all_gather x0 -> x1, blocking collectives: none -> 9.28 us  [on_device_blocks(): ranks = lax.all_gather(gathered.astype(jnp.bfloat16), 'replica', axis=0)]
  transfers between devices with their start and end apart: 2 -> 21, of which waited for: 1 -> 5; matrix products, arithmetic and copies ran while one was open for 22% -> 2% of each run, Pallas kernels for 0% -> 19%
where the time goes in v1:
time: 97.1 us; the launch traced here: 96.8 us
  waiting for transfers between devices  32.2 us (33%)
  starting transfers between devices  27.1 us (28%)
  Pallas kernels  19.1 us (20%)
  blocking collectives  9.28 us (10%)
  local copies, waits for them, and re-layouts  7.5 us (8%)
  other arithmetic  1.29 us (1%)
    ppermute x3, waiting for transfers between devices, base(): far_in = lax.ppermute(passed, 'tensor', flip(tensors, 2))  18.8 us
    ppermute x9, waiting for transfers between devices, swap(): return lax.ppermute(value, 'replica', flip(replicas, bits))  9.82 us
    all_gather x1, blocking collectives, on_device_blocks(): ranks = lax.all_gather(gathered.astype(jnp.bfloat16), 'replica', axis=0)  9.28 us
    ppermute x9, starting transfers between devices, swap(): return lax.ppermute(value, 'replica', flip(replicas, bits))  7.98 us
    unnamed x18, local copies, waits for them, and re-layouts  6.85 us
    ppermute x3, starting transfers between devices, on_device_blocks(): gathered = gathered + lax.ppermute(packed, 'tensor', flip(tensors, bits))  6.02 us
    ppermute x3, starting transfers between devices, base(): far_in = lax.ppermute(passed, 'tensor', flip(tensors, 2))  5.94 us
    pallas_call x3, Pallas kernels, base(): pl.pallas_call(functools.partial(base_out_kernel, n), out_shape=jax.Shape...  5.12 us
  transfers between devices with their start and end apart: 21, of which 5 were waited for; matrix products, arithmetic and copies ran while one was open for 2% of the time, Pallas kernels for 19%

profile of v1, /device:TPU:0, one launch (start us, length us, event | category | flops | bytes accessed | tf_op | source)
XLA Modules:
  0.0 96.8 jit_solution(17192996805735673364)
XLA Ops:
  0.0 2.9 %collective-permute-start.4 = (bf16[4,16,4096]{2,1,0:T(8,128)(2,1)}, bf16[4,16,4096]{2,1,0:T(8,128)(2,1)S(1)}, u32[]{:S(2)}, u32[]{:S(2)}) collective-permute-start(bf16[4,16,4096]{2,1,0:T(8,128)(2,1)} %refs_0_.5), channel_id=1, source_target_pairs={{0,8},{4,12},{8,0},{12,4},{16,24},{20,28},{24,16},{28,20},{1,9},{5... | collective-permute-start | bytes 1572872 | tf_op jit(solution)/shard_map/ppermute | solution.py:173
  2.9 1.5 %collective-permute-start.6 = (bf16[4,16,4096]{2,1,0:T(8,128)(2,1)}, bf16[4,16,4096]{2,1,0:T(8,128)(2,1)S(1)}, u32[]{:S(2)}, u32[]{:S(2)}) collective-permute-start(bf16[4,16,4096]{2,1,0:T(8,128)(2,1)} %refs_0_.5), channel_id=1, source_target_pairs={{0,16},{4,20},{8,24},{12,28},{16,0},{20,4},{24,8},{28,12},{1,17},{... | collective-permute-start | bytes 1572872 | tf_op jit(solution)/shard_map/ppermute | solution.py:173
  6.2 8.9 %collective-permute-done.4.refs_0_.refs_2_ = bf16[4,16,4096]{2,1,0:T(8,128)(2,1)S(1)} collective-permute-done((bf16[4,16,4096]{2,1,0:T(8,128)(2,1)}, bf16[4,16,4096]{2,1,0:T(8,128)(2,1)S(1)}, u32[]{:S(2)}, u32[]{:S(2)}) %collective-permute-start.4) | collective-permute-done | bytes 524320 | tf_op jit(solution)/shard_map/ppermute | solution.py:173
  15.1 1.8 %collective-permute-start.11 = (bf16[2,16,4096]{2,1,0:T(8,128)(2,1)S(1)}, bf16[2,16,4096]{2,1,0:T(8,128)(2,1)S(1)}, u32[]{:S(2)}, u32[]{:S(2)}) collective-permute-start(bf16[2,16,4096]{2,1,0:T(8,128)(2,1)S(1)} %slice.36), channel_id=1, source_target_pairs={{0,16},{4,20},{8,24},{12,28},{16,0},{20,4},{24,8},{28,12},{1,17},{... | collective-permute-start | bytes 786440 | tf_op jit(solution)/shard_map/ppermute | solution.py:173
  18.5 5.8 %copy-done = bf16[4096,2048]{1,0:T(8,128)(2,1)S(1)} copy-done((bf16[4096,2048]{1,0:T(8,128)(2,1)S(1)}, bf16[4096,2048]{1,0:T(8,128)(2,1)}, u32[]{:S(2)}) %copy-start) | copy-done | bytes 16777240
  24.3 1.0 %copy-done.1 = bf16[4,16,4096]{2,1,0:T(8,128)(2,1)S(1)} copy-done((bf16[4,16,4096]{2,1,0:T(8,128)(2,1)S(1)}, bf16[4,16,4096]{2,1,0:T(8,128)(2,1)}, u32[]{:S(2)}) %copy-start.1) | copy-done | bytes 524312
  25.3 1.4 %shard_map.65 = bf16[2,128,512]{2,1,0:T(8,128)(2,1)S(1)} custom-call(bf16[4,16,4096]{2,1,0:T(8,128)(2,1)S(1)} %copy-done.1, bf16[4,16,4096]{2,1,0:T(8,128)(2,1)S(1)} %collective-permute-done.refs_1_, bf16[4096,2048]{1,0:T(8,128)(2,1)S(1)} %copy-done), custom_call_target="tpu_custom_call" | custom-call | flops 1073741824 | bytes 2097152 | tf_op jit(solution)/shard_map/pallas_call | solution.py:213
  26.7 1.6 %collective-permute-start.1 = (bf16[2,128,512]{2,1,0:T(8,128)(2,1)S(1)}, bf16[2,128,512]{2,1,0:T(8,128)(2,1)S(1)}, u32[]{:S(2)}, u32[]{:S(2)}) collective-permute-start(bf16[2,128,512]{2,1,0:T(8,128)(2,1)S(1)} %shard_map.65), channel_id=1, source_target_pairs={{0,1},{1,0},{2,3},{3,2},{4,5},{5,4},{6,7},{7,6},{8,9},{9,8},{10,11... | collective-permute-start | bytes 786440 | tf_op jit(solution)/shard_map/ppermute | solution.py:222
  29.5 1.4 %shard_map.64 = (f32[128,512]{1,0:T(8,128)S(1)}, f32[128,512]{1,0:T(8,128)S(1)}) custom-call(bf16[4,16,4096]{2,1,0:T(8,128)(2,1)S(1)} %copy-done.1, bf16[4,16,4096]{2,1,0:T(8,128)(2,1)S(1)} %collective-permute-done.refs_1_, bf16[4096,2048]{1,0:T(8,128)(2,1)S(1)} %copy-done), custom_call_target="tpu_custom_call" | custom-call | flops 1073741824 | bytes 2097152 | tf_op jit(solution)/shard_map/pallas_call | solution.py:224
  30.9 3.1 %collective-permute-done.1.refs_1_ = bf16[2,128,512]{2,1,0:T(8,128)(2,1)S(1)} collective-permute-done((bf16[2,128,512]{2,1,0:T(8,128)(2,1)S(1)}, bf16[2,128,512]{2,1,0:T(8,128)(2,1)S(1)}, u32[]{:S(2)}, u32[]{:S(2)}) %collective-permute-start.1) | collective-permute-done | bytes 262176 | tf_op jit(solution)/shard_map/ppermute | solution.py:222
  34.9 3.6 %shard_map.70 = f32[96,128]{1,0:T(8,128)S(1)} custom-call(bf16[4,16,4096]{2,1,0:T(8,128)(2,1)S(1)} %copy-done.2, bf16[4,16,4096]{2,1,0:T(8,128)(2,1)S(1)} %collective-permute-done.refs_1_, bf16[4,16,4096]{2,1,0:T(8,128)(2,1)S(1)} %collective-permute-done.4.refs_0_.refs_2_, bf16[4,16,4096]{2,1,0:T(8,128)(2,1)S(1)} %collective-permute-done.5.refs_1_.refs_3_, ...), custom_call_target="tpu_custom_call" | custom-call | flops 2147483648 | bytes 4194304 | tf_op jit(solution)/shard_map/pallas_call | solution.py:245
  38.5 3.7 %collective-permute-start.20 = (f32[96,128]{1,0:T(8,128)S(1)}, f32[96,128]{1,0:T(8,128)S(1)}, u32[]{:S(2)}, u32[]{:S(2)}) collective-permute-start(f32[96,128]{1,0:T(8,128)S(1)} %shard_map.70), channel_id=1, source_target_pairs={{0,3},{1,2},{2,1},{3,0},{4,7},{5,6},{6,5},{7,4},{8,11},{9,10},{10,... | collective-permute-start | bytes 147464 | tf_op jit(solution)/shard_map/ppermute | solution.py:258
  42.3 2.3 %collective-permute-start.19 = (f32[96,128]{1,0:T(8,128)S(1)}, f32[96,128]{1,0:T(8,128)S(1)}, u32[]{:S(2)}, u32[]{:S(2)}) collective-permute-start(f32[96,128]{1,0:T(8,128)S(1)} %shard_map.70), channel_id=1, source_target_pairs={{0,2},{1,3},{2,0},{3,1},{4,6},{5,7},{6,4},{7,5},{8,10},{9,11},{10,... | collective-permute-start | bytes 147464 | tf_op jit(solution)/shard_map/ppermute | solution.py:258
  44.6 2.4 %shard_map.67 = bf16[2,256,512]{2,1,0:T(8,128)(2,1)S(1)} custom-call(bf16[4,16,4096]{2,1,0:T(8,128)(2,1)S(1)} %collective-permute-done.4.refs_0_.refs_2_, bf16[4,16,4096]{2,1,0:T(8,128)(2,1)S(1)} %collective-permute-done.5.refs_1_.refs_3_, bf16[4,16,4096]{2,1,0:T(8,128)(2,1)S(1)} %collective-permute-done.6.refs_2_.refs_4_, ...), custom_call_target="tpu_custom_call" | custom-call | flops 2147483648 | bytes 4194304 | tf_op jit(solution)/shard_map/pallas_call | solution.py:213
  47.0 2.1 %collective-permute-start.8 = (bf16[2,256,512]{2,1,0:T(8,128)(2,1)S(1)}, bf16[2,256,512]{2,1,0:T(8,128)(2,1)S(1)}, u32[]{:S(2)}, u32[]{:S(2)}) collective-permute-start(bf16[2,256,512]{2,1,0:T(8,128)(2,1)S(1)} %shard_map.67), channel_id=1, source_target_pairs={{0,1},{1,0},{2,3},{3,2},{4,5},{5,4},{6,7},{7,6},{8,9},{9,8},{10,11... | collective-permute-start | bytes 1572872 | tf_op jit(solution)/shard_map/ppermute | solution.py:222
  49.1 1.4 %shard_map.69 = bf16[2,128,512]{2,1,0:T(8,128)(2,1)S(1)} custom-call(bf16[2,16,4096]{2,1,0:T(8,128)(2,1)S(1)} %collective-permute-done.11.refs_0_.refs_6_, bf16[2,16,4096]{2,1,0:T(8,128)(2,1)S(1)} %collective-permute-done.12.refs_1_.refs_7_, bf16[2,16,4096]{2,1,0:T(8,128)(2,1)S(1)} %collective-permute-done.13.refs_2_.refs_8_, ...), custom_call_target="tpu_custom_call" | custom-call | flops 1073741824 | bytes 2097152 | tf_op jit(solution)/shard_map/pallas_call | solution.py:213
  50.4 2.4 %shard_map.66 = (f32[256,512]{1,0:T(8,128)S(1)}, f32[256,512]{1,0:T(8,128)S(1)}) custom-call(bf16[4,16,4096]{2,1,0:T(8,128)(2,1)S(1)} %collective-permute-done.4.refs_0_.refs_2_, bf16[4,16,4096]{2,1,0:T(8,128)(2,1)S(1)} %collective-permute-done.5.refs_1_.refs_3_, bf16[4,16,4096]{2,1,0:T(8,128)(2,1)S(1)} %collective-permute-done.6.refs_2_.refs_4_, ...), custom_call_target="tpu_custom_call" | custom-call | flops 2147483648 | bytes 4194304 | tf_op jit(solution)/shard_map/pallas_call | solution.py:224
  52.9 1.4 %shard_map.68 = (f32[128,512]{1,0:T(8,128)S(1)}, f32[128,512]{1,0:T(8,128)S(1)}) custom-call(bf16[2,16,4096]{2,1,0:T(8,128)(2,1)S(1)} %collective-permute-done.11.refs_0_.refs_6_, bf16[2,16,4096]{2,1,0:T(8,128)(2,1)S(1)} %collective-permute-done.12.refs_1_.refs_7_, bf16[2,16,4096]{2,1,0:T(8,128)(2,1)S(1)} %collective-permute-done.13.refs_2_.refs_8_, ...), custom_call_target="tpu_custom_call" | custom-call | flops 1073741824 | bytes 2097152 | tf_op jit(solution)/shard_map/pallas_call | solution.py:224
  54.9 1.3 %collective-permute-start.15 = (bf16[2,128,512]{2,1,0:T(8,128)(2,1)S(1)}, bf16[2,128,512]{2,1,0:T(8,128)(2,1)S(1)}, u32[]{:S(2)}, u32[]{:S(2)}) collective-permute-start(bf16[2,128,512]{2,1,0:T(8,128)(2,1)S(1)} %shard_map.69), channel_id=1, source_target_pairs={{0,1},{1,0},{2,3},{3,2},{4,5},{5,4},{6,7},{7,6},{8,9},{9,8},{10,11... | collective-permute-start | bytes 786440 | tf_op jit(solution)/shard_map/ppermute | solution.py:222
  56.9 9.3 %all-gather = bf16[768,128]{1,0:T(8,128)(2,1)S(1)} all-gather(bf16[96,128]{1,0:T(8,128)(2,1)S(1)} %add_convert_fusion), channel_id=2, replica_groups=mesh['replica'=8,'tensor'=4] {'replica'}, dimensions={0}, use_global_device_ids=true | all-gather | bytes 221184 | tf_op jit(solution)/shard_map/all_gather | solution.py:260
  67.4 5.1 %collective-permute-start.9 = (bf16[256,512]{1,0:T(8,128)(2,1)S(1)}, bf16[256,512]{1,0:T(8,128)(2,1)S(1)}, u32[]{:S(2)}, u32[]{:S(2)}) collective-permute-start(bf16[256,512]{1,0:T(8,128)(2,1)S(1)} %fusion), channel_id=1, source_target_pairs={{0,2},{1,3},{2,0},{3,1},{4,6},{5,7},{6,4},{7,5},{8,10},{9,11},{10,... | collective-permute-start | bytes 786440 | tf_op jit(solution)/shard_map/ppermute | solution.py:234
  72.7 4.2 %shard_map.71.refs_12_ = f32[512,512]{1,0:T(8,128)S(1)} custom-call(bf16[8,96,128]{2,1,0:T(8,128)(2,1)S(1)} %bitcast.23, bf16[64,64,512]{2,1,0:T(8,128)(2,1)S(1)} %copy-done.4, s32[512,1]{1,0:T(8,128)S(1)} %broadcast_in_dim_reshape.6.refs_11_.slot, s32[512,1]{1,0:T(8,128)S(1)} %add.130.column), custom_call_target="tpu_custom_call" | custom-call | flops 2147483648 | bytes 4194304 | tf_op jit(solution)/shard_map/pallas_call | solution.py:261
  77.0 18.8 %collective-permute-done.16.refs_10_ = bf16[128,512]{1,0:T(8,128)(2,1)S(1)} collective-permute-done((bf16[128,512]{1,0:T(8,128)(2,1)S(1)}, bf16[128,512]{1,0:T(8,128)(2,1)S(1)}, u32[]{:S(2)}, u32[]{:S(2)}) %collective-permute-start.16) | collective-permute-done | bytes 131104 | tf_op jit(solution)/shard_map/ppermute | solution.py:234
  95.8 1.1 %shard_map.72 = bf16[4,128,512]{2,1,0:T(8,128)(2,1)} custom-call(f32[128,512]{1,0:T(8,128)S(1)} %get-tuple-element.11.refs_0_, bf16[2,128,512]{2,1,0:T(8,128)(2,1)S(1)} %collective-permute-done.1.refs_1_, bf16[128,512]{1,0:T(8,128)(2,1)S(1)} %collective-permute-done.2.refs_2_, bf16[128,512]{1,0:T(8,128)(2,1)S(1)} %collective-permute-done.3.refs_3_, ...), custom_call_target="tpu_custom_call" | custom-call | tf_op jit(solution)/shard_map/pallas_call | solution.py:275
  (70 shorter events, 8.1 us)
Async XLA Ops:
  0.0 15.1 %collective-permute-start.4 = (bf16[4,16,4096]{2,1,0:T(8,128)(2,1)}, bf16[4,16,4096]{2,1,0:T(8,128)(2,1)S(1)}, u32[]{:S(2)}, u32[]{:S(2)}) collective-permute-start(bf16[4,16,4096]{2,1,0:T(8,128)(2,1)} %refs_0_.5), channel_id=1, source_target_pairs={{0,8},{4,12},{8,0},{12,4},{16,24},{20,28},{24,16},{28,20},{1,9},{5... | collective-permute-start | bytes 1572872 | tf_op jit(solution)/shard_map/ppermute | solution.py:173
  2.9 15.6 %collective-permute-start = (bf16[4,16,4096]{2,1,0:T(8,128)(2,1)}, bf16[4,16,4096]{2,1,0:T(8,128)(2,1)S(1)}, u32[]{:S(2)}, u32[]{:S(2)}) collective-permute-start(bf16[4,16,4096]{2,1,0:T(8,128)(2,1)} %refs_0_.5), channel_id=1, source_target_pairs={{0,4},{4,0},{8,12},{12,8},{16,20},{20,16},{24,28},{28,24},{1,5},{5... | collective-permute-start | bytes 1572872 | tf_op jit(solution)/shard_map/ppermute | solution.py:173
  2.9 14.9 %collective-permute-start.6 = (bf16[4,16,4096]{2,1,0:T(8,128)(2,1)}, bf16[4,16,4096]{2,1,0:T(8,128)(2,1)S(1)}, u32[]{:S(2)}, u32[]{:S(2)}) collective-permute-start(bf16[4,16,4096]{2,1,0:T(8,128)(2,1)} %refs_0_.5), channel_id=1, source_target_pairs={{0,16},{4,20},{8,24},{12,28},{16,0},{20,4},{24,8},{28,12},{1,17},{... | collective-permute-start | bytes 1572872 | tf_op jit(solution)/shard_map/ppermute | solution.py:173
  15.1 13.8 %collective-permute-start.11 = (bf16[2,16,4096]{2,1,0:T(8,128)(2,1)S(1)}, bf16[2,16,4096]{2,1,0:T(8,128)(2,1)S(1)}, u32[]{:S(2)}, u32[]{:S(2)}) collective-permute-start(bf16[2,16,4096]{2,1,0:T(8,128)(2,1)S(1)} %slice.36), channel_id=1, source_target_pairs={{0,16},{4,20},{8,24},{12,28},{16,0},{20,4},{24,8},{28,12},{1,17},{... | collective-permute-start | bytes 786440 | tf_op jit(solution)/shard_map/ppermute | solution.py:173
  17.9 11.1 %collective-permute-start.12 = (bf16[2,16,4096]{2,1,0:T(8,128)(2,1)S(1)}, bf16[2,16,4096]{2,1,0:T(8,128)(2,1)S(1)}, u32[]{:S(2)}, u32[]{:S(2)}) collective-permute-start(bf16[2,16,4096]{2,1,0:T(8,128)(2,1)S(1)} %slice.37), channel_id=1, source_target_pairs={{0,8},{4,12},{8,0},{12,4},{16,24},{20,28},{24,16},{28,20},{1,9},{5... | collective-permute-start | bytes 786440 | tf_op jit(solution)/shard_map/ppermute | solution.py:173
  25.3 19.2 %slice-start = ((s8[16777216]{0:T(1024)(128)(4,1)}), s8[4194304]{0:T(1024)(128)(4,1)S(1)}, s32[]{:S(2)}) async-start(s8[16777216]{0:T(1024)(128)(4,1)} %bitcast.20), calls=%async_computation | async-start | bytes 8388608
  25.3 19.2 %slice-start.1 = ((s8[16777216]{0:T(1024)(128)(4,1)}), s8[4194304]{0:T(1024)(128)(4,1)S(1)}, s32[]{:S(2)}) async-start(s8[16777216]{0:T(1024)(128)(4,1)} %bitcast.20), calls=%async_computation.1 | async-start | bytes 8388608
  26.7 7.2 %collective-permute-start.1 = (bf16[2,128,512]{2,1,0:T(8,128)(2,1)S(1)}, bf16[2,128,512]{2,1,0:T(8,128)(2,1)S(1)}, u32[]{:S(2)}, u32[]{:S(2)}) collective-permute-start(bf16[2,128,512]{2,1,0:T(8,128)(2,1)S(1)} %shard_map.65), channel_id=1, source_target_pairs={{0,1},{1,0},{2,3},{3,2},{4,5},{5,4},{6,7},{7,6},{8,9},{9,8},{10,11... | collective-permute-start | bytes 786440 | tf_op jit(solution)/shard_map/ppermute | solution.py:222
  28.3 6.5 %collective-permute-start.5 = (bf16[4,16,4096]{2,1,0:T(8,128)(2,1)S(1)}, bf16[4,16,4096]{2,1,0:T(8,128)(2,1)S(1)}, u32[]{:S(2)}, u32[]{:S(2)}) collective-permute-start(bf16[4,16,4096]{2,1,0:T(8,128)(2,1)S(1)} %collective-permute-done.4.refs_0_.refs_2_), channel_id=1, source_target_pairs={{0,4},{4,0},{8,12},{12,8},{16,20},{20,16},{24,28},{28,24},{1,5},{5... | collective-permute-start | bytes 1572872 | tf_op jit(solution)/shard_map/ppermute | solution.py:173
  28.3 6.5 %collective-permute-start.7 = (bf16[4,16,4096]{2,1,0:T(8,128)(2,1)S(1)}, bf16[4,16,4096]{2,1,0:T(8,128)(2,1)S(1)}, u32[]{:S(2)}, u32[]{:S(2)}) collective-permute-start(bf16[4,16,4096]{2,1,0:T(8,128)(2,1)S(1)} %collective-permute-done.6.refs_2_.refs_4_), channel_id=1, source_target_pairs={{0,4},{4,0},{8,12},{12,8},{16,20},{20,16},{24,28},{28,24},{1,5},{5... | collective-permute-start | bytes 1572872 | tf_op jit(solution)/shard_map/ppermute | solution.py:173
  28.9 5.9 %collective-permute-start.13 = (bf16[2,16,4096]{2,1,0:T(8,128)(2,1)S(1)}, bf16[2,16,4096]{2,1,0:T(8,128)(2,1)S(1)}, u32[]{:S(2)}, u32[]{:S(2)}) collective-permute-start(bf16[2,16,4096]{2,1,0:T(8,128)(2,1)S(1)} %collective-permute-done.11.refs_0_.refs_6_), channel_id=1, source_target_pairs={{0,4},{4,0},{8,12},{12,8},{16,20},{20,16},{24,28},{28,24},{1,5},{5... | collective-permute-start | bytes 786440 | tf_op jit(solution)/shard_map/ppermute | solution.py:173
  29.0 5.8 %collective-permute-start.14 = (bf16[2,16,4096]{2,1,0:T(8,128)(2,1)S(1)}, bf16[2,16,4096]{2,1,0:T(8,128)(2,1)S(1)}, u32[]{:S(2)}, u32[]{:S(2)}) collective-permute-start(bf16[2,16,4096]{2,1,0:T(8,128)(2,1)S(1)} %collective-permute-done.12.refs_1_.refs_7_), channel_id=1, source_target_pairs={{0,4},{4,0},{8,12},{12,8},{16,20},{20,16},{24,28},{28,24},{1,5},{5... | collective-permute-start | bytes 786440 | tf_op jit(solution)/shard_map/ppermute | solution.py:173
  33.9 38.7 %collective-permute-start.3 = (bf16[128,512]{1,0:T(8,128)(2,1)S(1)}, bf16[128,512]{1,0:T(8,128)(2,1)S(1)}, u32[]{:S(2)}, u32[]{:S(2)}) collective-permute-start(bf16[128,512]{1,0:T(8,128)(2,1)S(1)} %slice_bitcast_fusion.2), channel_id=1, source_target_pairs={{1,2},{2,1},{5,6},{6,5},{9,10},{10,9},{13,14},{14,13},{17,18},{18,... | collective-permute-start | bytes 393224 | tf_op jit(solution)/shard_map/ppermute | solution.py:223
  38.5 15.7 %collective-permute-start.20 = (f32[96,128]{1,0:T(8,128)S(1)}, f32[96,128]{1,0:T(8,128)S(1)}, u32[]{:S(2)}, u32[]{:S(2)}) collective-permute-start(f32[96,128]{1,0:T(8,128)S(1)} %shard_map.70), channel_id=1, source_target_pairs={{0,3},{1,2},{2,1},{3,0},{4,7},{5,6},{6,5},{7,4},{8,11},{9,10},{10,... | collective-permute-start | bytes 147464 | tf_op jit(solution)/shard_map/ppermute | solution.py:258
  42.3 12.7 %collective-permute-start.19 = (f32[96,128]{1,0:T(8,128)S(1)}, f32[96,128]{1,0:T(8,128)S(1)}, u32[]{:S(2)}, u32[]{:S(2)}) collective-permute-start(f32[96,128]{1,0:T(8,128)S(1)} %shard_map.70), channel_id=1, source_target_pairs={{0,2},{1,3},{2,0},{3,1},{4,6},{5,7},{6,4},{7,5},{8,10},{9,11},{10,... | collective-permute-start | bytes 147464 | tf_op jit(solution)/shard_map/ppermute | solution.py:258
  44.5 11.7 %collective-permute-start.18 = (f32[96,128]{1,0:T(8,128)S(1)}, f32[96,128]{1,0:T(8,128)S(1)}, u32[]{:S(2)}, u32[]{:S(2)}) collective-permute-start(f32[96,128]{1,0:T(8,128)S(1)} %shard_map.70), channel_id=1, source_target_pairs={{0,1},{1,0},{2,3},{3,2},{4,5},{5,4},{6,7},{7,6},{8,9},{9,8},{10,11... | collective-permute-start | bytes 147464 | tf_op jit(solution)/shard_map/ppermute | solution.py:258
  47.0 19.2 %collective-permute-start.8 = (bf16[2,256,512]{2,1,0:T(8,128)(2,1)S(1)}, bf16[2,256,512]{2,1,0:T(8,128)(2,1)S(1)}, u32[]{:S(2)}, u32[]{:S(2)}) collective-permute-start(bf16[2,256,512]{2,1,0:T(8,128)(2,1)S(1)} %shard_map.67), channel_id=1, source_target_pairs={{0,1},{1,0},{2,3},{3,2},{4,5},{5,4},{6,7},{7,6},{8,9},{9,8},{10,11... | collective-permute-start | bytes 1572872 | tf_op jit(solution)/shard_map/ppermute | solution.py:222
  52.8 19.9 %copy-start.4 = (bf16[64,64,512]{2,1,0:T(8,128)(2,1)S(1)}, bf16[64,64,512]{2,1,0:T(8,128)(2,1)}, u32[]{:S(2)}) copy-start(bf16[64,64,512]{2,1,0:T(8,128)(2,1)} %up.1) | copy-start | bytes 12582916
  54.2 22.7 %collective-permute-start.2 = (bf16[128,512]{1,0:T(8,128)(2,1)S(1)}, bf16[128,512]{1,0:T(8,128)(2,1)S(1)}, u32[]{:S(2)}, u32[]{:S(2)}) collective-permute-start(bf16[128,512]{1,0:T(8,128)(2,1)S(1)} %fusion.2), channel_id=1, source_target_pairs={{0,2},{1,3},{2,0},{3,1},{4,6},{5,7},{6,4},{7,5},{8,10},{9,11},{10,... | collective-permute-start | bytes 393224 | tf_op jit(solution)/shard_map/ppermute | solution.py:234
  54.9 12.5 %collective-permute-start.15 = (bf16[2,128,512]{2,1,0:T(8,128)(2,1)S(1)}, bf16[2,128,512]{2,1,0:T(8,128)(2,1)S(1)}, u32[]{:S(2)}, u32[]{:S(2)}) collective-permute-start(bf16[2,128,512]{2,1,0:T(8,128)(2,1)S(1)} %shard_map.69), channel_id=1, source_target_pairs={{0,1},{1,0},{2,3},{3,2},{4,5},{5,4},{6,7},{7,6},{8,9},{9,8},{10,11... | collective-permute-start | bytes 786440 | tf_op jit(solution)/shard_map/ppermute | solution.py:222
  56.2 20.7 %collective-permute-start.17 = (bf16[128,512]{1,0:T(8,128)(2,1)S(1)}, bf16[128,512]{1,0:T(8,128)(2,1)S(1)}, u32[]{:S(2)}, u32[]{:S(2)}) collective-permute-start(bf16[128,512]{1,0:T(8,128)(2,1)S(1)} %slice_bitcast_fusion.1), channel_id=1, source_target_pairs={{1,2},{2,1},{5,6},{6,5},{9,10},{10,9},{13,14},{14,13},{17,18},{18,... | collective-permute-start | bytes 393224 | tf_op jit(solution)/shard_map/ppermute | solution.py:223
  66.2 10.7 %collective-permute-start.10 = (bf16[256,512]{1,0:T(8,128)(2,1)S(1)}, bf16[256,512]{1,0:T(8,128)(2,1)S(1)}, u32[]{:S(2)}, u32[]{:S(2)}) collective-permute-start(bf16[256,512]{1,0:T(8,128)(2,1)S(1)} %slice_bitcast_fusion), channel_id=1, source_target_pairs={{1,2},{2,1},{5,6},{6,5},{9,10},{10,9},{13,14},{14,13},{17,18},{18,... | collective-permute-start | bytes 786440 | tf_op jit(solution)/shard_map/ppermute | solution.py:223
  67.4 28.4 %collective-permute-start.9 = (bf16[256,512]{1,0:T(8,128)(2,1)S(1)}, bf16[256,512]{1,0:T(8,128)(2,1)S(1)}, u32[]{:S(2)}, u32[]{:S(2)}) collective-permute-start(bf16[256,512]{1,0:T(8,128)(2,1)S(1)} %fusion), channel_id=1, source_target_pairs={{0,2},{1,3},{2,0},{3,1},{4,6},{5,7},{6,4},{7,5},{8,10},{9,11},{10,... | collective-permute-start | bytes 786440 | tf_op jit(solution)/shard_map/ppermute | solution.py:234
  72.6 23.2 %collective-permute-start.16 = (bf16[128,512]{1,0:T(8,128)(2,1)S(1)}, bf16[128,512]{1,0:T(8,128)(2,1)S(1)}, u32[]{:S(2)}, u32[]{:S(2)}) collective-permute-start(bf16[128,512]{1,0:T(8,128)(2,1)S(1)} %fusion.1), channel_id=1, source_target_pairs={{0,2},{1,3},{2,0},{3,1},{4,6},{5,7},{6,4},{7,5},{8,10},{9,11},{10,... | collective-permute-start | bytes 393224 | tf_op jit(solution)/shard_map/ppermute | solution.py:234
  (6 other events, 50.1 us)

commit v2 on v1

v2 whole, which is shorter than its diff:
```python
import functools

import jax
import jax.numpy as jnp
from jax import lax
from jax.experimental import pallas as pl
from jax.experimental.pallas import tpu as pltpu
from jax.sharding import PartitionSpec as P

OWN_CAP = 48


adapter_scale = 0.5

MIB = 2**20
WIDE = 256
VMEM = pl.BlockSpec(memory_space=pltpu.VMEM)
HBM = pl.BlockSpec(memory_space=pltpu.HBM)


def params(mib):
    return pltpu.CompilerParams(vmem_limit_bytes=mib * MIB)


def stack_rows(parts, rows_ref):
    at = 0
    for part in parts:
        steps, requests, feats = part.shape
        rows_ref[pl.ds(at, steps * requests), :] = part[...].reshape(steps * requests, feats)
        at += steps * requests


def load_kernel(weight, out, sems):
    cols = out.shape[-1]
    mine = lax.axis_index("tensor")
    copies = [
        pltpu.make_async_copy(
            weight.at[:, pl.ds(pl.multiple_of((mine ^ flip) * cols, cols), cols)], out.at[slot], sems.at[slot]
        )
        for slot, flip in enumerate((1, 3))
    ]
    for copy in copies:
        copy.start()
    for copy in copies:
        copy.wait()


def outer_dots(rows, weight, near, mid):
    cols = mid.shape[-1]
    for at in range(0, cols, WIDE):
        where = pl.ds(at, WIDE)
        near[0, :, where] = jnp.dot(
            rows[...], weight[0, :, where], preferred_element_type=jnp.float32
        ).astype(near.dtype)
    for at in range(0, cols, WIDE):
        where = pl.ds(at, WIDE)
        value = jnp.dot(
            rows[...], weight[1, :, where], preferred_element_type=jnp.float32
        ).astype(near.dtype)
        near[1, :, where] = value
        mid[:, where] = value


def first_outer_kernel(n, *refs):
    parts, weight, whole, near, mid, rest, rows, sems = refs[:n], *refs[n:]
    cols = mid.shape[-1]
    mine = lax.axis_index("tensor")
    copies = [
        pltpu.make_async_copy(
            whole.at[:, pl.ds(pl.multiple_of((mine ^ flip) * cols, cols), cols)], rest.at[slot], sems.at[slot]
        )
        for slot, flip in enumerate((2, 0))
    ]
    for copy in copies:
        copy.start()
    stack_rows(parts, rows)
    outer_dots(rows, weight, near, mid)
    for copy in copies:
        copy.wait()


def outer_kernel(n, *refs):
    parts, weight, near, mid, rows = refs[:n], *refs[n:]
    stack_rows(parts, rows)
    outer_dots(rows, weight, near, mid)


def inner_kernel(n, *refs):
    parts, weight, far, own, rows = refs[:n], *refs[n:]
    cols = own.shape[-1]
    stack_rows(parts, rows)
    for slot, out in enumerate((far, own)):
        for at in range(0, cols, WIDE):
            where = pl.ds(at, WIDE)
            out[:, where] = jnp.dot(rows[...], weight[slot, :, where], preferred_element_type=jnp.float32)


def rank_kernel(order, before, n, *refs):
    parts, rest, rows = refs[:n], refs[n:-1], refs[-1]
    down, slot, place, out = rest[0], rest[1], rest[2], rest[-1]
    me = lax.axis_index("replica")
    adapters, rank, feats = down.shape
    stack_rows(parts, rows)
    total = rows.shape[0]
    block = total // len(order)
    starts = [pl.multiple_of((me ^ k) * block, block) for k in order]
    reduced = lax.dot_general(
        rows[...],
        down[...].reshape(adapters * rank, feats),
        (((1,), (1,)), ((), ())),
        preferred_element_type=jnp.float32,
    )
    local = jnp.concatenate([slot[pl.ds(at, block), :] for at in starts], axis=0) - me * adapters
    adapter_of = lax.broadcasted_iota(jnp.int32, (total, adapters * rank), 1) // rank
    picked = jnp.where(adapter_of == local, reduced, 0.0)
    width = adapters * rank
    while width > rank:
        width //= 2
        picked = picked[:, :width] + picked[:, width:]
    half = out.shape[0]
    packed = 2 * half
    where = jnp.concatenate([place[pl.ds(me ^ k, 1), :] for k in order], axis=1) - me * packed
    chosen = (lax.broadcasted_iota(jnp.int32, (packed, total), 0) == where).astype(jnp.float32)
    packed_rank = jnp.dot(
        chosen, picked, preferred_element_type=jnp.float32, precision=lax.Precision.HIGHEST
    )
    value = jnp.concatenate([packed_rank[:half], packed_rank[half:]], axis=1)
    out[...] = value + rest[3][...] if before else value


def up_kernel(packed_rank, up, slot, column, out):
    total = slot.shape[0]
    adapters, rank, cols = up.shape
    owners, held, _ = packed_rank.shape
    chosen = (
        lax.broadcasted_iota(jnp.int32, (total, owners * held), 1) == column[...]
    ).astype(jnp.bfloat16)
    both = jnp.dot(
        chosen, packed_rank[...].reshape(owners * held, 2 * rank), preferred_element_type=jnp.float32
    )
    early_rows = total // owners // 2
    late = (lax.broadcasted_iota(jnp.int32, (total, rank), 0) // early_rows) % 2
    rank_rows = jnp.where(late == 1, both[:, rank:], both[:, :rank])
    group = 8
    wide = jnp.concatenate([rank_rows] * group, axis=1).astype(jnp.bfloat16)
    adapter_of = lax.broadcasted_iota(jnp.int32, (total, group * rank), 1) // rank
    local = slot[...] - adapter_of
    out[...] = jnp.zeros_like(out)

    def step(g, carry):
        spread = jnp.where(local == g * group, wide, jnp.zeros_like(wide))
        weight = up[pl.ds(g * group, group)].reshape(group * rank, cols)
        out[...] += jnp.dot(spread, weight, preferred_element_type=jnp.float32)
        return carry

    lax.fori_loop(0, adapters // group, step, 0)
    out[...] = adapter_scale * out[...]


def finish_kernel(pieces, *refs):
    out, delta = refs[-1], refs[-2]
    steps, _, cols = out.shape
    me = lax.axis_index("replica")
    at = 0
    for order in pieces:
        own, near, far, mid = refs[at : at + 4]
        at += 4
        rows = own.shape[0] // len(order)
        requests = rows // steps
        for i, k in enumerate(order):
            here = pl.ds(i * rows, rows)
            who = me ^ k
            total = own[here, :] + near[0, here, :].astype(jnp.float32)
            total += far[here, :].astype(jnp.float32) + mid[here, :].astype(jnp.float32)
            total += delta[pl.ds(pl.multiple_of(who * rows, rows), rows), :]
            out[:, pl.ds(pl.multiple_of(who * requests, requests), requests), :] = total.astype(
                out.dtype
            ).reshape(steps, requests, cols)


def flip(size, bits):
    return [(i, i ^ bits) for i in range(size)]


def on_device_blocks(
    attention_output,
    output_weight,
    adapter_down_weight,
    adapter_up_weight,
    request_adapter,
    adapter_storage_row,
):
    replicas, tensors = lax.axis_size("replica"), lax.axis_size("tensor")
    steps, own_requests, feats = attention_output.shape
    cols = output_weight.shape[1] // tensors
    adapters_here, _, rank = adapter_down_weight.shape
    requests = request_adapter.shape[0]
    rows = steps * own_requests
    half = steps // 2
    me, mine = lax.axis_index("replica"), lax.axis_index("tensor")
    inner = (mine == 1) | (mine == 2)

    def swap(value, bits):
        return lax.ppermute(value, "replica", flip(replicas, bits))

    def along(value, bits):
        return lax.ppermute(value, "tensor", flip(tensors, bits))

    passed = []

    def tie(*values):
        held = lax.optimization_barrier((*values, *passed))[: len(values)]
        return held[0] if len(values) == 1 else held

    def done(*values):
        passed[:] = values

    def wait(*values):
        passed.extend(values)

    adapter_ids = jnp.arange(adapter_storage_row.shape[0], dtype=jnp.int32)
    slot_of = jnp.sum(
        jnp.where(request_adapter[:, None] == adapter_ids[None, :], adapter_storage_row[None, :], 0),
        axis=1,
    )
    owner_of = slot_of // adapters_here
    index = jnp.arange(requests, dtype=jnp.int32)
    rank_in = jnp.sum(
        ((owner_of[:, None] == owner_of[None, :]) & (index[None, :] < index[:, None])).astype(jnp.int32),
        axis=1,
    )

    def by_row(per_request, per_step):
        return per_request.reshape(replicas, 1, own_requests) + per_step.reshape(1, steps, 1)

    step = jnp.arange(steps, dtype=jnp.int32)
    slot_rows = by_row(slot_of, 0 * step).reshape(-1, 1)
    place_rows = by_row(owner_of * (steps * OWN_CAP) + rank_in, step * OWN_CAP).reshape(replicas, rows)
    column_rows = by_row(
        (owner_of ^ me) * (half * OWN_CAP) + rank_in, (step % half) * OWN_CAP
    ).reshape(-1, 1)

    def cost(n, width):
        return pl.CostEstimate(flops=n * width, bytes_accessed=n, transcendentals=0)

    def outer(parts, *weights):
        n = sum(p.shape[0] * p.shape[1] for p in parts)
        first = len(weights) == 2
        shapes = [
            jax.ShapeDtypeStruct((2, n, cols), jnp.bfloat16),
            jax.ShapeDtypeStruct((n, cols), jnp.bfloat16),
        ]
        scratch = [pltpu.VMEM((n, feats), jnp.bfloat16)]
        return pl.pallas_call(
            functools.partial(first_outer_kernel if first else outer_kernel, len(parts)),
            out_shape=shapes + [pltpu.VMEM((2, feats, cols), jnp.bfloat16)] * first,
            in_specs=[VMEM] * (len(parts) + 1) + [HBM] * first,
            out_specs=[VMEM] * (2 + first),
            scratch_shapes=scratch + [pltpu.SemaphoreType.DMA((2,))] * first,
            compiler_params=params(8),
            cost_estimate=cost(n, 2 * cols),
        )(*parts, *weights)

    def inside(parts, weight):
        n = sum(p.shape[0] * p.shape[1] for p in parts)
        return pl.pallas_call(
            functools.partial(inner_kernel, len(parts)),
            out_shape=[jax.ShapeDtypeStruct((n, cols), jnp.float32)] * 2,
            in_specs=[VMEM] * (len(parts) + 1),
            out_specs=[VMEM, VMEM],
            scratch_shapes=[pltpu.VMEM((n, feats), jnp.bfloat16)],
            compiler_params=params(8),
            cost_estimate=cost(n, 2 * cols),
        )(*parts, weight)

    down = jnp.transpose(adapter_down_weight, (0, 2, 1))

    def ranked(order, parts, *before):
        n = rows * len(order)
        return pl.pallas_call(
            functools.partial(rank_kernel, order, len(before) > 0, len(parts)),
            out_shape=jax.ShapeDtypeStruct((half * OWN_CAP, 2 * rank), jnp.float32),
            in_specs=[VMEM] * (len(parts) + 3 + len(before)),
            out_specs=VMEM,
            scratch_shapes=[pltpu.VMEM((n, feats), jnp.bfloat16)],
            compiler_params=params(10),
            cost_estimate=cost(n, adapters_here * rank),
        )(*parts, down, slot_rows, place_rows, *before)

    def pass_on(far, near_in):
        both = far + jnp.where(inner, near_in[1].astype(jnp.float32), 0.0)
        both = both.astype(jnp.bfloat16)
        return along(both, 2), both

    def across(mid):
        return lax.ppermute(mid, "tensor", [(1, 2), (2, 1)])

    x0 = attention_output
    x1, x2, x4 = swap(x0, 1), swap(x0, 2), swap(x0, 4)
    weight = pltpu.with_memory_space_constraint(output_weight, pltpu.HBM)
    held_out = pl.pallas_call(
        load_kernel,
        out_shape=pltpu.VMEM((2, feats, cols), jnp.bfloat16),
        in_specs=[HBM],
        out_specs=VMEM,
        scratch_shapes=[pltpu.SemaphoreType.DMA((2,))],
        compiler_params=params(2),
    )(weight)
    near0, mid0, held_in = outer([x0, x1], held_out, weight)
    done(near0)
    near0_in, mid0_in = along(near0, 1), across(mid0)
    far0, own0 = inside([tie(x0), x1], held_in)
    done(own0)
    packed = ranked((0, 1), [tie(x0), x1])
    done(packed)

    far0_in, sent = pass_on(far0, tie(near0_in))
    wait(sent)

    wait(x2, x4, mid0_in)
    x2, x4 = tie(x2, x4)
    x3, x6a = swap(x2, 1), swap(x2[:half], 4)
    x5, x6b = swap(x4, 1), swap(x4[half:], 2)
    wait(x3)
    near1, mid1 = outer([tie(x2), x3], held_out)
    done(near1)
    near1_in = along(near1, 1)
    wait(x5)
    mid1_in = across(tie(mid1))
    far1, own1 = inside([tie(x2), x3], held_in)
    done(own1)
    packed = ranked((2, 3), [tie(x2), x3], packed)
    done(packed)

    wait(x6a, x6b)
    x6a, x6b = tie(x6a, x6b)
    x7a, x7b = swap(x6a, 1), swap(x6b, 1)
    near2, mid2 = outer([tie(x4), x5], held_out)
    done(near2)
    wait(x7a, x7b, far0_in)
    near2_in, mid2_in = along(tie(near2), 1), across(tie(mid2))
    packed = ranked((4, 5, 6, 7), [tie(x4), x5, x6a, x6b, x7a, x7b], packed)
    done(packed)
    packed_in = along(packed, 1)
    wait(near1_in, mid1_in)
    far1_in, sent = pass_on(far1, tie(near1_in))
    wait(sent)
    near3, mid3 = outer([tie(x6a), x6b, x7a, x7b], held_out)
    done(near3)
    near3_in = along(near3, 1)
    wait(packed_in)
    packed = packed + tie(packed_in)
    done(packed)
    packed_in = along(packed, 2)
    far2, own2 = inside([tie(x4), x5], held_in)
    done(own2)
    wait(mid2_in, near2_in)
    mid3_in = across(tie(mid3))
    far2_in, sent = pass_on(far2, tie(near2_in))
    wait(sent)
    far3, own3 = inside([tie(x6a), x6b, x7a, x7b], held_in)
    done(own3)
    wait(packed_in)
    ranks = (packed + tie(packed_in)).astype(jnp.bfloat16)[None]
    done(ranks)
    got = swap(ranks, 1)
    wait(far1_in, got)
    ranks = jnp.concatenate([ranks, tie(got)], axis=0)
    done(ranks)
    got = swap(ranks, 2)
    wait(near3_in)
    far3_in, sent = pass_on(far3, tie(near3_in))
    wait(sent, got, far2_in)
    ranks = jnp.concatenate([ranks, tie(got)], axis=0)
    done(ranks)
    got = swap(ranks, 4)
    wait(got, mid3_in)
    ranks = jnp.concatenate([ranks, tie(got)], axis=0)

    delta = pl.pallas_call(
        up_kernel,
        out_shape=jax.ShapeDtypeStruct((replicas * rows, cols), jnp.float32),
        in_specs=[VMEM] * 4,
        out_specs=VMEM,
        compiler_params=params(12),
        cost_estimate=pl.CostEstimate(
            flops=2 * replicas * rows * cols * adapter_up_weight.shape[0] * rank,
            bytes_accessed=4 * MIB,
            transcendentals=0,
        ),
    )(ranks, adapter_up_weight, slot_rows, column_rows)

    pieces = [(0, 1), (2, 3), (4, 5), (6, 7)]
    shares = [
        (own0, near0_in, far0_in, mid0_in),
        (own1, near1_in, far1_in, mid1_in),
        (own2, near2_in, far2_in, mid2_in),
        (own3, near3_in, far3_in, mid3_in),
    ]
    return pl.pallas_call(
        functools.partial(finish_kernel, pieces),
        out_shape=jax.ShapeDtypeStruct((steps, requests, cols), jnp.bfloat16),
        in_specs=[VMEM] * 17,
        out_specs=VMEM,
        compiler_params=params(12),
    )(*[ref for share in shares for ref in share], delta)


def on_device(
    attention_output,
    output_weight,
    adapter_down_weight,
    adapter_up_weight,
    request_adapter,
    adapter_storage_row,
):
    replicas = lax.axis_size("replica")
    my_index = lax.axis_index("replica")
    owner_partial = adapter_down_weight.shape[0]
    requests = request_adapter.shape[0]
    everyone = lax.all_gather(attention_output, "replica", axis=1, tiled=True)
    partial_sums = jnp.einsum(
        "sif,fc->sic", everyone, output_weight, preferred_element_type=jnp.float32
    )
    base_output = lax.psum_scatter(partial_sums, "tensor", scatter_dimension=2, tiled=True)
    adapter_ids = jnp.arange(adapter_storage_row.shape[0], dtype=jnp.int32)
    storage_row_of = jnp.sum(
        jnp.where(
            request_adapter[:, None] == adapter_ids[None, :], adapter_storage_row[None, :], 0
        ),
        axis=1,
    )
    owner_of = storage_row_of // owner_partial
    owner_table = owner_of[:, None] == jnp.arange(replicas, dtype=jnp.int32)[None, :]
    running = jnp.cumsum(owner_table.astype(jnp.int32), axis=0) - 1
    rank_in = jnp.sum(jnp.where(owner_table, running, 0), axis=1)
    owned_here = owner_of == my_index
    target = jnp.where(owned_here, rank_in, OWN_CAP)
    chosen = (
        jnp.zeros((OWN_CAP,), jnp.int32)
        .at[target]
        .set(jnp.arange(requests, dtype=jnp.int32), mode="drop")
    )
    filled = jnp.zeros((OWN_CAP,), jnp.int32).at[target].set(1, mode="drop")
    local_slot = storage_row_of[chosen] - my_index * owner_partial
    slot_pick = jnp.where(
        local_slot[:, None] == jnp.arange(owner_partial, dtype=jnp.int32)[None, :],
        filled[:, None],
        0,
    ).astype(jnp.float32)
    selected_rows = everyone[:, chosen, :]
    reduced_input = jnp.einsum(
        "ldu,hun->ldhn", selected_rows, adapter_down_weight, preferred_element_type=jnp.float32
    )
    rank_part = jnp.sum(reduced_input * slot_pick[None, :, :, None], axis=2)
    spread = jnp.where(
        owned_here[None, :, None], rank_part[:, jnp.minimum(rank_in, OWN_CAP - 1), :], 0.0
    )
    rank_full = lax.psum(spread, ("replica", "tensor"))
    rank_values = rank_full.astype(jnp.bfloat16)
    selected_up_rows = adapter_up_weight[storage_row_of]
    adapter_delta = jnp.einsum(
        "ajz,jzt->ajt", rank_values, selected_up_rows, preferred_element_type=jnp.float32
    )
    return (base_output + adapter_scale * adapter_delta).astype(jnp.bfloat16)


def solution(mesh):
    in_specs = (
        P(None, "replica", "tensor"),
        P("tensor", "replica"),
        P("replica", "tensor", None),
        P(None, None, ("replica", "tensor")),
        P(),
        P(),
    )
    out_specs = P(None, None, ("replica", "tensor"))
    blocks = mesh.shape["replica"] == 8 and mesh.shape["tensor"] == 4
    return jax.shard_map(
        on_device_blocks if blocks else on_device,
        mesh=mesh,
        in_specs=in_specs,
        out_specs=out_specs,
        check_vma=False,
    )
```

time: 97.1 us -> 104 us (1.071)
  local copies, waits for them, and re-layouts: 7.5 us -> 23.6 us
  waiting for transfers between devices: 32.2 us -> 16.1 us
  Pallas kernels: 19.1 us -> 28.8 us
  blocking collectives: 9.28 us -> 0 us
  starting transfers between devices: 27.1 us -> 31.8 us
  other arithmetic: 1.29 us -> 2.77 us
    unnamed x18 -> x58, local copies, waits for them, and re-layouts: 6.85 us -> 22.9 us
    ppermute x12 -> x14, waiting for transfers between devices: 22.4 us -> 10.4 us  [the longest x10 10.4 us: along(): return lax.ppermute(value, 'tensor', flip(tensors, bits))]
    pallas_call x8 -> x13, Pallas kernels: 18 us -> 27.7 us  [the longest x4 9.13 us: outer(): pl.pallas_call(functools.partial(first_outer_kernel if first else outer_k...]
    all_gather x1 -> x0, blocking collectives: 9.28 us -> none  [on_device_blocks(): ranks = lax.all_gather(gathered.astype(jnp.bfloat16), 'replica', axis=0)]
    ppermute x9 -> x12, waiting for transfers between devices: 9.82 us -> 5.68 us  [swap(): return lax.ppermute(value, 'replica', flip(replicas, bits))]
    ppermute x12 -> x14, starting transfers between devices: 19.1 us -> 22.7 us  [the longest x10 19.7 us: along(): return lax.ppermute(value, 'tensor', flip(tensors, bits))]
    concatenate x0 -> x3, other arithmetic: none -> 1.58 us  [on_device_blocks(): ranks = jnp.concatenate([ranks, tie(got)], axis=0)]
    ppermute x9 -> x12, starting transfers between devices: 7.98 us -> 9.13 us  [swap(): return lax.ppermute(value, 'replica', flip(replicas, bits))]
  transfers between devices with their start and end apart: 21 -> 26, of which waited for: 5 -> 6; matrix products, arithmetic and copies ran while one was open for 2% -> 3% of each run, Pallas kernels for 19% -> 27%
where the time goes in v2:
time: 104 us
  starting transfers between devices  31.8 us (31%)
  Pallas kernels  28.8 us (28%)
  local copies, waits for them, and re-layouts  23.6 us (23%)
  waiting for transfers between devices  16.1 us (15%)
  other arithmetic  2.77 us (3%)
    unnamed x58, local copies, waits for them, and re-layouts  22.9 us
    ppermute x10, starting transfers between devices, along(): return lax.ppermute(value, 'tensor', flip(tensors, bits))  19.7 us
    ppermute x10, waiting for transfers between devices, along(): return lax.ppermute(value, 'tensor', flip(tensors, bits))  10.4 us
    ppermute x12, starting transfers between devices, swap(): return lax.ppermute(value, 'replica', flip(replicas, bits))  9.13 us
    pallas_call x4, Pallas kernels, outer(): pl.pallas_call(functools.partial(first_outer_kernel if first else outer_k...  9.13 us
    pallas_call x3, Pallas kernels, ranked(): pl.pallas_call(functools.partial(rank_kernel, order, len(before) > 0, len...  5.79 us
    ppermute x12, waiting for transfers between devices, swap(): return lax.ppermute(value, 'replica', flip(replicas, bits))  5.68 us
    pallas_call x4, Pallas kernels, inside(): pl.pallas_call(functools.partial(inner_kernel, len(parts)), out_shape=[ja...  5.04 us
  transfers between devices with their start and end apart: 26, of which 6 were waited for; matrix products, arithmetic and copies ran while one was open for 3% of the time, Pallas kernels for 27%

profile of v2, /device:TPU:0, one launch (start us, length us, event | category | flops | bytes accessed | tf_op | source)
XLA Modules:
  0.0 103.6 jit_solution(8647967995872367361)
XLA Ops:
  0.5 2.5 %collective-permute-start.4 = (bf16[4,16,4096]{2,1,0:T(8,128)(2,1)}, bf16[4,16,4096]{2,1,0:T(8,128)(2,1)S(1)}, u32[]{:S(2)}, u32[]{:S(2)}) collective-permute-start(bf16[4,16,4096]{2,1,0:T(8,128)(2,1)} %refs_0_.3), channel_id=1, source_target_pairs={{0,8},{4,12},{8,0},{12,4},{16,24},{20,28},{24,16},{28,20},{1,9},{5... | collective-permute-start | bytes 1572872 | tf_op jit(solution)/shard_map/ppermute | solution.py:204
  4.5 3.5 %shard_map.64.refs_2_.refs_4_ = bf16[2,4096,512]{2,1,0:T(8,128)(2,1)S(1)} custom-call(bf16[4096,2048]{1,0:T(8,128)(2,1)} %refs_3_.1), custom_call_target="tpu_custom_call" | custom-call | tf_op jit(solution)/shard_map/pallas_call | solution.py:301
  8.0 3.3 %copy-done = bf16[2,4096,512]{2,1,0:T(8,128)(2,1)} copy-done((bf16[2,4096,512]{2,1,0:T(8,128)(2,1)}, bf16[2,4096,512]{2,1,0:T(8,128)(2,1)S(1)}, u32[]{:S(2)}) %copy-start) | copy-done | bytes 8388632
  11.8 3.4 %copy-done.1 = bf16[2,4096,512]{2,1,0:T(8,128)(2,1)S(1)} copy-done((bf16[2,4096,512]{2,1,0:T(8,128)(2,1)S(1)}, bf16[2,4096,512]{2,1,0:T(8,128)(2,1)}, u32[]{:S(2)}) %copy-start.1) | copy-done | bytes 8388632
  15.2 4.7 %shard_map.65 = (bf16[2,128,512]{2,1,0:T(8,128)(2,1)S(1)}, bf16[128,512]{1,0:T(8,128)(2,1)S(1)}, bf16[2,4096,512]{2,1,0:T(8,128)(2,1)S(1)}) custom-call(bf16[4,16,4096]{2,1,0:T(8,128)(2,1)S(1)} %copy-done.8, bf16[4,16,4096]{2,1,0:T(8,128)(2,1)S(1)} %collective-permute-done.refs_1_, bf16[2,4096,512]{2,1,0:T(8,128)(2,1)S(1)} %copy-done.1, ...), custom_call_target="tpu_custom_call" | custom-call | flops 131072 | bytes 128 | tf_op jit(solution)/shard_map/pallas_call | solution.py:254
  19.9 3.3 %copy-done.3 = bf16[2,4096,512]{2,1,0:T(8,128)(2,1)} copy-done((bf16[2,4096,512]{2,1,0:T(8,128)(2,1)}, bf16[2,4096,512]{2,1,0:T(8,128)(2,1)S(1)}, u32[]{:S(2)}) %copy-start.3) | copy-done | bytes 8388632
  25.8 3.4 %copy-done.4 = bf16[2,4096,512]{2,1,0:T(8,128)(2,1)S(1)} copy-done((bf16[2,4096,512]{2,1,0:T(8,128)(2,1)S(1)}, bf16[2,4096,512]{2,1,0:T(8,128)(2,1)}, u32[]{:S(2)}) %copy-start.4) | copy-done | bytes 8388632
  31.3 2.5 %copy-done.6 = bf16[8,4096,64]{1,2,0:T(8,128)(2,1)S(1)} copy-done((bf16[8,4096,64]{1,2,0:T(8,128)(2,1)S(1)}, bf16[8,4096,64]{1,2,0:T(8,128)(2,1)}, u32[]{:S(2)}) %copy-start.6) | copy-done | bytes 4194328
  33.8 1.9 %shard_map.67.refs_5_ = f32[96,128]{1,0:T(8,128)S(1)} custom-call(bf16[4,16,4096]{2,1,0:T(8,128)(2,1)S(1)} %copy-done.8, bf16[4,16,4096]{2,1,0:T(8,128)(2,1)S(1)} %collective-permute-done.refs_1_, bf16[8,64,4096]{2,1,0:T(8,128)(2,1)S(1)} %bitcast.21, s32[512,1]{1,0:T(8,128)S(1)} %reshape.152.refs_3_.refs_7_.slot, s32[8,64]{1,0:T(8,128)S(1)} %broadcast_add_fusion.1.refs_4_.refs_8_), custom_call_target="tpu_custom_call" | custom-call | flops 65536 | bytes 128 | tf_op jit(solution)/shard_map/pallas_call | solution.py:280
  37.8 3.4 %copy-done.2 = bf16[2,4096,512]{2,1,0:T(8,128)(2,1)S(1)} copy-done((bf16[2,4096,512]{2,1,0:T(8,128)(2,1)S(1)}, bf16[2,4096,512]{2,1,0:T(8,128)(2,1)}, u32[]{:S(2)}) %copy-start.2) | copy-done | bytes 8388632
  43.8 1.9 %shard_map.70.refs_9_ = f32[96,128]{1,0:T(8,128)S(1)} custom-call(bf16[4,16,4096]{2,1,0:T(8,128)(2,1)S(1)} %collective-permute-done.4.refs_0_, bf16[4,16,4096]{2,1,0:T(8,128)(2,1)S(1)} %collective-permute-done.6.refs_1_, bf16[8,64,4096]{2,1,0:T(8,128)(2,1)S(1)} %bitcast.22, s32[512,1]{1,0:T(8,128)S(1)} %reshape.152.refs_3_.refs_7_.slot, ...), custom_call_target="tpu_custom_call" | custom-call | flops 65536 | bytes 128 | tf_op jit(solution)/shard_map/pallas_call | solution.py:280
  46.3 4.2 %collective-permute-start.8 = (bf16[2,128,512]{2,1,0:T(8,128)(2,1)S(1)}, bf16[2,128,512]{2,1,0:T(8,128)(2,1)S(1)}, u32[]{:S(2)}, u32[]{:S(2)}) collective-permute-start(bf16[2,128,512]{2,1,0:T(8,128)(2,1)S(1)} %get-tuple-element.59), channel_id=1, source_target_pairs={{0,1},{1,0},{2,3},{3,2},{4,5},{5,4},{6,7},{7,6},{8,9},{9,8},{10,11... | collective-permute-start | bytes 786440 | tf_op jit(solution)/shard_map/ppermute | solution.py:207
  52.7 6.5 %collective-permute-done.2.refs_2_ = bf16[128,512]{1,0:T(8,128)(2,1)S(1)} collective-permute-done((bf16[128,512]{1,0:T(8,128)(2,1)S(1)}, bf16[128,512]{1,0:T(8,128)(2,1)S(1)}, u32[]{:S(2)}, u32[]{:S(2)}) %collective-permute-start.2) | collective-permute-done | bytes 131104 | tf_op jit(solution)/shard_map/ppermute | solution.py:207
  59.9 2.8 %collective-permute-start.16 = (bf16[2,128,512]{2,1,0:T(8,128)(2,1)S(1)}, bf16[2,128,512]{2,1,0:T(8,128)(2,1)S(1)}, u32[]{:S(2)}, u32[]{:S(2)}) collective-permute-start(bf16[2,128,512]{2,1,0:T(8,128)(2,1)S(1)} %get-tuple-element.78), channel_id=1, source_target_pairs={{0,1},{1,0},{2,3},{3,2},{4,5},{5,4},{6,7},{7,6},{8,9},{9,8},{10,11... | collective-permute-start | bytes 786440 | tf_op jit(solution)/shard_map/ppermute | solution.py:207
  62.6 2.0 %shard_map.72 = f32[96,128]{1,0:T(8,128)S(1)} custom-call(bf16[4,16,4096]{2,1,0:T(8,128)(2,1)S(1)} %collective-permute-done.5.refs_0_, bf16[4,16,4096]{2,1,0:T(8,128)(2,1)S(1)} %collective-permute-done.7.refs_1_, bf16[2,16,4096]{2,1,0:T(8,128)(2,1)S(1)} %collective-permute-done.9.refs_2_.refs_0_, ...), custom_call_target="tpu_custom_call" | custom-call | flops 131072 | bytes 256 | tf_op jit(solution)/shard_map/pallas_call | solution.py:280
  65.6 4.8 %collective-permute-start.14 = (bf16[128,512]{1,0:T(8,128)(2,1)S(1)}, bf16[128,512]{1,0:T(8,128)(2,1)S(1)}, u32[]{:S(2)}, u32[]{:S(2)}) collective-permute-start(bf16[128,512]{1,0:T(8,128)(2,1)S(1)} %fusion.2), channel_id=1, source_target_pairs={{0,2},{1,3},{2,0},{3,1},{4,6},{5,7},{6,4},{7,5},{8,10},{9,11},{10,... | collective-permute-start | bytes 393224 | tf_op jit(solution)/shard_map/ppermute | solution.py:207
  70.4 1.9 %shard_map.73 = (bf16[2,128,512]{2,1,0:T(8,128)(2,1)S(1)}, bf16[128,512]{1,0:T(8,128)(2,1)}) custom-call(bf16[2,16,4096]{2,1,0:T(8,128)(2,1)S(1)} %collective-permute-done.9.refs_2_.refs_0_, bf16[2,16,4096]{2,1,0:T(8,128)(2,1)S(1)} %collective-permute-done.10.refs_3_.refs_1_, bf16[2,16,4096]{2,1,0:T(8,128)(2,1)S(1)} %collective-permute-done.11.refs_4_.refs_2_, ...), custom_call_target="tpu_custom_call" | custom-call | flops 131072 | bytes 128 | tf_op jit(solution)/shard_map/pallas_call | solution.py:254
  72.3 2.8 %collective-permute-start.20 = (f32[96,128]{1,0:T(8,128)S(1)}, f32[96,128]{1,0:T(8,128)S(1)}, u32[]{:S(2)}, u32[]{:S(2)}) collective-permute-start(f32[96,128]{1,0:T(8,128)S(1)} %add.119), channel_id=1, source_target_pairs={{0,2},{1,3},{2,0},{3,1},{4,6},{5,7},{6,4},{7,5},{8,10},{9,11},{10,... | collective-permute-start | bytes 147464 | tf_op jit(solution)/shard_map/ppermute | solution.py:207
  79.4 3.1 %collective-permute-start.18 = (bf16[128,512]{1,0:T(8,128)(2,1)S(1)}, bf16[128,512]{1,0:T(8,128)(2,1)S(1)}, u32[]{:S(2)}, u32[]{:S(2)}) collective-permute-start(bf16[128,512]{1,0:T(8,128)(2,1)S(1)} %fusion.1), channel_id=1, source_target_pairs={{0,2},{1,3},{2,0},{3,1},{4,6},{5,7},{6,4},{7,5},{8,10},{9,11},{10,... | collective-permute-start | bytes 393224 | tf_op jit(solution)/shard_map/ppermute | solution.py:207
  85.1 2.3 %collective-permute-done.24 = bf16[2,96,128]{2,1,0:T(8,128)(2,1)S(1)} collective-permute-done((bf16[2,96,128]{2,1,0:T(8,128)(2,1)S(1)}, bf16[2,96,128]{2,1,0:T(8,128)(2,1)S(1)}, u32[]{:S(2)}, u32[]{:S(2)}) %collective-permute-start.24) | collective-permute-done | bytes 49184 | tf_op jit(solution)/shard_map/ppermute | solution.py:204
  87.3 2.3 %collective-permute-done.18.refs_10_ = bf16[128,512]{1,0:T(8,128)(2,1)S(1)} collective-permute-done((bf16[128,512]{1,0:T(8,128)(2,1)S(1)}, bf16[128,512]{1,0:T(8,128)(2,1)S(1)}, u32[]{:S(2)}, u32[]{:S(2)}) %collective-permute-start.18) | collective-permute-done | bytes 131104 | tf_op jit(solution)/shard_map/ppermute | solution.py:207
  92.0 3.1 %collective-permute-done.25 = bf16[4,96,128]{2,1,0:T(8,128)(2,1)} collective-permute-done((bf16[4,96,128]{2,1,0:T(8,128)(2,1)}, bf16[4,96,128]{2,1,0:T(8,128)(2,1)}, u32[]{:S(2)}, u32[]{:S(2)}) %collective-permute-start.25) | collective-permute-done | bytes 98336 | tf_op jit(solution)/shard_map/ppermute | solution.py:204
  96.1 2.2 %copy-done.19 = bf16[64,64,512]{2,1,0:T(8,128)(2,1)S(1)} copy-done((bf16[64,64,512]{2,1,0:T(8,128)(2,1)S(1)}, bf16[64,64,512]{2,1,0:T(8,128)(2,1)}, u32[]{:S(2)}) %copy-start.19) | copy-done | bytes 4194328
  98.3 4.2 %shard_map.76.refs_16_ = f32[512,512]{1,0:T(8,128)S(1)} custom-call(bf16[8,96,128]{2,1,0:T(8,128)(2,1)S(1)} %pad_maximum_fusion.packed_rank, bf16[64,64,512]{2,1,0:T(8,128)(2,1)S(1)} %copy-done.19, s32[512,1]{1,0:T(8,128)S(1)} %reshape.152.refs_3_.refs_7_.slot, s32[512,1]{1,0:T(8,128)S(1)} %add.129.column), custom_call_target="tpu_custom_call" | custom-call | flops 2147483648 | bytes 4194304 | tf_op jit(solution)/shard_map/pallas_call | solution.py:380
  (129 shorter events, 27.3 us)
Async XLA Ops:
  0.0 11.8 %collective-permute-start = (bf16[4,16,4096]{2,1,0:T(8,128)(2,1)}, bf16[4,16,4096]{2,1,0:T(8,128)(2,1)S(1)}, u32[]{:S(2)}, u32[]{:S(2)}) collective-permute-start(bf16[4,16,4096]{2,1,0:T(8,128)(2,1)} %refs_0_.3), channel_id=1, source_target_pairs={{0,4},{4,0},{8,12},{12,8},{16,20},{20,16},{24,28},{28,24},{1,5},{5... | collective-permute-start | bytes 1572872 | tf_op jit(solution)/shard_map/ppermute | solution.py:204
  0.5 35.3 %collective-permute-start.4 = (bf16[4,16,4096]{2,1,0:T(8,128)(2,1)}, bf16[4,16,4096]{2,1,0:T(8,128)(2,1)S(1)}, u32[]{:S(2)}, u32[]{:S(2)}) collective-permute-start(bf16[4,16,4096]{2,1,0:T(8,128)(2,1)} %refs_0_.3), channel_id=1, source_target_pairs={{0,8},{4,12},{8,0},{12,4},{16,24},{20,28},{24,16},{28,20},{1,9},{5... | collective-permute-start | bytes 1572872 | tf_op jit(solution)/shard_map/ppermute | solution.py:204
  2.9 32.9 %collective-permute-start.5 = (bf16[4,16,4096]{2,1,0:T(8,128)(2,1)}, bf16[4,16,4096]{2,1,0:T(8,128)(2,1)S(1)}, u32[]{:S(2)}, u32[]{:S(2)}) collective-permute-start(bf16[4,16,4096]{2,1,0:T(8,128)(2,1)} %refs_0_.3), channel_id=1, source_target_pairs={{0,16},{4,20},{8,24},{12,28},{16,0},{20,4},{24,8},{28,12},{1,17},{... | collective-permute-start | bytes 1572872 | tf_op jit(solution)/shard_map/ppermute | solution.py:204
  23.8 11.9 %collective-permute-start.1 = (bf16[2,128,512]{2,1,0:T(8,128)(2,1)S(1)}, bf16[2,128,512]{2,1,0:T(8,128)(2,1)S(1)}, u32[]{:S(2)}, u32[]{:S(2)}) collective-permute-start(bf16[2,128,512]{2,1,0:T(8,128)(2,1)S(1)} %get-tuple-element.49), channel_id=1, source_target_pairs={{0,1},{1,0},{2,3},{3,2},{4,5},{5,4},{6,7},{7,6},{8,9},{9,8},{10,11... | collective-permute-start | bytes 786440 | tf_op jit(solution)/shard_map/ppermute | solution.py:207
  30.5 5.4 %collective-permute-start.3 = (bf16[128,512]{1,0:T(8,128)(2,1)S(1)}, bf16[128,512]{1,0:T(8,128)(2,1)S(1)}, u32[]{:S(2)}, u32[]{:S(2)}) collective-permute-start(bf16[128,512]{1,0:T(8,128)(2,1)S(1)} %copy-done.21), channel_id=1, source_target_pairs={{1,2},{2,1},{5,6},{6,5},{9,10},{10,9},{13,14},{14,13},{17,18},{18,... | collective-permute-start | bytes 393224 | tf_op jit(solution)/shard_map/ppermute | solution.py:296
  35.9 6.6 %collective-permute-start.7 = (bf16[4,16,4096]{2,1,0:T(8,128)(2,1)S(1)}, bf16[4,16,4096]{2,1,0:T(8,128)(2,1)S(1)}, u32[]{:S(2)}, u32[]{:S(2)}) collective-permute-start(bf16[4,16,4096]{2,1,0:T(8,128)(2,1)S(1)} %collective-permute-done.5.refs_0_), channel_id=1, source_target_pairs={{0,4},{4,0},{8,12},{12,8},{16,20},{20,16},{24,28},{28,24},{1,5},{5... | collective-permute-start | bytes 1572872 | tf_op jit(solution)/shard_map/ppermute | solution.py:204
  36.5 9.3 %collective-permute-start.9 = (bf16[2,16,4096]{2,1,0:T(8,128)(2,1)S(1)}, bf16[2,16,4096]{2,1,0:T(8,128)(2,1)S(1)}, u32[]{:S(2)}, u32[]{:S(2)}) collective-permute-start(bf16[2,16,4096]{2,1,0:T(8,128)(2,1)S(1)} %slice.19), channel_id=1, source_target_pairs={{0,16},{4,20},{8,24},{12,28},{16,0},{20,4},{24,8},{28,12},{1,17},{... | collective-permute-start | bytes 786440 | tf_op jit(solution)/shard_map/ppermute | solution.py:204
  37.0 8.7 %collective-permute-start.10 = (bf16[2,16,4096]{2,1,0:T(8,128)(2,1)S(1)}, bf16[2,16,4096]{2,1,0:T(8,128)(2,1)S(1)}, u32[]{:S(2)}, u32[]{:S(2)}) collective-permute-start(bf16[2,16,4096]{2,1,0:T(8,128)(2,1)S(1)} %slice.20), channel_id=1, source_target_pairs={{0,8},{4,12},{8,0},{12,4},{16,24},{20,28},{24,16},{28,20},{1,9},{5... | collective-permute-start | bytes 786440 | tf_op jit(solution)/shard_map/ppermute | solution.py:204
  45.7 14.1 %collective-permute-start.11 = (bf16[2,16,4096]{2,1,0:T(8,128)(2,1)S(1)}, bf16[2,16,4096]{2,1,0:T(8,128)(2,1)S(1)}, u32[]{:S(2)}, u32[]{:S(2)}) collective-permute-start(bf16[2,16,4096]{2,1,0:T(8,128)(2,1)S(1)} %collective-permute-done.9.refs_2_.refs_0_), channel_id=1, source_target_pairs={{0,4},{4,0},{8,12},{12,8},{16,20},{20,16},{24,28},{28,24},{1,5},{5... | collective-permute-start | bytes 786440 | tf_op jit(solution)/shard_map/ppermute | solution.py:204
  46.0 13.9 %collective-permute-start.12 = (bf16[2,16,4096]{2,1,0:T(8,128)(2,1)S(1)}, bf16[2,16,4096]{2,1,0:T(8,128)(2,1)S(1)}, u32[]{:S(2)}, u32[]{:S(2)}) collective-permute-start(bf16[2,16,4096]{2,1,0:T(8,128)(2,1)S(1)} %collective-permute-done.10.refs_3_.refs_1_), channel_id=1, source_target_pairs={{0,4},{4,0},{8,12},{12,8},{16,20},{20,16},{24,28},{28,24},{1,5},{5... | collective-permute-start | bytes 786440 | tf_op jit(solution)/shard_map/ppermute | solution.py:204
  46.3 18.4 %collective-permute-start.8 = (bf16[2,128,512]{2,1,0:T(8,128)(2,1)S(1)}, bf16[2,128,512]{2,1,0:T(8,128)(2,1)S(1)}, u32[]{:S(2)}, u32[]{:S(2)}) collective-permute-start(bf16[2,128,512]{2,1,0:T(8,128)(2,1)S(1)} %get-tuple-element.59), channel_id=1, source_target_pairs={{0,1},{1,0},{2,3},{3,2},{4,5},{5,4},{6,7},{7,6},{8,9},{9,8},{10,11... | collective-permute-start | bytes 786440 | tf_op jit(solution)/shard_map/ppermute | solution.py:207
  50.5 8.7 %collective-permute-start.2 = (bf16[128,512]{1,0:T(8,128)(2,1)S(1)}, bf16[128,512]{1,0:T(8,128)(2,1)S(1)}, u32[]{:S(2)}, u32[]{:S(2)}) collective-permute-start(bf16[128,512]{1,0:T(8,128)(2,1)S(1)} %fusion.3), channel_id=1, source_target_pairs={{0,2},{1,3},{2,0},{3,1},{4,6},{5,7},{6,4},{7,5},{8,10},{9,11},{10,... | collective-permute-start | bytes 393224 | tf_op jit(solution)/shard_map/ppermute | solution.py:207
  50.7 14.0 %collective-permute-start.13 = (bf16[128,512]{1,0:T(8,128)(2,1)S(1)}, bf16[128,512]{1,0:T(8,128)(2,1)S(1)}, u32[]{:S(2)}, u32[]{:S(2)}) collective-permute-start(bf16[128,512]{1,0:T(8,128)(2,1)S(1)} %get-tuple-element.71), channel_id=1, source_target_pairs={{1,2},{2,1},{5,6},{6,5},{9,10},{10,9},{13,14},{14,13},{17,18},{18,... | collective-permute-start | bytes 393224 | tf_op jit(solution)/shard_map/ppermute | solution.py:296
  59.9 16.5 %collective-permute-start.16 = (bf16[2,128,512]{2,1,0:T(8,128)(2,1)S(1)}, bf16[2,128,512]{2,1,0:T(8,128)(2,1)S(1)}, u32[]{:S(2)}, u32[]{:S(2)}) collective-permute-start(bf16[2,128,512]{2,1,0:T(8,128)(2,1)S(1)} %get-tuple-element.78), channel_id=1, source_target_pairs={{0,1},{1,0},{2,3},{3,2},{4,5},{5,4},{6,7},{7,6},{8,9},{9,8},{10,11... | collective-permute-start | bytes 786440 | tf_op jit(solution)/shard_map/ppermute | solution.py:207
  64.6 7.7 %collective-permute-start.15 = (f32[96,128]{1,0:T(8,128)S(1)}, f32[96,128]{1,0:T(8,128)S(1)}, u32[]{:S(2)}, u32[]{:S(2)}) collective-permute-start(f32[96,128]{1,0:T(8,128)S(1)} %shard_map.72), channel_id=1, source_target_pairs={{0,1},{1,0},{2,3},{3,2},{4,5},{5,4},{6,7},{7,6},{8,9},{9,8},{10,11... | collective-permute-start | bytes 147464 | tf_op jit(solution)/shard_map/ppermute | solution.py:207
  64.7 11.7 %collective-permute-start.17 = (bf16[128,512]{1,0:T(8,128)(2,1)S(1)}, bf16[128,512]{1,0:T(8,128)(2,1)S(1)}, u32[]{:S(2)}, u32[]{:S(2)}) collective-permute-start(bf16[128,512]{1,0:T(8,128)(2,1)S(1)} %get-tuple-element.81), channel_id=1, source_target_pairs={{1,2},{2,1},{5,6},{6,5},{9,10},{10,9},{13,14},{14,13},{17,18},{18,... | collective-permute-start | bytes 393224 | tf_op jit(solution)/shard_map/ppermute | solution.py:296
  65.6 17.5 %collective-permute-start.14 = (bf16[128,512]{1,0:T(8,128)(2,1)S(1)}, bf16[128,512]{1,0:T(8,128)(2,1)S(1)}, u32[]{:S(2)}, u32[]{:S(2)}) collective-permute-start(bf16[128,512]{1,0:T(8,128)(2,1)S(1)} %fusion.2), channel_id=1, source_target_pairs={{0,2},{1,3},{2,0},{3,1},{4,6},{5,7},{6,4},{7,5},{8,10},{9,11},{10,... | collective-permute-start | bytes 393224 | tf_op jit(solution)/shard_map/ppermute | solution.py:207
  72.3 12.1 %collective-permute-start.19 = (bf16[2,128,512]{2,1,0:T(8,128)(2,1)S(1)}, bf16[2,128,512]{2,1,0:T(8,128)(2,1)S(1)}, u32[]{:S(2)}, u32[]{:S(2)}) collective-permute-start(bf16[2,128,512]{2,1,0:T(8,128)(2,1)S(1)} %get-tuple-element.74), channel_id=1, source_target_pairs={{0,1},{1,0},{2,3},{3,2},{4,5},{5,4},{6,7},{7,6},{8,9},{9,8},{10,11... | collective-permute-start | bytes 786440 | tf_op jit(solution)/shard_map/ppermute | solution.py:207
  72.3 7.0 %collective-permute-start.20 = (f32[96,128]{1,0:T(8,128)S(1)}, f32[96,128]{1,0:T(8,128)S(1)}, u32[]{:S(2)}, u32[]{:S(2)}) collective-permute-start(f32[96,128]{1,0:T(8,128)S(1)} %add.119), channel_id=1, source_target_pairs={{0,2},{1,3},{2,0},{3,1},{4,6},{5,7},{6,4},{7,5},{8,10},{9,11},{10,... | collective-permute-start | bytes 147464 | tf_op jit(solution)/shard_map/ppermute | solution.py:207
  79.4 10.2 %collective-permute-start.18 = (bf16[128,512]{1,0:T(8,128)(2,1)S(1)}, bf16[128,512]{1,0:T(8,128)(2,1)S(1)}, u32[]{:S(2)}, u32[]{:S(2)}) collective-permute-start(bf16[128,512]{1,0:T(8,128)(2,1)S(1)} %fusion.1), channel_id=1, source_target_pairs={{0,2},{1,3},{2,0},{3,1},{4,6},{5,7},{6,4},{7,5},{8,10},{9,11},{10,... | collective-permute-start | bytes 393224 | tf_op jit(solution)/shard_map/ppermute | solution.py:207
  82.5 9.6 %collective-permute-start.23 = (bf16[128,512]{1,0:T(8,128)(2,1)}, bf16[128,512]{1,0:T(8,128)(2,1)S(1)}, u32[]{:S(2)}, u32[]{:S(2)}) collective-permute-start(bf16[128,512]{1,0:T(8,128)(2,1)} %get-tuple-element.90), channel_id=1, source_target_pairs={{1,2},{2,1},{5,6},{6,5},{9,10},{10,9},{13,14},{14,13},{17,18},{18,... | collective-permute-start | bytes 393224 | tf_op jit(solution)/shard_map/ppermute | solution.py:296
  83.2 4.2 %collective-permute-start.24 = (bf16[2,96,128]{2,1,0:T(8,128)(2,1)S(1)}, bf16[2,96,128]{2,1,0:T(8,128)(2,1)S(1)}, u32[]{:S(2)}, u32[]{:S(2)}) collective-permute-start(bf16[2,96,128]{2,1,0:T(8,128)(2,1)S(1)} %pad_maximum_fusion.2), channel_id=1, source_target_pairs={{0,8},{4,12},{8,0},{12,4},{16,24},{20,28},{24,16},{28,20},{1,9},{5... | collective-permute-start | bytes 147464 | tf_op jit(solution)/shard_map/ppermute | solution.py:204
  90.3 4.9 %collective-permute-start.25 = (bf16[4,96,128]{2,1,0:T(8,128)(2,1)}, bf16[4,96,128]{2,1,0:T(8,128)(2,1)}, u32[]{:S(2)}, u32[]{:S(2)}) collective-permute-start(bf16[4,96,128]{2,1,0:T(8,128)(2,1)} %pad_maximum_fusion.1), channel_id=1, source_target_pairs={{0,16},{4,20},{8,24},{12,28},{16,0},{20,4},{24,8},{28,12},{1,17},{... | collective-permute-start | bytes 294920 | tf_op jit(solution)/shard_map/ppermute | solution.py:204
  91.7 10.8 %collective-permute-start.22 = (bf16[128,512]{1,0:T(8,128)(2,1)}, bf16[128,512]{1,0:T(8,128)(2,1)S(1)}, u32[]{:S(2)}, u32[]{:S(2)}) collective-permute-start(bf16[128,512]{1,0:T(8,128)(2,1)} %fusion), channel_id=1, source_target_pairs={{0,2},{1,3},{2,0},{3,1},{4,6},{5,7},{6,4},{7,5},{8,10},{9,11},{10,... | collective-permute-start | bytes 393224 | tf_op jit(solution)/shard_map/ppermute | solution.py:207
  (31 other events, 243.4 us)

commit v3 on v2

--- a/solution.py
+++ b/solution.py
@@ -30,17 +30,53 @@
         at += steps * requests
 
 
-def load_kernel(weight, out, sems):
+def fetch(weight, out, sems, flips):
     cols = out.shape[-1]
     mine = lax.axis_index("tensor")
-    copies = [
-        pltpu.make_async_copy(
-            weight.at[:, pl.ds(pl.multiple_of((mine ^ flip) * cols, cols), cols)], out.at[slot], sems.at[slot]
-        )
-        for slot, flip in enumerate((1, 3))
-    ]
+    copies = []
+    for slot, bits in enumerate(flips):
+        chunk = pl.ds(pl.multiple_of((mine ^ bits) * cols, cols), cols)
+        copies.append(pltpu.make_async_copy(weight.at[:, chunk], out.at[slot], sems.at[slot]))
     for copy in copies:
         copy.start()
+    return copies
+
+
+def turned(row):
+    n = row.shape[1]
+    same = lax.broadcasted_iota(jnp.int32, (n, n), 0) == lax.broadcasted_iota(jnp.int32, (n, n), 1)
+    return jnp.sum(jnp.where(same, row, 0), axis=1, keepdims=True)
+
+
+def load_kernel(replicas, steps, adapters, weight, request, storage, out, where, inner, sems):
+    copies = fetch(weight, out, sems, (1, 3))
+    me, mine = lax.axis_index("replica"), lax.axis_index("tensor")
+    requests = request.shape[0]
+    stored = turned(storage[...].reshape(1, storage.shape[0]))
+    count = stored.shape[0]
+    asked = lax.broadcasted_iota(jnp.int32, (count, requests), 0) == request[...].reshape(1, requests)
+    slot_row = jnp.sum(jnp.where(asked, stored, 0), axis=0, keepdims=True)
+    slot = turned(slot_row)
+
+    def owner_of(slots):
+        return sum((slots >= first * adapters).astype(jnp.int32) for first in range(1, replicas))
+
+    owner = owner_of(slot)
+    square = (requests, requests)
+    earlier = lax.broadcasted_iota(jnp.int32, square, 1) < lax.broadcasted_iota(jnp.int32, square, 0)
+    order = jnp.sum(jnp.where(earlier & (owner_of(slot_row) == owner), 1, 0), axis=1, keepdims=True)
+    half = steps // 2
+    place = owner * (steps * OWN_CAP) + order
+    column = (owner ^ me) * (half * OWN_CAP) + order
+    own = requests // replicas
+    for replica in range(replicas):
+        mine_here = slice(replica * own, (replica + 1) * own)
+        for step in range(steps):
+            rows = pl.ds((replica * steps + step) * own, own)
+            where[rows, 0:1] = slot[mine_here]
+            where[rows, 1:2] = place[mine_here] + step * OWN_CAP
+            where[rows, 2:3] = column[mine_here] + (step % half) * OWN_CAP
+    inner[...] = jnp.where((mine == 1) | (mine == 2), jnp.ones_like(inner), jnp.zeros_like(inner))
     for copy in copies:
         copy.wait()
 
@@ -61,43 +97,38 @@
         mid[:, where] = value
 
 
-def first_outer_kernel(n, *refs):
-    parts, weight, whole, near, mid, rest, rows, sems = refs[:n], *refs[n:]
-    cols = mid.shape[-1]
-    mine = lax.axis_index("tensor")
-    copies = [
-        pltpu.make_async_copy(
-            whole.at[:, pl.ds(pl.multiple_of((mine ^ flip) * cols, cols), cols)], rest.at[slot], sems.at[slot]
-        )
-        for slot, flip in enumerate((2, 0))
-    ]
-    for copy in copies:
-        copy.start()
-    stack_rows(parts, rows)
-    outer_dots(rows, weight, near, mid)
-    for copy in copies:
-        copy.wait()
-
-
 def outer_kernel(n, *refs):
     parts, weight, near, mid, rows = refs[:n], *refs[n:]
     stack_rows(parts, rows)
     outer_dots(rows, weight, near, mid)
 
 
-def inner_kernel(n, *refs):
-    parts, weight, far, own, rows = refs[:n], *refs[n:]
+def inner_dots(rows, weight, far, own):
     cols = own.shape[-1]
-    stack_rows(parts, rows)
     for slot, out in enumerate((far, own)):
         for at in range(0, cols, WIDE):
             where = pl.ds(at, WIDE)
             out[:, where] = jnp.dot(rows[...], weight[slot, :, where], preferred_element_type=jnp.float32)
 
 
+def first_inner_kernel(n, *refs):
+    parts, whole, far, own, weight, rows, sems = refs[:n], *refs[n:]
+    copies = fetch(whole, weight, sems, (2, 0))
+    stack_rows(parts, rows)
+    for copy in copies:
+        copy.wait()
+    inner_dots(rows, weight, far, own)
+
+
+def inner_kernel(n, *refs):
+    parts, weight, far, own, rows = refs[:n], *refs[n:]
+    stack_rows(parts, rows)
+    inner_dots(rows, weight, far, own)
+
+
 def rank_kernel(order, before, n, *refs):
     parts, rest, rows = refs[:n], refs[n:-1], refs[-1]
-    down, slot, place, out = rest[0], rest[1], rest[2], rest[-1]
+    down, where, out = rest[0], rest[1], rest[-1]
     me = lax.axis_index("replica")
     adapters, rank, feats = down.shape
     stack_rows(parts, rows)
@@ -110,7 +141,8 @@
         (((1,), (1,)), ((), ())),
         preferred_element_type=jnp.float32,
     )
-    local = jnp.concatenate([slot[pl.ds(at, block), :] for at in starts], axis=0) - me * adapters
+    here = jnp.concatenate([where[pl.ds(at, block), :] for at in starts], axis=0)
+    local = here[:, 0:1] - me * adapters
     adapter_of = lax.broadcasted_iota(jnp.int32, (total, adapters * rank), 1) // rank
     picked = jnp.where(adapter_of == local, reduced, 0.0)
     width = adapters * rank
@@ -119,21 +151,26 @@
         picked = picked[:, :width] + picked[:, width:]
     half = out.shape[0]
     packed = 2 * half
-    where = jnp.concatenate([place[pl.ds(me ^ k, 1), :] for k in order], axis=1) - me * packed
-    chosen = (lax.broadcasted_iota(jnp.int32, (packed, total), 0) == where).astype(jnp.float32)
-    packed_rank = jnp.dot(
-        chosen, picked, preferred_element_type=jnp.float32, precision=lax.Precision.HIGHEST
+    place = here[:, 1:2] - me * packed
+    chosen = (lax.broadcasted_iota(jnp.int32, (total, packed), 1) == place).astype(jnp.float32)
+    packed_rank = lax.dot_general(
+        chosen,
+        picked,
+        (((0,), (0,)), ((), ())),
+        preferred_element_type=jnp.float32,
+        precision=lax.Precision.HIGHEST,
     )
     value = jnp.concatenate([packed_rank[:half], packed_rank[half:]], axis=1)
-    out[...] = value + rest[3][...] if before else value
-
-
-def up_kernel(packed_rank, up, slot, column, out):
-    total = slot.shape[0]
+    out[...] = value + rest[2][...] if before else value
+
+
+def up_kernel(packed_rank, up, where, out):
+    total = where.shape[0]
+    slot, column = where[:, 0:1], where[:, 2:3]
     adapters, rank, cols = up.shape
     owners, held, _ = packed_rank.shape
     chosen = (
-        lax.broadcasted_iota(jnp.int32, (total, owners * held), 1) == column[...]
+        lax.broadcasted_iota(jnp.int32, (total, owners * held), 1) == column
     ).astype(jnp.bfloat16)
     both = jnp.dot(
         chosen, packed_rank[...].reshape(owners * held, 2 * rank), preferred_element_type=jnp.float32
@@ -144,7 +181,7 @@
     group = 8
     wide = jnp.concatenate([rank_rows] * group, axis=1).astype(jnp.bfloat16)
     adapter_of = lax.broadcasted_iota(jnp.int32, (total, group * rank), 1) // rank
-    local = slot[...] - adapter_of
+    local = slot - adapter_of
     out[...] = jnp.zeros_like(out)
 
     def step(g, carry):
@@ -197,8 +234,6 @@
     requests = request_adapter.shape[0]
     rows = steps * own_requests
     half = steps // 2
-    me, mine = lax.axis_index("replica"), lax.axis_index("tensor")
-    inner = (mine == 1) | (mine == 2)
 
     def swap(value, bits):
         return lax.ppermute(value, "replica", flip(replicas, bits))
@@ -218,54 +253,20 @@
     def wait(*values):
         passed.extend(values)
 
-    adapter_ids = jnp.arange(adapter_storage_row.shape[0], dtype=jnp.int32)
-    slot_of = jnp.sum(
-        jnp.where(request_adapter[:, None] == adapter_ids[None, :], adapter_storage_row[None, :], 0),
-        axis=1,
-    )
-    owner_of = slot_of // adapters_here
-    index = jnp.arange(requests, dtype=jnp.int32)
-    rank_in = jnp.sum(
-        ((owner_of[:, None] == owner_of[None, :]) & (index[None, :] < index[:, None])).astype(jnp.int32),
-        axis=1,
-    )
-
-    def by_row(per_request, per_step):
-        return per_request.reshape(replicas, 1, own_requests) + per_step.reshape(1, steps, 1)
-
-    step = jnp.arange(steps, dtype=jnp.int32)
-    slot_rows = by_row(slot_of, 0 * step).reshape(-1, 1)
-    place_rows = by_row(owner_of * (steps * OWN_CAP) + rank_in, step * OWN_CAP).reshape(replicas, rows)
-    column_rows = by_row(
-        (owner_of ^ me) * (half * OWN_CAP) + rank_in, (step % half) * OWN_CAP
-    ).reshape(-1, 1)
-
     def cost(n, width):
         return pl.CostEstimate(flops=n * width, bytes_accessed=n, transcendentals=0)
 
-    def outer(parts, *weights):
-        n = sum(p.shape[0] * p.shape[1] for p in parts)
-        first = len(weights) == 2
-        shapes = [
-            jax.ShapeDtypeStruct((2, n, cols), jnp.bfloat16),
-            jax.ShapeDtypeStruct((n, cols), jnp.bfloat16),
-        ]
-        scratch = [pltpu.VMEM((n, feats), jnp.bfloat16)]
-        return pl.pallas_call(
-            functools.partial(first_outer_kernel if first else outer_kernel, len(parts)),
-            out_shape=shapes + [pltpu.VMEM((2, feats, cols), jnp.bfloat16)] * first,
-            in_specs=[VMEM] * (len(parts) + 1) + [HBM] * first,
-            out_specs=[VMEM] * (2 + first),
-            scratch_shapes=scratch + [pltpu.SemaphoreType.DMA((2,))] * first,
-            compiler_params=params(8),
-            cost_estimate=cost(n, 2 * cols),
-        )(*parts, *weights)
-
-    def inside(parts, weight):
+    held = pltpu.VMEM((2, feats, cols), jnp.bfloat16)
+    copies = pltpu.SemaphoreType.DMA((2,))
+
+    def outer(parts, weight):
         n = sum(p.shape[0] * p.shape[1] for p in parts)
         return pl.pallas_call(
-            functools.partial(inner_kernel, len(parts)),
-            out_shape=[jax.ShapeDtypeStruct((n, cols), jnp.float32)] * 2,
+            functools.partial(outer_kernel, len(parts)),
+            out_shape=[
+                jax.ShapeDtypeStruct((2, n, cols), jnp.bfloat16),
+                jax.ShapeDtypeStruct((n, cols), jnp.bfloat16),
+            ],
             in_specs=[VMEM] * (len(parts) + 1),
             out_specs=[VMEM, VMEM],
             scratch_shapes=[pltpu.VMEM((n, feats), jnp.bfloat16)],
@@ -273,6 +274,18 @@
             cost_estimate=cost(n, 2 * cols),
         )(*parts, weight)
 
+    def inside(parts, weight, first=False):
+        n = sum(p.shape[0] * p.shape[1] for p in parts)
+        return pl.pallas_call(
+            functools.partial(first_inner_kernel if first else inner_kernel, len(parts)),
+            out_shape=[jax.ShapeDtypeStruct((n, cols), jnp.float32)] * 2 + [held] * first,
+            in_specs=[VMEM] * len(parts) + [HBM if first else VMEM],
+            out_specs=[VMEM] * (2 + first),
+            scratch_shapes=[pltpu.VMEM((n, feats), jnp.bfloat16)] + [copies] * first,
+            compiler_params=params(8),
+            cost_estimate=cost(n, 2 * cols),
+        )(*parts, weight)
+
     down = jnp.transpose(adapter_down_weight, (0, 2, 1))
 
     def ranked(order, parts, *before):
@@ -280,15 +293,15 @@
         return pl.pallas_call(
             functools.partial(rank_kernel, order, len(before) > 0, len(parts)),
             out_shape=jax.ShapeDtypeStruct((half * OWN_CAP, 2 * rank), jnp.float32),
-            in_specs=[VMEM] * (len(parts) + 3 + len(before)),
+            in_specs=[VMEM] * (len(parts) + 2 + len(before)),
             out_specs=VMEM,
             scratch_shapes=[pltpu.VMEM((n, feats), jnp.bfloat16)],
             compiler_params=params(10),
             cost_estimate=cost(n, adapters_here * rank),
-        )(*parts, down, slot_rows, place_rows, *before)
+        )(*parts, down, where, *before)
 
     def pass_on(far, near_in):
-        both = far + jnp.where(inner, near_in[1].astype(jnp.float32), 0.0)
+        both = far + jnp.where(inner > 0, near_in[1].astype(jnp.float32), 0.0)
         both = both.astype(jnp.bfloat16)
         return along(both, 2), both
 
@@ -298,22 +311,25 @@
     x0 = attention_output
     x1, x2, x4 = swap(x0, 1), swap(x0, 2), swap(x0, 4)
     weight = pltpu.with_memory_space_constraint(output_weight, pltpu.HBM)
-    held_out = pl.pallas_call(
-        load_kernel,
-        out_shape=pltpu.VMEM((2, feats, cols), jnp.bfloat16),
-        in_specs=[HBM],
-        out_specs=VMEM,
-        scratch_shapes=[pltpu.SemaphoreType.DMA((2,))],
-        compiler_params=params(2),
-    )(weight)
-    near0, mid0, held_in = outer([x0, x1], held_out, weight)
+    held_out, where, inner = pl.pallas_call(
+        functools.partial(load_kernel, replicas, steps, adapters_here),
+        out_shape=[
+            held,
+            jax.ShapeDtypeStruct((replicas * rows, 8), jnp.int32),
+            jax.ShapeDtypeStruct((1, cols), jnp.float32),
+        ],
+        in_specs=[HBM, VMEM, VMEM],
+        out_specs=[VMEM] * 3,
+        scratch_shapes=[copies],
+        compiler_params=params(4),
+    )(weight, request_adapter, adapter_storage_row)
+    near0, mid0 = outer([x0, x1], held_out)
     done(near0)
     near0_in, mid0_in = along(near0, 1), across(mid0)
-    far0, own0 = inside([tie(x0), x1], held_in)
+    far0, own0, held_in = inside([tie(x0), x1], weight, True)
     done(own0)
     packed = ranked((0, 1), [tie(x0), x1])
     done(packed)
-
     far0_in, sent = pass_on(far0, tie(near0_in))
     wait(sent)
 
@@ -380,7 +396,7 @@
     delta = pl.pallas_call(
         up_kernel,
         out_shape=jax.ShapeDtypeStruct((replicas * rows, cols), jnp.float32),
-        in_specs=[VMEM] * 4,
+        in_specs=[VMEM] * 3,
         out_specs=VMEM,
         compiler_params=params(12),
         cost_estimate=pl.CostEstimate(
@@ -388,7 +404,7 @@
             bytes_accessed=4 * MIB,
             transcendentals=0,
         ),
-    )(ranks, adapter_up_weight, slot_rows, column_rows)
+    )(ranks, adapter_up_weight, where)
 
     pieces = [(0, 1), (2, 3), (4, 5), (6, 7)]
     shares = [

time: 104 us -> 82.1 us (0.79)
  local copies, waits for them, and re-layouts: 23.6 us -> 1.36 us
  waiting for transfers between devices: 16.1 us -> 19.8 us
  other arithmetic: 2.77 us -> 0.22 us
    unnamed x58 -> x10, local copies, waits for them, and re-layouts: 22.9 us -> 1.32 us
    ppermute x12, waiting for transfers between devices: 5.68 us -> 8.99 us  [swap(): return lax.ppermute(value, 'replica', flip(replicas, bits))]
    concatenate x3, other arithmetic: 1.58 us -> 0.04 us  [on_device_blocks(): ranks = jnp.concatenate([ranks, tie(got)], axis=0)]
  transfers between devices with their start and end apart: 26 -> 26, of which waited for: 6 -> 8; matrix products, arithmetic and copies ran while one was open for 3% -> 0% of each run, Pallas kernels for 27% -> 34%
where the time goes in v3:
time: 82.1 us; the launch traced here: 81.9 us
  starting transfers between devices  31.5 us (38%)
  Pallas kernels  28.6 us (35%)
  waiting for transfers between devices  19.8 us (24%)
  local copies, waits for them, and re-layouts  1.36 us (2%)
    ppermute x10, starting transfers between devices, along(): return lax.ppermute(value, 'tensor', flip(tensors, bits))  19.7 us
    ppermute x10, waiting for transfers between devices, along(): return lax.ppermute(value, 'tensor', flip(tensors, bits))  10.8 us
    ppermute x12, waiting for transfers between devices, swap(): return lax.ppermute(value, 'replica', flip(replicas, bits))  8.99 us
    pallas_call x4, Pallas kernels, inside(): pl.pallas_call(functools.partial(first_inner_kernel if first else inner_k...  8.9 us
    ppermute x12, starting transfers between devices, swap(): return lax.ppermute(value, 'replica', flip(replicas, bits))  8.89 us
    pallas_call x3, Pallas kernels, ranked(): pl.pallas_call(functools.partial(rank_kernel, order, len(before) > 0, len...  5.85 us
    pallas_call x4, Pallas kernels, outer(): pl.pallas_call(functools.partial(outer_kernel, len(parts)), out_shape=[ja...  5.01 us
    pallas_call x1, Pallas kernels, on_device_blocks(): pl.pallas_call(up_kernel, out_shape=jax.ShapeDtypeStruct((replicas * rows...  4.21 us
  transfers between devices with their start and end apart: 26, of which 8 were waited for; matrix products, arithmetic and copies ran while one was open for 0% of the time, Pallas kernels for 34%

profile of v3, /device:TPU:0, one launch (start us, length us, event | category | flops | bytes accessed | tf_op | source)
XLA Modules:
  0.0 81.9 jit_solution(7915666089950741985)
XLA Ops:
  0.5 2.6 %collective-permute-start.5 = (bf16[4,16,4096]{2,1,0:T(8,128)(2,1)}, bf16[4,16,4096]{2,1,0:T(8,128)(2,1)S(1)}, u32[]{:S(2)}, u32[]{:S(2)}) collective-permute-start(bf16[4,16,4096]{2,1,0:T(8,128)(2,1)} %refs_0_.3), channel_id=1, source_target_pairs={{0,16},{4,20},{8,24},{12,28},{16,0},{20,4},{24,8},{28,12},{1,17},{... | collective-permute-start | bytes 1572872 | tf_op jit(solution)/shard_map/ppermute | solution.py:239
  3.0 1.5 %collective-permute-start.4 = (bf16[4,16,4096]{2,1,0:T(8,128)(2,1)}, bf16[4,16,4096]{2,1,0:T(8,128)(2,1)S(1)}, u32[]{:S(2)}, u32[]{:S(2)}) collective-permute-start(bf16[4,16,4096]{2,1,0:T(8,128)(2,1)} %refs_0_.3), channel_id=1, source_target_pairs={{0,8},{4,12},{8,0},{12,4},{16,24},{20,28},{24,16},{28,20},{1,9},{5... | collective-permute-start | bytes 1572872 | tf_op jit(solution)/shard_map/ppermute | solution.py:239
  5.8 3.6 %shard_map.64 = (bf16[2,4096,512]{2,1,0:T(8,128)(2,1)S(1)}, s32[512,8]{1,0:T(8,128)S(1)}, f32[1,512]{1,0:T(1,128)S(1)}) custom-call(bf16[4096,2048]{1,0:T(8,128)(2,1)} %refs_2_.1, s32[128]{0:T(128)S(1)} %copy-done.2, s32[64]{0:T(128)S(1)} %copy-done.3), custom_call_target="tpu_custom_call" | custom-call | tf_op jit(solution)/shard_map/pallas_call | solution.py:314
  10.7 1.6 %collective-permute-start.1 = (bf16[2,128,512]{2,1,0:T(8,128)(2,1)S(1)}, bf16[2,128,512]{2,1,0:T(8,128)(2,1)S(1)}, u32[]{:S(2)}, u32[]{:S(2)}) collective-permute-start(bf16[2,128,512]{2,1,0:T(8,128)(2,1)S(1)} %get-tuple-element.53), channel_id=1, source_target_pairs={{0,1},{1,0},{2,3},{3,2},{4,5},{5,4},{6,7},{7,6},{8,9},{9,8},{10,11... | collective-permute-start | bytes 786440 | tf_op jit(solution)/shard_map/ppermute | solution.py:242
  13.1 5.2 %shard_map.66 = (f32[128,512]{1,0:T(8,128)S(1)}, f32[128,512]{1,0:T(8,128)S(1)}, bf16[2,4096,512]{2,1,0:T(8,128)(2,1)S(1)}) custom-call(bf16[4,16,4096]{2,1,0:T(8,128)(2,1)S(1)} %copy-done.1, bf16[4,16,4096]{2,1,0:T(8,128)(2,1)S(1)} %collective-permute-done.refs_1_, bf16[4096,2048]{1,0:T(8,128)(2,1)} %refs_2_.1), custom_call_target="tpu_custom_call" | custom-call | flops 131072 | bytes 128 | tf_op jit(solution)/shard_map/pallas_call | solution.py:279
  18.3 1.9 %shard_map.67.refs_4_ = f32[96,128]{1,0:T(8,128)S(1)} custom-call(bf16[4,16,4096]{2,1,0:T(8,128)(2,1)S(1)} %copy-done.1, bf16[4,16,4096]{2,1,0:T(8,128)(2,1)S(1)} %collective-permute-done.refs_1_, bf16[8,64,4096]{2,1,0:T(8,128)(2,1)S(1)} %bitcast.15, s32[512,8]{1,0:T(8,128)S(1)} %get-tuple-element.59.refs_3_.refs_7_.where), custom_call_target="tpu_custom_call" | custom-call | flops 65536 | bytes 128 | tf_op jit(solution)/shard_map/pallas_call | solution.py:293
  24.8 1.9 %shard_map.70.refs_8_ = f32[96,128]{1,0:T(8,128)S(1)} custom-call(bf16[4,16,4096]{2,1,0:T(8,128)(2,1)S(1)} %collective-permute-done.4.refs_0_, bf16[4,16,4096]{2,1,0:T(8,128)(2,1)S(1)} %collective-permute-done.6.refs_1_, bf16[8,64,4096]{2,1,0:T(8,128)(2,1)S(1)} %bitcast.16, s32[512,8]{1,0:T(8,128)S(1)} %get-tuple-element.59.refs_3_.refs_7_.where, ...), custom_call_target="tpu_custom_call" | custom-call | flops 65536 | bytes 128 | tf_op jit(solution)/shard_map/pallas_call | solution.py:293
  26.8 2.5 %collective-permute-done.10.refs_3_.refs_1_ = bf16[2,16,4096]{2,1,0:T(8,128)(2,1)S(1)} collective-permute-done((bf16[2,16,4096]{2,1,0:T(8,128)(2,1)S(1)}, bf16[2,16,4096]{2,1,0:T(8,128)(2,1)S(1)}, u32[]{:S(2)}, u32[]{:S(2)}) %collective-permute-start.10) | collective-permute-done | bytes 262176 | tf_op jit(solution)/shard_map/ppermute | solution.py:239
  30.1 4.2 %collective-permute-start.8 = (bf16[2,128,512]{2,1,0:T(8,128)(2,1)S(1)}, bf16[2,128,512]{2,1,0:T(8,128)(2,1)S(1)}, u32[]{:S(2)}, u32[]{:S(2)}) collective-permute-start(bf16[2,128,512]{2,1,0:T(8,128)(2,1)S(1)} %get-tuple-element.64), channel_id=1, source_target_pairs={{0,1},{1,0},{2,3},{3,2},{4,5},{5,4},{6,7},{7,6},{8,9},{9,8},{10,11... | collective-permute-start | bytes 786440 | tf_op jit(solution)/shard_map/ppermute | solution.py:242
  35.0 1.3 %shard_map.71 = (bf16[2,128,512]{2,1,0:T(8,128)(2,1)S(1)}, bf16[128,512]{1,0:T(8,128)(2,1)S(1)}) custom-call(bf16[4,16,4096]{2,1,0:T(8,128)(2,1)S(1)} %collective-permute-done.5.refs_0_, bf16[4,16,4096]{2,1,0:T(8,128)(2,1)S(1)} %collective-permute-done.7.refs_1_, bf16[2,4096,512]{2,1,0:T(8,128)(2,1)S(1)} %get-tuple-element.52.refs_2_.refs_4_), custom_call_target="tpu_custom_call" | custom-call | flops 131072 | bytes 128 | tf_op jit(solution)/shard_map/pallas_call | solution.py:264
  36.2 6.7 %collective-permute-done.2.refs_2_ = bf16[128,512]{1,0:T(8,128)(2,1)S(1)} collective-permute-done((bf16[128,512]{1,0:T(8,128)(2,1)S(1)}, bf16[128,512]{1,0:T(8,128)(2,1)S(1)}, u32[]{:S(2)}, u32[]{:S(2)}) %collective-permute-start.2) | collective-permute-done | bytes 131104 | tf_op jit(solution)/shard_map/ppermute | solution.py:242
  42.9 1.9 %collective-permute-start.16 = (bf16[2,128,512]{2,1,0:T(8,128)(2,1)S(1)}, bf16[2,128,512]{2,1,0:T(8,128)(2,1)S(1)}, u32[]{:S(2)}, u32[]{:S(2)}) collective-permute-start(bf16[2,128,512]{2,1,0:T(8,128)(2,1)S(1)} %get-tuple-element.84), channel_id=1, source_target_pairs={{0,1},{1,0},{2,3},{3,2},{4,5},{5,4},{6,7},{7,6},{8,9},{9,8},{10,11... | collective-permute-start | bytes 786440 | tf_op jit(solution)/shard_map/ppermute | solution.py:242
  44.8 2.0 %shard_map.72 = f32[96,128]{1,0:T(8,128)S(1)} custom-call(bf16[4,16,4096]{2,1,0:T(8,128)(2,1)S(1)} %collective-permute-done.5.refs_0_, bf16[4,16,4096]{2,1,0:T(8,128)(2,1)S(1)} %collective-permute-done.7.refs_1_, bf16[2,16,4096]{2,1,0:T(8,128)(2,1)S(1)} %collective-permute-done.9.refs_2_.refs_0_, ...), custom_call_target="tpu_custom_call" | custom-call | flops 131072 | bytes 256 | tf_op jit(solution)/shard_map/pallas_call | solution.py:293
  47.9 4.8 %collective-permute-start.14 = (bf16[128,512]{1,0:T(8,128)(2,1)S(1)}, bf16[128,512]{1,0:T(8,128)(2,1)S(1)}, u32[]{:S(2)}, u32[]{:S(2)}) collective-permute-start(bf16[128,512]{1,0:T(8,128)(2,1)S(1)} %fusion.5), channel_id=1, source_target_pairs={{0,2},{1,3},{2,0},{3,1},{4,6},{5,7},{6,4},{7,5},{8,10},{9,11},{10,... | collective-permute-start | bytes 393224 | tf_op jit(solution)/shard_map/ppermute | solution.py:242
  52.6 1.3 %shard_map.73 = (bf16[2,128,512]{2,1,0:T(8,128)(2,1)S(1)}, bf16[128,512]{1,0:T(8,128)(2,1)S(1)}) custom-call(bf16[2,16,4096]{2,1,0:T(8,128)(2,1)S(1)} %collective-permute-done.9.refs_2_.refs_0_, bf16[2,16,4096]{2,1,0:T(8,128)(2,1)S(1)} %collective-permute-done.10.refs_3_.refs_1_, bf16[2,16,4096]{2,1,0:T(8,128)(2,1)S(1)} %collective-permute-done.11.refs_4_.refs_2_, ...), custom_call_target="tpu_custom_call" | custom-call | flops 131072 | bytes 128 | tf_op jit(solution)/shard_map/pallas_call | solution.py:264
  54.5 3.0 %collective-permute-start.20 = (f32[96,128]{1,0:T(8,128)S(1)}, f32[96,128]{1,0:T(8,128)S(1)}, u32[]{:S(2)}, u32[]{:S(2)}) collective-permute-start(f32[96,128]{1,0:T(8,128)S(1)} %add.20), channel_id=1, source_target_pairs={{0,2},{1,3},{2,0},{3,1},{4,6},{5,7},{6,4},{7,5},{8,10},{9,11},{10,... | collective-permute-start | bytes 147464 | tf_op jit(solution)/shard_map/ppermute | solution.py:242
  58.8 1.3 %shard_map.75 = (f32[128,512]{1,0:T(8,128)S(1)}, f32[128,512]{1,0:T(8,128)S(1)}) custom-call(bf16[2,16,4096]{2,1,0:T(8,128)(2,1)S(1)} %collective-permute-done.9.refs_2_.refs_0_, bf16[2,16,4096]{2,1,0:T(8,128)(2,1)S(1)} %collective-permute-done.10.refs_3_.refs_1_, bf16[2,16,4096]{2,1,0:T(8,128)(2,1)S(1)} %collective-permute-done.11.refs_4_.refs_2_, ...), custom_call_target="tpu_custom_call" | custom-call | flops 131072 | bytes 128 | tf_op jit(solution)/shard_map/pallas_call | solution.py:279
  60.1 1.6 %collective-permute-done.20 = f32[96,128]{1,0:T(8,128)S(1)} collective-permute-done((f32[96,128]{1,0:T(8,128)S(1)}, f32[96,128]{1,0:T(8,128)S(1)}, u32[]{:S(2)}, u32[]{:S(2)}) %collective-permute-start.20) | collective-permute-done | bytes 49184 | tf_op jit(solution)/shard_map/ppermute | solution.py:242
  61.8 2.7 %collective-permute-start.18 = (bf16[128,512]{1,0:T(8,128)(2,1)S(1)}, bf16[128,512]{1,0:T(8,128)(2,1)S(1)}, u32[]{:S(2)}, u32[]{:S(2)}) collective-permute-start(bf16[128,512]{1,0:T(8,128)(2,1)S(1)} %fusion.3), channel_id=1, source_target_pairs={{0,2},{1,3},{2,0},{3,1},{4,6},{5,7},{6,4},{7,5},{8,10},{9,11},{10,... | collective-permute-start | bytes 393224 | tf_op jit(solution)/shard_map/ppermute | solution.py:242
  65.2 1.6 %collective-permute-start.24 = (bf16[2,96,128]{2,1,0:T(8,128)(2,1)S(1)}, bf16[2,96,128]{2,1,0:T(8,128)(2,1)S(1)}, u32[]{:S(2)}, u32[]{:S(2)}) collective-permute-start(bf16[2,96,128]{2,1,0:T(8,128)(2,1)S(1)} %pad_maximum_fusion.2), channel_id=1, source_target_pairs={{0,8},{4,12},{8,0},{12,4},{16,24},{20,28},{24,16},{28,20},{1,9},{5... | collective-permute-start | bytes 147464 | tf_op jit(solution)/shard_map/ppermute | solution.py:239
  66.8 2.6 %collective-permute-done.24 = bf16[2,96,128]{2,1,0:T(8,128)(2,1)S(1)} collective-permute-done((bf16[2,96,128]{2,1,0:T(8,128)(2,1)S(1)}, bf16[2,96,128]{2,1,0:T(8,128)(2,1)S(1)}, u32[]{:S(2)}, u32[]{:S(2)}) %collective-permute-start.24) | collective-permute-done | bytes 49184 | tf_op jit(solution)/shard_map/ppermute | solution.py:239
  69.3 2.6 %collective-permute-done.18.refs_10_ = bf16[128,512]{1,0:T(8,128)(2,1)S(1)} collective-permute-done((bf16[128,512]{1,0:T(8,128)(2,1)S(1)}, bf16[128,512]{1,0:T(8,128)(2,1)S(1)}, u32[]{:S(2)}, u32[]{:S(2)}) %collective-permute-start.18) | collective-permute-done | bytes 131104 | tf_op jit(solution)/shard_map/ppermute | solution.py:242
  73.2 3.4 %collective-permute-done.25 = bf16[4,96,128]{2,1,0:T(8,128)(2,1)S(1)} collective-permute-done((bf16[4,96,128]{2,1,0:T(8,128)(2,1)S(1)}, bf16[4,96,128]{2,1,0:T(8,128)(2,1)S(1)}, u32[]{:S(2)}, u32[]{:S(2)}) %collective-permute-start.25) | collective-permute-done | bytes 98336 | tf_op jit(solution)/shard_map/ppermute | solution.py:239
  76.6 4.2 %shard_map.76.refs_16_ = f32[512,512]{1,0:T(8,128)S(1)} custom-call(bf16[8,96,128]{2,1,0:T(8,128)(2,1)S(1)} %pad_maximum_fusion.packed_rank, bf16[64,64,512]{2,1,0:T(8,128)(2,1)S(1)} %copy-done.4, s32[512,8]{1,0:T(8,128)S(1)} %get-tuple-element.59.refs_3_.refs_7_.where), custom_call_target="tpu_custom_call" | custom-call | flops 2147483648 | bytes 4194304 | tf_op jit(solution)/shard_map/pallas_call | solution.py:396
  (64 shorter events, 15.9 us)
Async XLA Ops:
  0.0 9.4 %collective-permute-start = (bf16[4,16,4096]{2,1,0:T(8,128)(2,1)}, bf16[4,16,4096]{2,1,0:T(8,128)(2,1)S(1)}, u32[]{:S(2)}, u32[]{:S(2)}) collective-permute-start(bf16[4,16,4096]{2,1,0:T(8,128)(2,1)} %refs_0_.3), channel_id=1, source_target_pairs={{0,4},{4,0},{8,12},{12,8},{16,20},{20,16},{24,28},{28,24},{1,5},{5... | collective-permute-start | bytes 1572872 | tf_op jit(solution)/shard_map/ppermute | solution.py:239
  0.5 19.9 %collective-permute-start.5 = (bf16[4,16,4096]{2,1,0:T(8,128)(2,1)}, bf16[4,16,4096]{2,1,0:T(8,128)(2,1)S(1)}, u32[]{:S(2)}, u32[]{:S(2)}) collective-permute-start(bf16[4,16,4096]{2,1,0:T(8,128)(2,1)} %refs_0_.3), channel_id=1, source_target_pairs={{0,16},{4,20},{8,24},{12,28},{16,0},{20,4},{24,8},{28,12},{1,17},{... | collective-permute-start | bytes 1572872 | tf_op jit(solution)/shard_map/ppermute | solution.py:239
  3.0 17.3 %collective-permute-start.4 = (bf16[4,16,4096]{2,1,0:T(8,128)(2,1)}, bf16[4,16,4096]{2,1,0:T(8,128)(2,1)S(1)}, u32[]{:S(2)}, u32[]{:S(2)}) collective-permute-start(bf16[4,16,4096]{2,1,0:T(8,128)(2,1)} %refs_0_.3), channel_id=1, source_target_pairs={{0,8},{4,12},{8,0},{12,4},{16,24},{20,28},{24,16},{28,20},{1,9},{5... | collective-permute-start | bytes 1572872 | tf_op jit(solution)/shard_map/ppermute | solution.py:239
  10.7 9.6 %collective-permute-start.1 = (bf16[2,128,512]{2,1,0:T(8,128)(2,1)S(1)}, bf16[2,128,512]{2,1,0:T(8,128)(2,1)S(1)}, u32[]{:S(2)}, u32[]{:S(2)}) collective-permute-start(bf16[2,128,512]{2,1,0:T(8,128)(2,1)S(1)} %get-tuple-element.53), channel_id=1, source_target_pairs={{0,1},{1,0},{2,3},{3,2},{4,5},{5,4},{6,7},{7,6},{8,9},{9,8},{10,11... | collective-permute-start | bytes 786440 | tf_op jit(solution)/shard_map/ppermute | solution.py:242
  12.3 8.0 %collective-permute-start.3 = (bf16[128,512]{1,0:T(8,128)(2,1)S(1)}, bf16[128,512]{1,0:T(8,128)(2,1)S(1)}, u32[]{:S(2)}, u32[]{:S(2)}) collective-permute-start(bf16[128,512]{1,0:T(8,128)(2,1)S(1)} %get-tuple-element.61), channel_id=1, source_target_pairs={{1,2},{2,1},{5,6},{6,5},{9,10},{10,9},{13,14},{14,13},{17,18},{18,... | collective-permute-start | bytes 393224 | tf_op jit(solution)/shard_map/ppermute | solution.py:309
  21.0 8.4 %collective-permute-start.10 = (bf16[2,16,4096]{2,1,0:T(8,128)(2,1)S(1)}, bf16[2,16,4096]{2,1,0:T(8,128)(2,1)S(1)}, u32[]{:S(2)}, u32[]{:S(2)}) collective-permute-start(bf16[2,16,4096]{2,1,0:T(8,128)(2,1)S(1)} %slice.20), channel_id=1, source_target_pairs={{0,8},{4,12},{8,0},{12,4},{16,24},{20,28},{24,16},{28,20},{1,9},{5... | collective-permute-start | bytes 786440 | tf_op jit(solution)/shard_map/ppermute | solution.py:239
  21.6 8.0 %collective-permute-start.9 = (bf16[2,16,4096]{2,1,0:T(8,128)(2,1)S(1)}, bf16[2,16,4096]{2,1,0:T(8,128)(2,1)S(1)}, u32[]{:S(2)}, u32[]{:S(2)}) collective-permute-start(bf16[2,16,4096]{2,1,0:T(8,128)(2,1)S(1)} %slice.19), channel_id=1, source_target_pairs={{0,16},{4,20},{8,24},{12,28},{16,0},{20,4},{24,8},{28,12},{1,17},{... | collective-permute-start | bytes 786440 | tf_op jit(solution)/shard_map/ppermute | solution.py:239
  29.6 13.3 %collective-permute-start.11 = (bf16[2,16,4096]{2,1,0:T(8,128)(2,1)S(1)}, bf16[2,16,4096]{2,1,0:T(8,128)(2,1)S(1)}, u32[]{:S(2)}, u32[]{:S(2)}) collective-permute-start(bf16[2,16,4096]{2,1,0:T(8,128)(2,1)S(1)} %collective-permute-done.9.refs_2_.refs_0_), channel_id=1, source_target_pairs={{0,4},{4,0},{8,12},{12,8},{16,20},{20,16},{24,28},{28,24},{1,5},{5... | collective-permute-start | bytes 786440 | tf_op jit(solution)/shard_map/ppermute | solution.py:239
  29.6 13.3 %collective-permute-start.12 = (bf16[2,16,4096]{2,1,0:T(8,128)(2,1)S(1)}, bf16[2,16,4096]{2,1,0:T(8,128)(2,1)S(1)}, u32[]{:S(2)}, u32[]{:S(2)}) collective-permute-start(bf16[2,16,4096]{2,1,0:T(8,128)(2,1)S(1)} %collective-permute-done.10.refs_3_.refs_1_), channel_id=1, source_target_pairs={{0,4},{4,0},{8,12},{12,8},{16,20},{20,16},{24,28},{28,24},{1,5},{5... | collective-permute-start | bytes 786440 | tf_op jit(solution)/shard_map/ppermute | solution.py:239
  30.1 16.9 %collective-permute-start.8 = (bf16[2,128,512]{2,1,0:T(8,128)(2,1)S(1)}, bf16[2,128,512]{2,1,0:T(8,128)(2,1)S(1)}, u32[]{:S(2)}, u32[]{:S(2)}) collective-permute-start(bf16[2,128,512]{2,1,0:T(8,128)(2,1)S(1)} %get-tuple-element.64), channel_id=1, source_target_pairs={{0,1},{1,0},{2,3},{3,2},{4,5},{5,4},{6,7},{7,6},{8,9},{9,8},{10,11... | collective-permute-start | bytes 786440 | tf_op jit(solution)/shard_map/ppermute | solution.py:242
  34.3 8.6 %collective-permute-start.2 = (bf16[128,512]{1,0:T(8,128)(2,1)S(1)}, bf16[128,512]{1,0:T(8,128)(2,1)S(1)}, u32[]{:S(2)}, u32[]{:S(2)}) collective-permute-start(bf16[128,512]{1,0:T(8,128)(2,1)S(1)} %fusion.7), channel_id=1, source_target_pairs={{0,2},{1,3},{2,0},{3,1},{4,6},{5,7},{6,4},{7,5},{8,10},{9,11},{10,... | collective-permute-start | bytes 393224 | tf_op jit(solution)/shard_map/ppermute | solution.py:242
  34.3 12.7 %collective-permute-start.13 = (bf16[128,512]{1,0:T(8,128)(2,1)S(1)}, bf16[128,512]{1,0:T(8,128)(2,1)S(1)}, u32[]{:S(2)}, u32[]{:S(2)}) collective-permute-start(bf16[128,512]{1,0:T(8,128)(2,1)S(1)} %get-tuple-element.77), channel_id=1, source_target_pairs={{1,2},{2,1},{5,6},{6,5},{9,10},{10,9},{13,14},{14,13},{17,18},{18,... | collective-permute-start | bytes 393224 | tf_op jit(solution)/shard_map/ppermute | solution.py:309
  42.9 15.9 %collective-permute-start.16 = (bf16[2,128,512]{2,1,0:T(8,128)(2,1)S(1)}, bf16[2,128,512]{2,1,0:T(8,128)(2,1)S(1)}, u32[]{:S(2)}, u32[]{:S(2)}) collective-permute-start(bf16[2,128,512]{2,1,0:T(8,128)(2,1)S(1)} %get-tuple-element.84), channel_id=1, source_target_pairs={{0,1},{1,0},{2,3},{3,2},{4,5},{5,4},{6,7},{7,6},{8,9},{9,8},{10,11... | collective-permute-start | bytes 786440 | tf_op jit(solution)/shard_map/ppermute | solution.py:242
  46.8 7.7 %collective-permute-start.15 = (f32[96,128]{1,0:T(8,128)S(1)}, f32[96,128]{1,0:T(8,128)S(1)}, u32[]{:S(2)}, u32[]{:S(2)}) collective-permute-start(f32[96,128]{1,0:T(8,128)S(1)} %shard_map.72), channel_id=1, source_target_pairs={{0,1},{1,0},{2,3},{3,2},{4,5},{5,4},{6,7},{7,6},{8,9},{9,8},{10,11... | collective-permute-start | bytes 147464 | tf_op jit(solution)/shard_map/ppermute | solution.py:242
  47.0 11.8 %collective-permute-start.17 = (bf16[128,512]{1,0:T(8,128)(2,1)S(1)}, bf16[128,512]{1,0:T(8,128)(2,1)S(1)}, u32[]{:S(2)}, u32[]{:S(2)}) collective-permute-start(bf16[128,512]{1,0:T(8,128)(2,1)S(1)} %get-tuple-element.87), channel_id=1, source_target_pairs={{1,2},{2,1},{5,6},{6,5},{9,10},{10,9},{13,14},{14,13},{17,18},{18,... | collective-permute-start | bytes 393224 | tf_op jit(solution)/shard_map/ppermute | solution.py:309
  47.9 17.3 %collective-permute-start.14 = (bf16[128,512]{1,0:T(8,128)(2,1)S(1)}, bf16[128,512]{1,0:T(8,128)(2,1)S(1)}, u32[]{:S(2)}, u32[]{:S(2)}) collective-permute-start(bf16[128,512]{1,0:T(8,128)(2,1)S(1)} %fusion.5), channel_id=1, source_target_pairs={{0,2},{1,3},{2,0},{3,1},{4,6},{5,7},{6,4},{7,5},{8,10},{9,11},{10,... | collective-permute-start | bytes 393224 | tf_op jit(solution)/shard_map/ppermute | solution.py:242
  53.9 12.8 %collective-permute-start.19 = (bf16[2,128,512]{2,1,0:T(8,128)(2,1)S(1)}, bf16[2,128,512]{2,1,0:T(8,128)(2,1)S(1)}, u32[]{:S(2)}, u32[]{:S(2)}) collective-permute-start(bf16[2,128,512]{2,1,0:T(8,128)(2,1)S(1)} %get-tuple-element.80), channel_id=1, source_target_pairs={{0,1},{1,0},{2,3},{3,2},{4,5},{5,4},{6,7},{7,6},{8,9},{9,8},{10,11... | collective-permute-start | bytes 786440 | tf_op jit(solution)/shard_map/ppermute | solution.py:242
  54.5 7.2 %collective-permute-start.20 = (f32[96,128]{1,0:T(8,128)S(1)}, f32[96,128]{1,0:T(8,128)S(1)}, u32[]{:S(2)}, u32[]{:S(2)}) collective-permute-start(f32[96,128]{1,0:T(8,128)S(1)} %add.20), channel_id=1, source_target_pairs={{0,2},{1,3},{2,0},{3,1},{4,6},{5,7},{6,4},{7,5},{8,10},{9,11},{10,... | collective-permute-start | bytes 147464 | tf_op jit(solution)/shard_map/ppermute | solution.py:242
  61.7 3.4 %collective-permute-start.21 = (bf16[1,96,128]{2,1,0:T(8,128)(2,1)S(1)}, bf16[1,96,128]{2,1,0:T(8,128)(2,1)S(1)}, u32[]{:S(2)}, u32[]{:S(2)}) collective-permute-start(bf16[1,96,128]{2,1,0:T(8,128)(2,1)S(1)} %fusion.8), channel_id=1, source_target_pairs={{0,4},{4,0},{8,12},{12,8},{16,20},{20,16},{24,28},{28,24},{1,5},{5... | collective-permute-start | bytes 73736 | tf_op jit(solution)/shard_map/ppermute | solution.py:239
  61.8 10.1 %collective-permute-start.18 = (bf16[128,512]{1,0:T(8,128)(2,1)S(1)}, bf16[128,512]{1,0:T(8,128)(2,1)S(1)}, u32[]{:S(2)}, u32[]{:S(2)}) collective-permute-start(bf16[128,512]{1,0:T(8,128)(2,1)S(1)} %fusion.3), channel_id=1, source_target_pairs={{0,2},{1,3},{2,0},{3,1},{4,6},{5,7},{6,4},{7,5},{8,10},{9,11},{10,... | collective-permute-start | bytes 393224 | tf_op jit(solution)/shard_map/ppermute | solution.py:242
  64.5 8.8 %collective-permute-start.23 = (bf16[128,512]{1,0:T(8,128)(2,1)S(1)}, bf16[128,512]{1,0:T(8,128)(2,1)S(1)}, u32[]{:S(2)}, u32[]{:S(2)}) collective-permute-start(bf16[128,512]{1,0:T(8,128)(2,1)S(1)} %get-tuple-element.96), channel_id=1, source_target_pairs={{1,2},{2,1},{5,6},{6,5},{9,10},{10,9},{13,14},{14,13},{17,18},{18,... | collective-permute-start | bytes 393224 | tf_op jit(solution)/shard_map/ppermute | solution.py:309
  65.2 4.2 %collective-permute-start.24 = (bf16[2,96,128]{2,1,0:T(8,128)(2,1)S(1)}, bf16[2,96,128]{2,1,0:T(8,128)(2,1)S(1)}, u32[]{:S(2)}, u32[]{:S(2)}) collective-permute-start(bf16[2,96,128]{2,1,0:T(8,128)(2,1)S(1)} %pad_maximum_fusion.2), channel_id=1, source_target_pairs={{0,8},{4,12},{8,0},{12,4},{16,24},{20,28},{24,16},{28,20},{1,9},{5... | collective-permute-start | bytes 147464 | tf_op jit(solution)/shard_map/ppermute | solution.py:239
  71.9 4.7 %collective-permute-start.25 = (bf16[4,96,128]{2,1,0:T(8,128)(2,1)S(1)}, bf16[4,96,128]{2,1,0:T(8,128)(2,1)S(1)}, u32[]{:S(2)}, u32[]{:S(2)}) collective-permute-start(bf16[4,96,128]{2,1,0:T(8,128)(2,1)S(1)} %pad_maximum_fusion.1), channel_id=1, source_target_pairs={{0,16},{4,20},{8,24},{12,28},{16,0},{20,4},{24,8},{28,12},{1,17},{... | collective-permute-start | bytes 294920 | tf_op jit(solution)/shard_map/ppermute | solution.py:239
  72.4 8.4 %collective-permute-start.22 = (bf16[128,512]{1,0:T(8,128)(2,1)S(1)}, bf16[128,512]{1,0:T(8,128)(2,1)S(1)}, u32[]{:S(2)}, u32[]{:S(2)}) collective-permute-start(bf16[128,512]{1,0:T(8,128)(2,1)S(1)} %fusion.1), channel_id=1, source_target_pairs={{0,2},{1,3},{2,0},{3,1},{4,6},{5,7},{6,4},{7,5},{8,10},{9,11},{10,... | collective-permute-start | bytes 393224 | tf_op jit(solution)/shard_map/ppermute | solution.py:242
  (7 other events, 43.9 us)

commit v4 on v3

--- a/solution.py
+++ b/solution.py
@@ -16,6 +16,7 @@
 WIDE = 256
 VMEM = pl.BlockSpec(memory_space=pltpu.VMEM)
 HBM = pl.BlockSpec(memory_space=pltpu.HBM)
+ANY = pl.BlockSpec(memory_space=pl.ANY)
 
 
 def params(mib):
@@ -48,9 +49,15 @@
     return jnp.sum(jnp.where(same, row, 0), axis=1, keepdims=True)
 
 
-def load_kernel(replicas, steps, adapters, weight, request, storage, out, where, inner, sems):
+def load_kernel(replicas, steps, adapters, weight, request_in, storage_in, out, where, request, storage, sems, small):
+    asked_for = pltpu.make_async_copy(request_in, request, small.at[0])
+    stored_at = pltpu.make_async_copy(storage_in, storage, small.at[1])
+    asked_for.start()
+    stored_at.start()
     copies = fetch(weight, out, sems, (1, 3))
-    me, mine = lax.axis_index("replica"), lax.axis_index("tensor")
+    me = lax.axis_index("replica")
+    asked_for.wait()
+    stored_at.wait()
     requests = request.shape[0]
     stored = turned(storage[...].reshape(1, storage.shape[0]))
     count = stored.shape[0]
@@ -76,31 +83,24 @@
             where[rows, 0:1] = slot[mine_here]
             where[rows, 1:2] = place[mine_here] + step * OWN_CAP
             where[rows, 2:3] = column[mine_here] + (step % half) * OWN_CAP
-    inner[...] = jnp.where((mine == 1) | (mine == 2), jnp.ones_like(inner), jnp.zeros_like(inner))
     for copy in copies:
         copy.wait()
 
 
-def outer_dots(rows, weight, near, mid):
-    cols = mid.shape[-1]
-    for at in range(0, cols, WIDE):
-        where = pl.ds(at, WIDE)
-        near[0, :, where] = jnp.dot(
-            rows[...], weight[0, :, where], preferred_element_type=jnp.float32
-        ).astype(near.dtype)
-    for at in range(0, cols, WIDE):
-        where = pl.ds(at, WIDE)
-        value = jnp.dot(
-            rows[...], weight[1, :, where], preferred_element_type=jnp.float32
-        ).astype(near.dtype)
-        near[1, :, where] = value
-        mid[:, where] = value
+def outer_dots(rows, weight, near):
+    cols = near.shape[-1]
+    for slot in range(2):
+        for at in range(0, cols, WIDE):
+            where = pl.ds(at, WIDE)
+            near[slot, :, where] = jnp.dot(
+                rows[...], weight[slot, :, where], preferred_element_type=jnp.float32
+            ).astype(near.dtype)
 
 
 def outer_kernel(n, *refs):
-    parts, weight, near, mid, rows = refs[:n], *refs[n:]
+    parts, weight, near, rows = refs[:n], *refs[n:]
     stack_rows(parts, rows)
-    outer_dots(rows, weight, near, mid)
+    outer_dots(rows, weight, near)
 
 
 def inner_dots(rows, weight, far, own):
@@ -164,34 +164,33 @@
     out[...] = value + rest[2][...] if before else value
 
 
-def up_kernel(packed_rank, up, where, out):
-    total = where.shape[0]
-    slot, column = where[:, 0:1], where[:, 2:3]
-    adapters, rank, cols = up.shape
-    owners, held, _ = packed_rank.shape
-    chosen = (
-        lax.broadcasted_iota(jnp.int32, (total, owners * held), 1) == column
-    ).astype(jnp.bfloat16)
-    both = jnp.dot(
-        chosen, packed_rank[...].reshape(owners * held, 2 * rank), preferred_element_type=jnp.float32
-    )
-    early_rows = total // owners // 2
+def up_kernel(first, before, *refs):
+    ranks, rest = refs[: -4 - before], refs[-4 - before :]
+    up, where, out = rest[0], rest[1], rest[-2]
+    wide = rest[-1]
+    me = lax.axis_index("replica")
+    total, cols = out.shape
+    rank = up.shape[1]
+    held = ranks[0].shape[1]
+    packed_rank = jnp.concatenate([r[...].reshape(-1, r.shape[-1]) for r in ranks], axis=0)
+    owners = packed_rank.shape[0] // held
+    slot, column = where[:, 0:1], where[:, 2:3] - first * held
+    chosen = (lax.broadcasted_iota(jnp.int32, (total, owners * held), 1) == column).astype(jnp.bfloat16)
+    both = jnp.dot(chosen, packed_rank, preferred_element_type=jnp.float32)
+    early_rows = total // lax.axis_size("replica") // 2
     late = (lax.broadcasted_iota(jnp.int32, (total, rank), 0) // early_rows) % 2
-    rank_rows = jnp.where(late == 1, both[:, rank:], both[:, :rank])
-    group = 8
-    wide = jnp.concatenate([rank_rows] * group, axis=1).astype(jnp.bfloat16)
-    adapter_of = lax.broadcasted_iota(jnp.int32, (total, group * rank), 1) // rank
-    local = slot - adapter_of
-    out[...] = jnp.zeros_like(out)
-
-    def step(g, carry):
-        spread = jnp.where(local == g * group, wide, jnp.zeros_like(wide))
-        weight = up[pl.ds(g * group, group)].reshape(group * rank, cols)
-        out[...] += jnp.dot(spread, weight, preferred_element_type=jnp.float32)
-        return carry
-
-    lax.fori_loop(0, adapters // group, step, 0)
-    out[...] = adapter_scale * out[...]
+    rank_rows = adapter_scale * jnp.where(late == 1, both[:, rank:], both[:, :rank])
+    group = wide.shape[1] // rank
+    wide[...] = jnp.concatenate([rank_rows] * group, axis=1).astype(jnp.bfloat16)
+    adapter_of = slot - lax.broadcasted_iota(jnp.int32, wide.shape, 1) // rank
+    made = rest[2][...] if before else None
+    for owner in range(owners):
+        at = (me ^ (first + owner)) * group
+        spread = jnp.where(adapter_of == at, wide[...], jnp.zeros_like(wide))
+        weight = up[pl.ds(at, group)].reshape(group * rank, cols)
+        part = jnp.dot(spread, weight, preferred_element_type=jnp.float32)
+        made = part if made is None else made + part
+    out[...] = made
 
 
 def finish_kernel(pieces, *refs):
@@ -200,15 +199,15 @@
     me = lax.axis_index("replica")
     at = 0
     for order in pieces:
-        own, near, far, mid = refs[at : at + 4]
-        at += 4
+        own, near, far = refs[at : at + 3]
+        at += 3
         rows = own.shape[0] // len(order)
         requests = rows // steps
         for i, k in enumerate(order):
             here = pl.ds(i * rows, rows)
             who = me ^ k
             total = own[here, :] + near[0, here, :].astype(jnp.float32)
-            total += far[here, :].astype(jnp.float32) + mid[here, :].astype(jnp.float32)
+            total += far[here, :].astype(jnp.float32)
             total += delta[pl.ds(pl.multiple_of(who * rows, rows), rows), :]
             out[:, pl.ds(pl.multiple_of(who * requests, requests), requests), :] = total.astype(
                 out.dtype
@@ -254,7 +253,7 @@
         passed.extend(values)
 
     def cost(n, width):
-        return pl.CostEstimate(flops=n * width, bytes_accessed=n, transcendentals=0)
+        return pl.CostEstimate(flops=2 * n * feats * width, bytes_accessed=2 * n * feats, transcendentals=0)
 
     held = pltpu.VMEM((2, feats, cols), jnp.bfloat16)
     copies = pltpu.SemaphoreType.DMA((2,))
@@ -263,12 +262,9 @@
         n = sum(p.shape[0] * p.shape[1] for p in parts)
         return pl.pallas_call(
             functools.partial(outer_kernel, len(parts)),
-            out_shape=[
-                jax.ShapeDtypeStruct((2, n, cols), jnp.bfloat16),
-                jax.ShapeDtypeStruct((n, cols), jnp.bfloat16),
-            ],
+            out_shape=jax.ShapeDtypeStruct((2, n, cols), jnp.bfloat16),
             in_specs=[VMEM] * (len(parts) + 1),
-            out_specs=[VMEM, VMEM],
+            out_specs=VMEM,
             scratch_shapes=[pltpu.VMEM((n, feats), jnp.bfloat16)],
             compiler_params=params(8),
             cost_estimate=cost(n, 2 * cols),
@@ -301,125 +297,102 @@
         )(*parts, down, where, *before)
 
     def pass_on(far, near_in):
-        both = far + jnp.where(inner > 0, near_in[1].astype(jnp.float32), 0.0)
-        both = both.astype(jnp.bfloat16)
-        return along(both, 2), both
-
-    def across(mid):
-        return lax.ppermute(mid, "tensor", [(1, 2), (2, 1)])
+        return (far + near_in[1].astype(jnp.float32)).astype(jnp.bfloat16)
 
     x0 = attention_output
     x1, x2, x4 = swap(x0, 1), swap(x0, 2), swap(x0, 4)
     weight = pltpu.with_memory_space_constraint(output_weight, pltpu.HBM)
-    held_out, where, inner = pl.pallas_call(
+    held_out, where = pl.pallas_call(
         functools.partial(load_kernel, replicas, steps, adapters_here),
-        out_shape=[
-            held,
-            jax.ShapeDtypeStruct((replicas * rows, 8), jnp.int32),
-            jax.ShapeDtypeStruct((1, cols), jnp.float32),
+        out_shape=[held, jax.ShapeDtypeStruct((replicas * rows, 8), jnp.int32)],
+        in_specs=[HBM] * 3,
+        out_specs=[VMEM] * 2,
+        scratch_shapes=[
+            pltpu.VMEM(request_adapter.shape, jnp.int32),
+            pltpu.VMEM(adapter_storage_row.shape, jnp.int32),
+            copies,
+            copies,
         ],
-        in_specs=[HBM, VMEM, VMEM],
-        out_specs=[VMEM] * 3,
-        scratch_shapes=[copies],
         compiler_params=params(4),
-    )(weight, request_adapter, adapter_storage_row)
-    near0, mid0 = outer([x0, x1], held_out)
+    )(weight, *(pltpu.with_memory_space_constraint(v, pltpu.HBM) for v in (request_adapter, adapter_storage_row)))
+    near0 = outer([x0, x1], held_out)
     done(near0)
-    near0_in, mid0_in = along(near0, 1), across(mid0)
+    near0_in = along(near0, 1)
     far0, own0, held_in = inside([tie(x0), x1], weight, True)
     done(own0)
-    packed = ranked((0, 1), [tie(x0), x1])
-    done(packed)
-    far0_in, sent = pass_on(far0, tie(near0_in))
-    wait(sent)
-
-    wait(x2, x4, mid0_in)
+
+    wait(x2, x4, near0_in)
     x2, x4 = tie(x2, x4)
-    x3, x6a = swap(x2, 1), swap(x2[:half], 4)
-    x5, x6b = swap(x4, 1), swap(x4[half:], 2)
-    wait(x3)
-    near1, mid1 = outer([tie(x2), x3], held_out)
+    x3, x5 = swap(x2, 1), swap(x4, 1)
+    x6a, x6b = swap(x2[:half], 4), swap(x4[half:], 2)
+    near1 = outer([x2, x3, x4, x5], held_out)
     done(near1)
     near1_in = along(near1, 1)
-    wait(x5)
-    mid1_in = across(tie(mid1))
-    far1, own1 = inside([tie(x2), x3], held_in)
+    far0_out = pass_on(far0, tie(near0_in))
+    far0_in = along(far0_out, 2)
+    wait(far0_out)
+    far1, own1 = inside([tie(x2), x3, x4, x5], held_in)
     done(own1)
-    packed = ranked((2, 3), [tie(x2), x3], packed)
+    packed = ranked((0, 1, 2, 3, 4, 5), [tie(x0), x1, x2, x3, x4, x5])
     done(packed)
 
     wait(x6a, x6b)
     x6a, x6b = tie(x6a, x6b)
     x7a, x7b = swap(x6a, 1), swap(x6b, 1)
-    near2, mid2 = outer([tie(x4), x5], held_out)
-    done(near2)
-    wait(x7a, x7b, far0_in)
-    near2_in, mid2_in = along(tie(near2), 1), across(tie(mid2))
-    packed = ranked((4, 5, 6, 7), [tie(x4), x5, x6a, x6b, x7a, x7b], packed)
+    packed = ranked((6, 7), [x6a, x6b, x7a, x7b], packed)
     done(packed)
     packed_in = along(packed, 1)
-    wait(near1_in, mid1_in)
-    far1_in, sent = pass_on(far1, tie(near1_in))
-    wait(sent)
-    near3, mid3 = outer([tie(x6a), x6b, x7a, x7b], held_out)
-    done(near3)
-    near3_in = along(near3, 1)
-    wait(packed_in)
+    near2 = outer([tie(x6a), x6b, x7a, x7b], held_out)
+    done(near2)
+    near2_in = along(near2, 1)
+    wait(far0_in)
+    far1_out = pass_on(far1, tie(near1_in))
+    wait(far1_out, packed_in)
     packed = packed + tie(packed_in)
     done(packed)
     packed_in = along(packed, 2)
-    far2, own2 = inside([tie(x4), x5], held_in)
+    far1_in = along(far1_out, 2)
+    far2, own2 = inside([tie(x6a), x6b, x7a, x7b], held_in)
     done(own2)
-    wait(mid2_in, near2_in)
-    mid3_in = across(tie(mid3))
-    far2_in, sent = pass_on(far2, tie(near2_in))
-    wait(sent)
-    far3, own3 = inside([tie(x6a), x6b, x7a, x7b], held_in)
-    done(own3)
+    far2_out = pass_on(far2, tie(near2_in))
+    far2_in = along(far2_out, 2)
+    wait(far2_out)
+
+    def up(first, ranks, *before):
+        return pl.pallas_call(
+            functools.partial(up_kernel, first, len(before)),
+            out_shape=jax.ShapeDtypeStruct((replicas * rows, cols), jnp.float32),
+            in_specs=[VMEM] * (len(ranks) + 2 + len(before)),
+            out_specs=VMEM,
+            scratch_shapes=[pltpu.VMEM((replicas * rows, adapters_here * rank), jnp.bfloat16)],
+            compiler_params=params(12),
+        )(*ranks, adapter_up_weight, where, *before)
+
     wait(packed_in)
     ranks = (packed + tie(packed_in)).astype(jnp.bfloat16)[None]
     done(ranks)
     got = swap(ranks, 1)
-    wait(far1_in, got)
+    wait(got)
     ranks = jnp.concatenate([ranks, tie(got)], axis=0)
     done(ranks)
-    got = swap(ranks, 2)
-    wait(near3_in)
-    far3_in, sent = pass_on(far3, tie(near3_in))
-    wait(sent, got, far2_in)
-    ranks = jnp.concatenate([ranks, tie(got)], axis=0)
-    done(ranks)
-    got = swap(ranks, 4)
-    wait(got, mid3_in)
-    ranks = jnp.concatenate([ranks, tie(got)], axis=0)
-
-    delta = pl.pallas_call(
-        up_kernel,
-        out_shape=jax.ShapeDtypeStruct((replicas * rows, cols), jnp.float32),
-        in_specs=[VMEM] * 3,
-        out_specs=VMEM,
-        compiler_params=params(12),
-        cost_estimate=pl.CostEstimate(
-            flops=2 * replicas * rows * cols * adapter_up_weight.shape[0] * rank,
-            bytes_accessed=4 * MIB,
-            transcendentals=0,
-        ),
-    )(ranks, adapter_up_weight, where)
-
-    pieces = [(0, 1), (2, 3), (4, 5), (6, 7)]
-    shares = [
-        (own0, near0_in, far0_in, mid0_in),
-        (own1, near1_in, far1_in, mid1_in),
-        (own2, near2_in, far2_in, mid2_in),
-        (own3, near3_in, far3_in, mid3_in),
-    ]
+    got2, got4, got6 = (swap(ranks, bits) for bits in (2, 4, 6))
+    delta = up(0, [tie(ranks)])
+    done(delta)
+    wait(got2, got4)
+    delta = up(2, [tie(got2), got4], delta)
+    done(delta)
+    wait(got6, far1_in)
+    delta = up(6, [tie(got6)], delta)
+
+    pieces = [(0, 1), (2, 3, 4, 5), (6, 7)]
+    arrived = [(own0, near0_in, far0_in), (own1, near1_in, far1_in), (own2, near2_in, far2_in)]
     return pl.pallas_call(
         functools.partial(finish_kernel, pieces),
         out_shape=jax.ShapeDtypeStruct((steps, requests, cols), jnp.bfloat16),
-        in_specs=[VMEM] * 17,
+        in_specs=[VMEM] * 10,
         out_specs=VMEM,
         compiler_params=params(12),
-    )(*[ref for share in shares for ref in share], delta)
+    )(*[ref for piece in arrived for ref in piece], delta)
 
 
 def on_device(

time: 82.1 us -> 66.4 us (0.81); the launches traced: 81.9 us -> 65.1 us
  starting transfers between devices: 31.5 us -> 23.3 us
  waiting for transfers between devices: 19.8 us -> 14.9 us
  Pallas kernels: 28.6 us -> 26.4 us
  local copies, waits for them, and re-layouts: 1.36 us -> 0.05 us
    ppermute x10 -> x8, starting transfers between devices: 19.7 us -> 12.3 us  [along(): return lax.ppermute(value, 'tensor', flip(tensors, bits))]
    ppermute x12 -> x13, waiting for transfers between devices: 8.99 us -> 2.83 us  [swap(): return lax.ppermute(value, 'replica', flip(replicas, bits))]
    ppermute x4 -> x0, starting transfers between devices: 2.95 us -> none  [across(): return lax.ppermute(mid, 'tensor', [(1, 2), (2, 1)])]
    ppermute x12 -> x13, starting transfers between devices: 8.89 us -> 11 us  [swap(): return lax.ppermute(value, 'replica', flip(replicas, bits))]
    pallas_call x3 -> x2, Pallas kernels: 5.85 us -> 4.4 us  [ranked(): pl.pallas_call(functools.partial(rank_kernel, order, len(before) > 0, len...]
    unnamed x10 -> x6, local copies, waits for them, and re-layouts: 1.32 us -> 0.02 us
    ppermute x10 -> x8, waiting for transfers between devices: 10.8 us -> 12.1 us  [along(): return lax.ppermute(value, 'tensor', flip(tensors, bits))]
    pallas_call x4 -> x3, Pallas kernels: 8.9 us -> 8.37 us  [inside(): pl.pallas_call(functools.partial(first_inner_kernel if first else inner_k...]
  transfers between devices with their start and end apart: 26 -> 21, of which waited for: 8 -> 10; matrix products, arithmetic and copies ran while one was open for 0% -> 0% of each run, Pallas kernels for 34% -> 39%
where the time goes in v4:
time: 66.4 us; the launch traced here: 65.1 us
  Pallas kernels  26.4 us (40%)
  starting transfers between devices  23.3 us (35%)
  waiting for transfers between devices  14.9 us (22%)
    ppermute x8, starting transfers between devices, along(): return lax.ppermute(value, 'tensor', flip(tensors, bits))  12.3 us
    ppermute x8, waiting for transfers between devices, along(): return lax.ppermute(value, 'tensor', flip(tensors, bits))  12.1 us
    ppermute x13, starting transfers between devices, swap(): return lax.ppermute(value, 'replica', flip(replicas, bits))  11 us
    pallas_call x3, Pallas kernels, inside(): pl.pallas_call(functools.partial(first_inner_kernel if first else inner_k...  8.37 us
    pallas_call x3, Pallas kernels, outer(): pl.pallas_call(functools.partial(outer_kernel, len(parts)), out_shape=jax...  4.83 us
    pallas_call x2, Pallas kernels, ranked(): pl.pallas_call(functools.partial(rank_kernel, order, len(before) > 0, len...  4.4 us
    pallas_call x3, Pallas kernels, up(): pl.pallas_call(functools.partial(up_kernel, first, len(before)), out_shap...  4.24 us
    pallas_call x1, Pallas kernels, on_device_blocks(): pl.pallas_call(functools.partial(load_kernel, replicas, steps, adapters_h...  3.58 us
  transfers between devices with their start and end apart: 21, of which 10 were waited for; matrix products, arithmetic and copies ran while one was open for 0% of the time, Pallas kernels for 39%

profile of v4, /device:TPU:0, one launch (start us, length us, event | category | flops | bytes accessed | tf_op | source)
XLA Modules:
  0.0 65.1 jit_solution(6349650892335290291)
XLA Ops:
  0.5 2.5 %collective-permute-start.2 = (bf16[4,16,4096]{2,1,0:T(8,128)(2,1)}, bf16[4,16,4096]{2,1,0:T(8,128)(2,1)S(1)}, u32[]{:S(2)}, u32[]{:S(2)}) collective-permute-start(bf16[4,16,4096]{2,1,0:T(8,128)(2,1)} %refs_0_.3), channel_id=1, source_target_pairs={{0,8},{4,12},{8,0},{12,4},{16,24},{20,28},{24,16},{28,20},{1,9},{5... | collective-permute-start | bytes 1572872 | tf_op jit(solution)/shard_map/ppermute | solution.py:238
  3.0 1.5 %collective-permute-start.3 = (bf16[4,16,4096]{2,1,0:T(8,128)(2,1)}, bf16[4,16,4096]{2,1,0:T(8,128)(2,1)S(1)}, u32[]{:S(2)}, u32[]{:S(2)}) collective-permute-start(bf16[4,16,4096]{2,1,0:T(8,128)(2,1)} %refs_0_.3), channel_id=1, source_target_pairs={{0,16},{4,20},{8,24},{12,28},{16,0},{20,4},{24,8},{28,12},{1,17},{... | collective-permute-start | bytes 1572872 | tf_op jit(solution)/shard_map/ppermute | solution.py:238
  4.5 3.6 %shard_map.64 = (bf16[2,4096,512]{2,1,0:T(8,128)(2,1)S(1)}, s32[512,8]{1,0:T(8,128)S(1)}) custom-call(bf16[4096,2048]{1,0:T(8,128)(2,1)} %refs_2_.2, s32[128]{0:T(128)} %request_in.1, s32[64]{0:T(128)} %storage_in.1), custom_call_target="tpu_custom_call" | custom-call | tf_op jit(solution)/shard_map/pallas_call | solution.py:305
  9.4 1.6 %collective-permute-start.1 = (bf16[2,128,512]{2,1,0:T(8,128)(2,1)S(1)}, bf16[2,128,512]{2,1,0:T(8,128)(2,1)S(1)}, u32[]{:S(2)}, u32[]{:S(2)}) collective-permute-start(bf16[2,128,512]{2,1,0:T(8,128)(2,1)S(1)} %shard_map.65), channel_id=1, source_target_pairs={{0,1},{1,0},{2,3},{3,2},{4,5},{5,4},{6,7},{7,6},{8,9},{9,8},{10,11... | collective-permute-start | bytes 786440 | tf_op jit(solution)/shard_map/ppermute | solution.py:241
  11.0 4.8 %shard_map.66 = (f32[128,512]{1,0:T(8,128)S(1)}, f32[128,512]{1,0:T(8,128)S(1)}, bf16[2,4096,512]{2,1,0:T(8,128)(2,1)S(1)}) custom-call(bf16[4,16,4096]{2,1,0:T(8,128)(2,1)S(1)} %copy-done.2, bf16[4,16,4096]{2,1,0:T(8,128)(2,1)S(1)} %collective-permute-done.refs_1_, bf16[4096,2048]{1,0:T(8,128)(2,1)} %refs_2_.2), custom_call_target="tpu_custom_call" | custom-call | flops 1073741824 | bytes 1048576 | tf_op jit(solution)/shard_map/pallas_call | solution.py:275
  15.8 1.4 %collective-permute-done.3.refs_2_.refs_4_ = bf16[4,16,4096]{2,1,0:T(8,128)(2,1)S(1)} collective-permute-done((bf16[4,16,4096]{2,1,0:T(8,128)(2,1)}, bf16[4,16,4096]{2,1,0:T(8,128)(2,1)S(1)}, u32[]{:S(2)}, u32[]{:S(2)}) %collective-permute-start.3) | collective-permute-done | bytes 524320 | tf_op jit(solution)/shard_map/ppermute | solution.py:238
  20.2 2.3 %shard_map.67 = bf16[2,256,512]{2,1,0:T(8,128)(2,1)S(1)} custom-call(bf16[4,16,4096]{2,1,0:T(8,128)(2,1)S(1)} %collective-permute-done.2.refs_0_.refs_2_, bf16[4,16,4096]{2,1,0:T(8,128)(2,1)S(1)} %collective-permute-done.4.refs_1_.refs_3_, bf16[4,16,4096]{2,1,0:T(8,128)(2,1)S(1)} %collective-permute-done.3.refs_2_.refs_4_, ...), custom_call_target="tpu_custom_call" | custom-call | flops 2147483648 | bytes 2097152 | tf_op jit(solution)/shard_map/pallas_call | solution.py:263
  22.5 1.6 %collective-permute-start.7 = (bf16[2,256,512]{2,1,0:T(8,128)(2,1)S(1)}, bf16[2,256,512]{2,1,0:T(8,128)(2,1)S(1)}, u32[]{:S(2)}, u32[]{:S(2)}) collective-permute-start(bf16[2,256,512]{2,1,0:T(8,128)(2,1)S(1)} %shard_map.67), channel_id=1, source_target_pairs={{0,1},{1,0},{2,3},{3,2},{4,5},{5,4},{6,7},{7,6},{8,9},{9,8},{10,11... | collective-permute-start | bytes 1572872 | tf_op jit(solution)/shard_map/ppermute | solution.py:241
  24.2 2.3 %shard_map.68 = (f32[256,512]{1,0:T(8,128)S(1)}, f32[256,512]{1,0:T(8,128)S(1)}) custom-call(bf16[4,16,4096]{2,1,0:T(8,128)(2,1)S(1)} %collective-permute-done.2.refs_0_.refs_2_, bf16[4,16,4096]{2,1,0:T(8,128)(2,1)S(1)} %collective-permute-done.4.refs_1_.refs_3_, bf16[4,16,4096]{2,1,0:T(8,128)(2,1)S(1)} %collective-permute-done.3.refs_2_.refs_4_, ...), custom_call_target="tpu_custom_call" | custom-call | flops 2147483648 | bytes 2097152 | tf_op jit(solution)/shard_map/pallas_call | solution.py:275
  26.5 2.5 %shard_map.69.refs_6_ = f32[96,128]{1,0:T(8,128)S(1)} custom-call(bf16[4,16,4096]{2,1,0:T(8,128)(2,1)S(1)} %copy-done.2, bf16[4,16,4096]{2,1,0:T(8,128)(2,1)S(1)} %collective-permute-done.refs_1_, bf16[4,16,4096]{2,1,0:T(8,128)(2,1)S(1)} %collective-permute-done.2.refs_0_.refs_2_, bf16[4,16,4096]{2,1,0:T(8,128)(2,1)S(1)} %collective-permute-done.4.refs_1_.refs_3_, ...), custom_call_target="tpu_custom_call" | custom-call | flops 1610612736 | bytes 3145728 | tf_op jit(solution)/shard_map/pallas_call | solution.py:289
  29.6 2.6 %collective-permute-start.6 = (bf16[128,512]{1,0:T(8,128)(2,1)S(1)}, bf16[128,512]{1,0:T(8,128)(2,1)S(1)}, u32[]{:S(2)}, u32[]{:S(2)}) collective-permute-start(bf16[128,512]{1,0:T(8,128)(2,1)S(1)} %fusion.2), channel_id=1, source_target_pairs={{0,2},{1,3},{2,0},{3,1},{4,6},{5,7},{6,4},{7,5},{8,10},{9,11},{10,... | collective-permute-start | bytes 393224 | tf_op jit(solution)/shard_map/ppermute | solution.py:241
  32.2 1.9 %shard_map.70 = f32[96,128]{1,0:T(8,128)S(1)} custom-call(bf16[2,16,4096]{2,1,0:T(8,128)(2,1)S(1)} %collective-permute-done.8.refs_0_, bf16[2,16,4096]{2,1,0:T(8,128)(2,1)S(1)} %collective-permute-done.9.refs_1_, bf16[2,16,4096]{2,1,0:T(8,128)(2,1)S(1)} %collective-permute-done.10.refs_2_, bf16[2,16,4096]{2,1,0:T(8,128)(2,1)S(1)} %collective-permute-done.11.refs_3_, ...), custom_call_target="tpu_custom_call" | custom-call | flops 536870912 | bytes 1048576 | tf_op jit(solution)/shard_map/pallas_call | solution.py:289
  34.7 1.3 %shard_map.71 = bf16[2,128,512]{2,1,0:T(8,128)(2,1)S(1)} custom-call(bf16[2,16,4096]{2,1,0:T(8,128)(2,1)S(1)} %collective-permute-done.8.refs_0_, bf16[2,16,4096]{2,1,0:T(8,128)(2,1)S(1)} %collective-permute-done.9.refs_1_, bf16[2,16,4096]{2,1,0:T(8,128)(2,1)S(1)} %collective-permute-done.10.refs_2_, ...), custom_call_target="tpu_custom_call" | custom-call | flops 1073741824 | bytes 1048576 | tf_op jit(solution)/shard_map/pallas_call | solution.py:263
  36.0 1.6 %collective-permute-start.14 = (bf16[2,128,512]{2,1,0:T(8,128)(2,1)S(1)}, bf16[2,128,512]{2,1,0:T(8,128)(2,1)S(1)}, u32[]{:S(2)}, u32[]{:S(2)}) collective-permute-start(bf16[2,128,512]{2,1,0:T(8,128)(2,1)S(1)} %shard_map.71), channel_id=1, source_target_pairs={{0,1},{1,0},{2,3},{3,2},{4,5},{5,4},{6,7},{7,6},{8,9},{9,8},{10,11... | collective-permute-start | bytes 786440 | tf_op jit(solution)/shard_map/ppermute | solution.py:241
  37.6 1.7 %collective-permute-done.6.refs_2_ = bf16[128,512]{1,0:T(8,128)(2,1)S(1)} collective-permute-done((bf16[128,512]{1,0:T(8,128)(2,1)S(1)}, bf16[128,512]{1,0:T(8,128)(2,1)S(1)}, u32[]{:S(2)}, u32[]{:S(2)}) %collective-permute-start.6) | collective-permute-done | bytes 131104 | tf_op jit(solution)/shard_map/ppermute | solution.py:241
  41.2 2.6 %collective-permute-start.16 = (f32[96,128]{1,0:T(8,128)S(1)}, f32[96,128]{1,0:T(8,128)S(1)}, u32[]{:S(2)}, u32[]{:S(2)}) collective-permute-start(f32[96,128]{1,0:T(8,128)S(1)} %add.17), channel_id=1, source_target_pairs={{0,2},{1,3},{2,0},{3,1},{4,6},{5,7},{6,4},{7,5},{8,10},{9,11},{10,... | collective-permute-start | bytes 147464 | tf_op jit(solution)/shard_map/ppermute | solution.py:241
  45.5 3.6 %collective-permute-done.14.refs_7_ = bf16[2,128,512]{2,1,0:T(8,128)(2,1)S(1)} collective-permute-done((bf16[2,128,512]{2,1,0:T(8,128)(2,1)S(1)}, bf16[2,128,512]{2,1,0:T(8,128)(2,1)S(1)}, u32[]{:S(2)}, u32[]{:S(2)}) %collective-permute-start.14) | collective-permute-done | bytes 262176 | tf_op jit(solution)/shard_map/ppermute | solution.py:241
  49.2 1.4 %collective-permute-start.15 = (bf16[128,512]{1,0:T(8,128)(2,1)S(1)}, bf16[128,512]{1,0:T(8,128)(2,1)S(1)}, u32[]{:S(2)}, u32[]{:S(2)}) collective-permute-start(bf16[128,512]{1,0:T(8,128)(2,1)S(1)} %fusion.1), channel_id=1, source_target_pairs={{0,2},{1,3},{2,0},{3,1},{4,6},{5,7},{6,4},{7,5},{8,10},{9,11},{10,... | collective-permute-start | bytes 393224 | tf_op jit(solution)/shard_map/ppermute | solution.py:241
  50.6 1.4 %collective-permute-start.19 = (bf16[2,96,128]{2,1,0:T(8,128)(2,1)S(1)}, bf16[2,96,128]{2,1,0:T(8,128)(2,1)S(1)}, u32[]{:S(2)}, u32[]{:S(2)}) collective-permute-start(bf16[2,96,128]{2,1,0:T(8,128)(2,1)S(1)} %pad_maximum_fusion.refs_0_), channel_id=1, source_target_pairs={{0,8},{4,12},{8,0},{12,4},{16,24},{20,28},{24,16},{28,20},{1,9},{5... | collective-permute-start | bytes 147464 | tf_op jit(solution)/shard_map/ppermute | solution.py:238
  52.8 1.4 %collective-permute-start.18 = (bf16[2,96,128]{2,1,0:T(8,128)(2,1)S(1)}, bf16[2,96,128]{2,1,0:T(8,128)(2,1)S(1)}, u32[]{:S(2)}, u32[]{:S(2)}) collective-permute-start(bf16[2,96,128]{2,1,0:T(8,128)(2,1)S(1)} %pad_maximum_fusion.refs_0_), channel_id=1, source_target_pairs={{0,24},{4,28},{8,16},{12,20},{16,8},{20,12},{24,0},{28,4},{1,25},{... | collective-permute-start | bytes 147464 | tf_op jit(solution)/shard_map/ppermute | solution.py:238
  54.2 1.3 %shard_map.73.refs_4_ = f32[512,512]{1,0:T(8,128)S(1)} custom-call(bf16[2,96,128]{2,1,0:T(8,128)(2,1)S(1)} %pad_maximum_fusion.refs_0_, bf16[64,64,512]{2,1,0:T(8,128)(2,1)S(1)} %copy-done, s32[512,8]{1,0:T(8,128)S(1)} %get-tuple-element.44.refs_7_.refs_5_.refs_2_.refs_3_), custom_call_target="tpu_custom_call" | custom-call | tf_op jit(solution)/shard_map/pallas_call | solution.py:362
  56.6 1.7 %shard_map.74.refs_3_ = f32[512,512]{1,0:T(8,128)S(1)} custom-call(bf16[2,96,128]{2,1,0:T(8,128)(2,1)S(1)} %collective-permute-done.19.refs_0_, bf16[2,96,128]{2,1,0:T(8,128)(2,1)S(1)} %collective-permute-done.20.refs_1_, bf16[64,64,512]{2,1,0:T(8,128)(2,1)S(1)} %copy-done, s32[512,8]{1,0:T(8,128)S(1)} %get-tuple-element.44.refs_7_.refs_5_.refs_2_.refs_3_, ...), custom_call_target="tpu_custom_call" | custom-call | tf_op jit(solution)/shard_map/pallas_call | solution.py:362
  58.4 1.5 %collective-permute-done.12.refs_5_ = bf16[256,512]{1,0:T(8,128)(2,1)S(1)} collective-permute-done((bf16[256,512]{1,0:T(8,128)(2,1)S(1)}, bf16[256,512]{1,0:T(8,128)(2,1)S(1)}, u32[]{:S(2)}, u32[]{:S(2)}) %collective-permute-start.12) | collective-permute-done | bytes 262176 | tf_op jit(solution)/shard_map/ppermute | solution.py:241
  61.0 3.0 %collective-permute-done.15.refs_8_ = bf16[128,512]{1,0:T(8,128)(2,1)S(1)} collective-permute-done((bf16[128,512]{1,0:T(8,128)(2,1)S(1)}, bf16[128,512]{1,0:T(8,128)(2,1)S(1)}, u32[]{:S(2)}, u32[]{:S(2)}) %collective-permute-start.15) | collective-permute-done | bytes 131104 | tf_op jit(solution)/shard_map/ppermute | solution.py:241
  (45 shorter events, 13.6 us)
Async XLA Ops:
  0.0 8.1 %copy-start.2 = (bf16[4,16,4096]{2,1,0:T(8,128)(2,1)S(1)}, bf16[4,16,4096]{2,1,0:T(8,128)(2,1)}, u32[]{:S(2)}) copy-start(bf16[4,16,4096]{2,1,0:T(8,128)(2,1)} %refs_0_.3) | copy-start | bytes 1572868
  0.0 8.1 %collective-permute-start = (bf16[4,16,4096]{2,1,0:T(8,128)(2,1)}, bf16[4,16,4096]{2,1,0:T(8,128)(2,1)S(1)}, u32[]{:S(2)}, u32[]{:S(2)}) collective-permute-start(bf16[4,16,4096]{2,1,0:T(8,128)(2,1)} %refs_0_.3), channel_id=1, source_target_pairs={{0,4},{4,0},{8,12},{12,8},{16,20},{20,16},{24,28},{28,24},{1,5},{5... | collective-permute-start | bytes 1572872 | tf_op jit(solution)/shard_map/ppermute | solution.py:238
  0.5 15.3 %collective-permute-start.2 = (bf16[4,16,4096]{2,1,0:T(8,128)(2,1)}, bf16[4,16,4096]{2,1,0:T(8,128)(2,1)S(1)}, u32[]{:S(2)}, u32[]{:S(2)}) collective-permute-start(bf16[4,16,4096]{2,1,0:T(8,128)(2,1)} %refs_0_.3), channel_id=1, source_target_pairs={{0,8},{4,12},{8,0},{12,4},{16,24},{20,28},{24,16},{28,20},{1,9},{5... | collective-permute-start | bytes 1572872 | tf_op jit(solution)/shard_map/ppermute | solution.py:238
  3.0 14.2 %collective-permute-start.3 = (bf16[4,16,4096]{2,1,0:T(8,128)(2,1)}, bf16[4,16,4096]{2,1,0:T(8,128)(2,1)S(1)}, u32[]{:S(2)}, u32[]{:S(2)}) collective-permute-start(bf16[4,16,4096]{2,1,0:T(8,128)(2,1)} %refs_0_.3), channel_id=1, source_target_pairs={{0,16},{4,20},{8,24},{12,28},{16,0},{20,4},{24,8},{28,12},{1,17},{... | collective-permute-start | bytes 1572872 | tf_op jit(solution)/shard_map/ppermute | solution.py:238
  9.4 8.2 %collective-permute-start.1 = (bf16[2,128,512]{2,1,0:T(8,128)(2,1)S(1)}, bf16[2,128,512]{2,1,0:T(8,128)(2,1)S(1)}, u32[]{:S(2)}, u32[]{:S(2)}) collective-permute-start(bf16[2,128,512]{2,1,0:T(8,128)(2,1)S(1)} %shard_map.65), channel_id=1, source_target_pairs={{0,1},{1,0},{2,3},{3,2},{4,5},{5,4},{6,7},{7,6},{8,9},{9,8},{10,11... | collective-permute-start | bytes 786440 | tf_op jit(solution)/shard_map/ppermute | solution.py:241
  17.6 2.4 %collective-permute-start.4 = (bf16[4,16,4096]{2,1,0:T(8,128)(2,1)S(1)}, bf16[4,16,4096]{2,1,0:T(8,128)(2,1)S(1)}, u32[]{:S(2)}, u32[]{:S(2)}) collective-permute-start(bf16[4,16,4096]{2,1,0:T(8,128)(2,1)S(1)} %collective-permute-done.2.refs_0_.refs_2_), channel_id=1, source_target_pairs={{0,4},{4,0},{8,12},{12,8},{16,20},{20,16},{24,28},{28,24},{1,5},{5... | collective-permute-start | bytes 1572872 | tf_op jit(solution)/shard_map/ppermute | solution.py:238
  17.6 2.7 %collective-permute-start.5 = (bf16[4,16,4096]{2,1,0:T(8,128)(2,1)S(1)}, bf16[4,16,4096]{2,1,0:T(8,128)(2,1)S(1)}, u32[]{:S(2)}, u32[]{:S(2)}) collective-permute-start(bf16[4,16,4096]{2,1,0:T(8,128)(2,1)S(1)} %collective-permute-done.3.refs_2_.refs_4_), channel_id=1, source_target_pairs={{0,4},{4,0},{8,12},{12,8},{16,20},{20,16},{24,28},{28,24},{1,5},{5... | collective-permute-start | bytes 1572872 | tf_op jit(solution)/shard_map/ppermute | solution.py:238
  18.1 8.4 %copy-start.1 = (bf16[8,4096,64]{1,2,0:T(8,128)(2,1)S(1)}, bf16[8,4096,64]{1,2,0:T(8,128)(2,1)}, u32[]{:S(2)}) copy-start(bf16[8,4096,64]{1,2,0:T(8,128)(2,1)} %param.8) | copy-start | bytes 12582916
  18.1 10.9 %collective-permute-start.8 = (bf16[2,16,4096]{2,1,0:T(8,128)(2,1)S(1)}, bf16[2,16,4096]{2,1,0:T(8,128)(2,1)S(1)}, u32[]{:S(2)}, u32[]{:S(2)}) collective-permute-start(bf16[2,16,4096]{2,1,0:T(8,128)(2,1)S(1)} %slice.16), channel_id=1, source_target_pairs={{0,16},{4,20},{8,24},{12,28},{16,0},{20,4},{24,8},{28,12},{1,17},{... | collective-permute-start | bytes 786440 | tf_op jit(solution)/shard_map/ppermute | solution.py:238
  19.4 9.6 %collective-permute-start.9 = (bf16[2,16,4096]{2,1,0:T(8,128)(2,1)S(1)}, bf16[2,16,4096]{2,1,0:T(8,128)(2,1)S(1)}, u32[]{:S(2)}, u32[]{:S(2)}) collective-permute-start(bf16[2,16,4096]{2,1,0:T(8,128)(2,1)S(1)} %slice.17), channel_id=1, source_target_pairs={{0,8},{4,12},{8,0},{12,4},{16,24},{20,28},{24,16},{28,20},{1,9},{5... | collective-permute-start | bytes 786440 | tf_op jit(solution)/shard_map/ppermute | solution.py:238
  22.5 17.6 %collective-permute-start.7 = (bf16[2,256,512]{2,1,0:T(8,128)(2,1)S(1)}, bf16[2,256,512]{2,1,0:T(8,128)(2,1)S(1)}, u32[]{:S(2)}, u32[]{:S(2)}) collective-permute-start(bf16[2,256,512]{2,1,0:T(8,128)(2,1)S(1)} %shard_map.67), channel_id=1, source_target_pairs={{0,1},{1,0},{2,3},{3,2},{4,5},{5,4},{6,7},{7,6},{8,9},{9,8},{10,11... | collective-permute-start | bytes 1572872 | tf_op jit(solution)/shard_map/ppermute | solution.py:241
  29.0 3.2 %collective-permute-start.10 = (bf16[2,16,4096]{2,1,0:T(8,128)(2,1)S(1)}, bf16[2,16,4096]{2,1,0:T(8,128)(2,1)S(1)}, u32[]{:S(2)}, u32[]{:S(2)}) collective-permute-start(bf16[2,16,4096]{2,1,0:T(8,128)(2,1)S(1)} %collective-permute-done.8.refs_0_), channel_id=1, source_target_pairs={{0,4},{4,0},{8,12},{12,8},{16,20},{20,16},{24,28},{28,24},{1,5},{5... | collective-permute-start | bytes 786440 | tf_op jit(solution)/shard_map/ppermute | solution.py:238
  29.1 3.1 %collective-permute-start.11 = (bf16[2,16,4096]{2,1,0:T(8,128)(2,1)S(1)}, bf16[2,16,4096]{2,1,0:T(8,128)(2,1)S(1)}, u32[]{:S(2)}, u32[]{:S(2)}) collective-permute-start(bf16[2,16,4096]{2,1,0:T(8,128)(2,1)S(1)} %collective-permute-done.9.refs_1_), channel_id=1, source_target_pairs={{0,4},{4,0},{8,12},{12,8},{16,20},{20,16},{24,28},{28,24},{1,5},{5... | collective-permute-start | bytes 786440 | tf_op jit(solution)/shard_map/ppermute | solution.py:238
  29.6 9.7 %collective-permute-start.6 = (bf16[128,512]{1,0:T(8,128)(2,1)S(1)}, bf16[128,512]{1,0:T(8,128)(2,1)S(1)}, u32[]{:S(2)}, u32[]{:S(2)}) collective-permute-start(bf16[128,512]{1,0:T(8,128)(2,1)S(1)} %fusion.2), channel_id=1, source_target_pairs={{0,2},{1,3},{2,0},{3,1},{4,6},{5,7},{6,4},{7,5},{8,10},{9,11},{10,... | collective-permute-start | bytes 393224 | tf_op jit(solution)/shard_map/ppermute | solution.py:241
  34.1 20.1 %copy-start = (bf16[64,64,512]{2,1,0:T(8,128)(2,1)S(1)}, bf16[64,64,512]{2,1,0:T(8,128)(2,1)}, u32[]{:S(2)}) copy-start(bf16[64,64,512]{2,1,0:T(8,128)(2,1)} %refs_1_.3) | copy-start | bytes 12582916
  34.1 7.1 %collective-permute-start.13 = (f32[96,128]{1,0:T(8,128)S(1)}, f32[96,128]{1,0:T(8,128)S(1)}, u32[]{:S(2)}, u32[]{:S(2)}) collective-permute-start(f32[96,128]{1,0:T(8,128)S(1)} %shard_map.70), channel_id=1, source_target_pairs={{0,1},{1,0},{2,3},{3,2},{4,5},{5,4},{6,7},{7,6},{8,9},{9,8},{10,11... | collective-permute-start | bytes 147464 | tf_op jit(solution)/shard_map/ppermute | solution.py:241
  36.0 13.1 %collective-permute-start.14 = (bf16[2,128,512]{2,1,0:T(8,128)(2,1)S(1)}, bf16[2,128,512]{2,1,0:T(8,128)(2,1)S(1)}, u32[]{:S(2)}, u32[]{:S(2)}) collective-permute-start(bf16[2,128,512]{2,1,0:T(8,128)(2,1)S(1)} %shard_map.71), channel_id=1, source_target_pairs={{0,1},{1,0},{2,3},{3,2},{4,5},{5,4},{6,7},{7,6},{8,9},{9,8},{10,11... | collective-permute-start | bytes 786440 | tf_op jit(solution)/shard_map/ppermute | solution.py:241
  41.2 7.9 %collective-permute-start.16 = (f32[96,128]{1,0:T(8,128)S(1)}, f32[96,128]{1,0:T(8,128)S(1)}, u32[]{:S(2)}, u32[]{:S(2)}) collective-permute-start(f32[96,128]{1,0:T(8,128)S(1)} %add.17), channel_id=1, source_target_pairs={{0,2},{1,3},{2,0},{3,1},{4,6},{5,7},{6,4},{7,5},{8,10},{9,11},{10,... | collective-permute-start | bytes 147464 | tf_op jit(solution)/shard_map/ppermute | solution.py:241
  43.9 16.0 %collective-permute-start.12 = (bf16[256,512]{1,0:T(8,128)(2,1)S(1)}, bf16[256,512]{1,0:T(8,128)(2,1)S(1)}, u32[]{:S(2)}, u32[]{:S(2)}) collective-permute-start(bf16[256,512]{1,0:T(8,128)(2,1)S(1)} %fusion), channel_id=1, source_target_pairs={{0,2},{1,3},{2,0},{3,1},{4,6},{5,7},{6,4},{7,5},{8,10},{9,11},{10,... | collective-permute-start | bytes 786440 | tf_op jit(solution)/shard_map/ppermute | solution.py:241
  49.2 1.5 %collective-permute-start.17 = (bf16[1,96,128]{2,1,0:T(8,128)(2,1)S(1)}, bf16[1,96,128]{2,1,0:T(8,128)(2,1)S(1)}, u32[]{:S(2)}, u32[]{:S(2)}) collective-permute-start(bf16[1,96,128]{2,1,0:T(8,128)(2,1)S(1)} %fusion.3), channel_id=1, source_target_pairs={{0,4},{4,0},{8,12},{12,8},{16,20},{20,16},{24,28},{28,24},{1,5},{5... | collective-permute-start | bytes 73736 | tf_op jit(solution)/shard_map/ppermute | solution.py:238
  49.2 14.9 %collective-permute-start.15 = (bf16[128,512]{1,0:T(8,128)(2,1)S(1)}, bf16[128,512]{1,0:T(8,128)(2,1)S(1)}, u32[]{:S(2)}, u32[]{:S(2)}) collective-permute-start(bf16[128,512]{1,0:T(8,128)(2,1)S(1)} %fusion.1), channel_id=1, source_target_pairs={{0,2},{1,3},{2,0},{3,1},{4,6},{5,7},{6,4},{7,5},{8,10},{9,11},{10,... | collective-permute-start | bytes 393224 | tf_op jit(solution)/shard_map/ppermute | solution.py:241
  50.6 4.9 %collective-permute-start.19 = (bf16[2,96,128]{2,1,0:T(8,128)(2,1)S(1)}, bf16[2,96,128]{2,1,0:T(8,128)(2,1)S(1)}, u32[]{:S(2)}, u32[]{:S(2)}) collective-permute-start(bf16[2,96,128]{2,1,0:T(8,128)(2,1)S(1)} %pad_maximum_fusion.refs_0_), channel_id=1, source_target_pairs={{0,8},{4,12},{8,0},{12,4},{16,24},{20,28},{24,16},{28,20},{1,9},{5... | collective-permute-start | bytes 147464 | tf_op jit(solution)/shard_map/ppermute | solution.py:238
  52.0 4.6 %collective-permute-start.20 = (bf16[2,96,128]{2,1,0:T(8,128)(2,1)S(1)}, bf16[2,96,128]{2,1,0:T(8,128)(2,1)S(1)}, u32[]{:S(2)}, u32[]{:S(2)}) collective-permute-start(bf16[2,96,128]{2,1,0:T(8,128)(2,1)S(1)} %pad_maximum_fusion.refs_0_), channel_id=1, source_target_pairs={{0,16},{4,20},{8,24},{12,28},{16,0},{20,4},{24,8},{28,12},{1,17},{... | collective-permute-start | bytes 147464 | tf_op jit(solution)/shard_map/ppermute | solution.py:238
  52.8 5.6 %collective-permute-start.18 = (bf16[2,96,128]{2,1,0:T(8,128)(2,1)S(1)}, bf16[2,96,128]{2,1,0:T(8,128)(2,1)S(1)}, u32[]{:S(2)}, u32[]{:S(2)}) collective-permute-start(bf16[2,96,128]{2,1,0:T(8,128)(2,1)S(1)} %pad_maximum_fusion.refs_0_), channel_id=1, source_target_pairs={{0,24},{4,28},{8,16},{12,20},{16,8},{20,12},{24,0},{28,4},{1,25},{... | collective-permute-start | bytes 147464 | tf_op jit(solution)/shard_map/ppermute | solution.py:238

commit v5 on v4

--- a/solution.py
+++ b/solution.py
@@ -126,22 +126,26 @@
     inner_dots(rows, weight, far, own)
 
 
-def rank_kernel(order, before, n, *refs):
+def rank_kernel(blocks, before, n, *refs):
     parts, rest, rows = refs[:n], refs[n:-1], refs[-1]
     down, where, out = rest[0], rest[1], rest[-1]
     me = lax.axis_index("replica")
     adapters, rank, feats = down.shape
     stack_rows(parts, rows)
     total = rows.shape[0]
-    block = total // len(order)
-    starts = [pl.multiple_of((me ^ k) * block, block) for k in order]
+    whole = where.shape[0] // lax.axis_size("replica")
+    here = []
+    for (bits, first), part in zip(blocks, parts):
+        steps, requests, _ = part.shape
+        at = pl.multiple_of((me ^ bits) * whole + first * requests, requests)
+        here.append(where[pl.ds(at, steps * requests), :])
+    here = jnp.concatenate(here, axis=0)
     reduced = lax.dot_general(
         rows[...],
         down[...].reshape(adapters * rank, feats),
         (((1,), (1,)), ((), ())),
         preferred_element_type=jnp.float32,
     )
-    here = jnp.concatenate([where[pl.ds(at, block), :] for at in starts], axis=0)
     local = here[:, 0:1] - me * adapters
     adapter_of = lax.broadcasted_iota(jnp.int32, (total, adapters * rank), 1) // rank
     picked = jnp.where(adapter_of == local, reduced, 0.0)
@@ -195,23 +199,24 @@
 
 def finish_kernel(pieces, *refs):
     out, delta = refs[-1], refs[-2]
-    steps, _, cols = out.shape
+    steps, requests, cols = out.shape
+    replicas = lax.axis_size("replica")
+    own_requests = requests // replicas
     me = lax.axis_index("replica")
-    at = 0
-    for order in pieces:
-        own, near, far = refs[at : at + 3]
-        at += 3
-        rows = own.shape[0] // len(order)
-        requests = rows // steps
-        for i, k in enumerate(order):
-            here = pl.ds(i * rows, rows)
-            who = me ^ k
+    for i, blocks in enumerate(pieces):
+        own, near, far = refs[3 * i : 3 * i + 3]
+        at = 0
+        for bits, first, count in blocks:
+            rows = count * own_requests
+            here = pl.ds(at, rows)
+            at += rows
+            who = me ^ bits
             total = own[here, :] + near[0, here, :].astype(jnp.float32)
             total += far[here, :].astype(jnp.float32)
-            total += delta[pl.ds(pl.multiple_of(who * rows, rows), rows), :]
-            out[:, pl.ds(pl.multiple_of(who * requests, requests), requests), :] = total.astype(
-                out.dtype
-            ).reshape(steps, requests, cols)
+            start = pl.multiple_of((who * steps + first) * own_requests, own_requests)
+            total += delta[pl.ds(start, rows), :]
+            place = pl.ds(pl.multiple_of(who * own_requests, own_requests), own_requests)
+            out[pl.ds(first, count), place, :] = total.astype(out.dtype).reshape(count, own_requests, cols)
 
 
 def flip(size, bits):
@@ -255,10 +260,14 @@
     def cost(n, width):
         return pl.CostEstimate(flops=2 * n * feats * width, bytes_accessed=2 * n * feats, transcendentals=0)
 
+    def held_back(piece):
+        return [tie(piece[0][0]), *(part for part, _, _ in piece[1:])]
+
     held = pltpu.VMEM((2, feats, cols), jnp.bfloat16)
     copies = pltpu.SemaphoreType.DMA((2,))
 
-    def outer(parts, weight):
+    def outer(piece, weight):
+        parts = held_back(piece)
         n = sum(p.shape[0] * p.shape[1] for p in parts)
         return pl.pallas_call(
             functools.partial(outer_kernel, len(parts)),
@@ -270,7 +279,8 @@
             cost_estimate=cost(n, 2 * cols),
         )(*parts, weight)
 
-    def inside(parts, weight, first=False):
+    def inside(piece, weight, first=False):
+        parts = held_back(piece)
         n = sum(p.shape[0] * p.shape[1] for p in parts)
         return pl.pallas_call(
             functools.partial(first_inner_kernel if first else inner_kernel, len(parts)),
@@ -284,16 +294,18 @@
 
     down = jnp.transpose(adapter_down_weight, (0, 2, 1))
 
-    def ranked(order, parts, *before):
-        n = rows * len(order)
+    def ranked(piece, *before):
+        parts = held_back(piece)
+        n = sum(p.shape[0] * p.shape[1] for p in parts)
+        blocks = [(bits, first) for _, bits, first in piece]
         return pl.pallas_call(
-            functools.partial(rank_kernel, order, len(before) > 0, len(parts)),
+            functools.partial(rank_kernel, blocks, len(before) > 0, len(parts)),
             out_shape=jax.ShapeDtypeStruct((half * OWN_CAP, 2 * rank), jnp.float32),
             in_specs=[VMEM] * (len(parts) + 2 + len(before)),
             out_specs=VMEM,
             scratch_shapes=[pltpu.VMEM((n, feats), jnp.bfloat16)],
             compiler_params=params(10),
-            cost_estimate=cost(n, adapters_here * rank),
+            cost_estimate=pl.CostEstimate(flops=0, bytes_accessed=0, transcendentals=0),
         )(*parts, down, where, *before)
 
     def pass_on(far, near_in):
@@ -315,48 +327,64 @@
         ],
         compiler_params=params(4),
     )(weight, *(pltpu.with_memory_space_constraint(v, pltpu.HBM) for v in (request_adapter, adapter_storage_row)))
-    near0 = outer([x0, x1], held_out)
+    p0 = [(x0, 0, 0), (x1, 1, 0)]
+    near0 = outer(p0, held_out)
     done(near0)
     near0_in = along(near0, 1)
-    far0, own0, held_in = inside([tie(x0), x1], weight, True)
+    far0, own0, held_in = inside(p0, weight, True)
     done(own0)
+    wait(near0_in)
+    far0_out = pass_on(far0, tie(near0_in))
+    far0_in = along(far0_out, 2)
+    wait(far0_out)
 
     wait(x2, x4, near0_in)
     x2, x4 = tie(x2, x4)
     x3, x5 = swap(x2, 1), swap(x4, 1)
     x6a, x6b = swap(x2[:half], 4), swap(x4[half:], 2)
-    near1 = outer([x2, x3, x4, x5], held_out)
+    p1 = [(x2, 2, 0), (x3, 3, 0)]
+    near1 = outer(p1, held_out)
     done(near1)
     near1_in = along(near1, 1)
-    far0_out = pass_on(far0, tie(near0_in))
-    far0_in = along(far0_out, 2)
-    wait(far0_out)
-    far1, own1 = inside([tie(x2), x3, x4, x5], held_in)
+    wait(x5)
+    p2 = [(x4, 4, 0), (x5, 5, 0)]
+    near2 = outer(p2, held_out)
+    done(near2)
+    near2_in = along(near2, 1)
+    far1, own1 = inside(p1, held_in)
     done(own1)
-    packed = ranked((0, 1, 2, 3, 4, 5), [tie(x0), x1, x2, x3, x4, x5])
-    done(packed)
+    far2, own2 = inside(p2, held_in)
+    done(own2)
 
     wait(x6a, x6b)
     x6a, x6b = tie(x6a, x6b)
     x7a, x7b = swap(x6a, 1), swap(x6b, 1)
-    packed = ranked((6, 7), [x6a, x6b, x7a, x7b], packed)
+    wait(near1_in, far0_in)
+    far1_out = pass_on(far1, tie(near1_in))
+    far1_in = along(far1_out, 2)
+    wait(far1_out, x7a, x7b)
+    p3 = [(x6a, 6, 0), (x6b, 6, half), (x7a, 7, 0), (x7b, 7, half)]
+    packed = ranked(p0 + p1 + p2 + p3)
     done(packed)
     packed_in = along(packed, 1)
-    near2 = outer([tie(x6a), x6b, x7a, x7b], held_out)
-    done(near2)
-    near2_in = along(near2, 1)
-    wait(far0_in)
-    far1_out = pass_on(far1, tie(near1_in))
-    wait(far1_out, packed_in)
+    near3 = outer(p3, held_out)
+    done(near3)
+    near3_in = along(near3, 1)
+    wait(near2_in, far1_in)
+    far2_out = pass_on(far2, tie(near2_in))
+    wait(far2_out, packed_in)
     packed = packed + tie(packed_in)
     done(packed)
     packed_in = along(packed, 2)
-    far1_in = along(far1_out, 2)
-    far2, own2 = inside([tie(x6a), x6b, x7a, x7b], held_in)
-    done(own2)
-    far2_out = pass_on(far2, tie(near2_in))
     far2_in = along(far2_out, 2)
-    wait(far2_out)
+    far3, own3 = inside(p3, held_in)
+    done(own3)
+    wait(near3_in)
+    far3_out = pass_on(far3, tie(near3_in))
+    far3_in = along(far3_out, 2)
+    wait(far3_out)
+    all_pieces = [p0, p1, p2, p3]
+    arrived = [(own0, near0_in, far0_in), (own1, near1_in, far1_in), (own2, near2_in, far2_in), (own3, near3_in, far3_in)]
 
     def up(first, ranks, *before):
         return pl.pallas_call(
@@ -372,7 +400,7 @@
     ranks = (packed + tie(packed_in)).astype(jnp.bfloat16)[None]
     done(ranks)
     got = swap(ranks, 1)
-    wait(got)
+    wait(got, far2_in)
     ranks = jnp.concatenate([ranks, tie(got)], axis=0)
     done(ranks)
     got2, got4, got6 = (swap(ranks, bits) for bits in (2, 4, 6))
@@ -381,15 +409,14 @@
     wait(got2, got4)
     delta = up(2, [tie(got2), got4], delta)
     done(delta)
-    wait(got6, far1_in)
+    wait(got6)
     delta = up(6, [tie(got6)], delta)
 
-    pieces = [(0, 1), (2, 3, 4, 5), (6, 7)]
-    arrived = [(own0, near0_in, far0_in), (own1, near1_in, far1_in), (own2, near2_in, far2_in)]
+    pieces = [[(bits, first, part.shape[0]) for part, bits, first in piece] for piece in all_pieces]
     return pl.pallas_call(
         functools.partial(finish_kernel, pieces),
         out_shape=jax.ShapeDtypeStruct((steps, requests, cols), jnp.bfloat16),
-        in_specs=[VMEM] * 10,
+        in_specs=[VMEM] * (3 * len(pieces) + 1),
         out_specs=VMEM,
         compiler_params=params(12),
     )(*[ref for piece in arrived for ref in piece], delta)

time: 66.4 us -> 62.9 us (0.947); the launches traced: 65.1 us -> 62.8 us
  waiting for transfers between devices: 14.9 us -> 11.6 us
  starting transfers between devices: 23.3 us -> 24.9 us
  Pallas kernels: 26.4 us -> 25.7 us
    ppermute x13, waiting for transfers between devices: 2.83 us -> 1.05 us  [swap(): return lax.ppermute(value, 'replica', flip(replicas, bits))]
    ppermute x8 -> x10, starting transfers between devices: 12.3 us -> 14 us  [along(): return lax.ppermute(value, 'tensor', flip(tensors, bits))]
    ppermute x8 -> x10, waiting for transfers between devices: 12.1 us -> 10.6 us  [along(): return lax.ppermute(value, 'tensor', flip(tensors, bits))]
    pallas_call x2 -> x1, Pallas kernels: 4.4 us -> 3.42 us  [ranked(): pl.pallas_call(functools.partial(rank_kernel, blocks, len(before) > 0, le...]
    pallas_call x3 -> x4, Pallas kernels: 8.37 us -> 8.7 us  [inside(): pl.pallas_call(functools.partial(first_inner_kernel if first else inner_k...]
    pallas_call x3 -> x4, Pallas kernels: 4.83 us -> 4.98 us  [outer(): pl.pallas_call(functools.partial(outer_kernel, len(parts)), out_shape=jax...]
  transfers between devices with their start and end apart: 21 -> 23, of which waited for: 10 -> 6; matrix products, arithmetic and copies ran while one was open for 0% -> 0% of each run, Pallas kernels for 39% -> 39%
where the time goes in v5:
time: 62.9 us; the launch traced here: 62.8 us
  Pallas kernels  25.7 us (41%)
  starting transfers between devices  24.9 us (40%)
  waiting for transfers between devices  11.6 us (18%)
    ppermute x10, starting transfers between devices, along(): return lax.ppermute(value, 'tensor', flip(tensors, bits))  14 us
    ppermute x13, starting transfers between devices, swap(): return lax.ppermute(value, 'replica', flip(replicas, bits))  10.9 us
    ppermute x10, waiting for transfers between devices, along(): return lax.ppermute(value, 'tensor', flip(tensors, bits))  10.6 us
    pallas_call x4, Pallas kernels, inside(): pl.pallas_call(functools.partial(first_inner_kernel if first else inner_k...  8.7 us
    pallas_call x4, Pallas kernels, outer(): pl.pallas_call(functools.partial(outer_kernel, len(parts)), out_shape=jax...  4.98 us
    pallas_call x3, Pallas kernels, up(): pl.pallas_call(functools.partial(up_kernel, first, len(before)), out_shap...  4.06 us
    pallas_call x1, Pallas kernels, on_device_blocks(): pl.pallas_call(functools.partial(load_kernel, replicas, steps, adapters_h...  3.58 us
    pallas_call x1, Pallas kernels, ranked(): pl.pallas_call(functools.partial(rank_kernel, blocks, len(before) > 0, le...  3.42 us
  transfers between devices with their start and end apart: 23, of which 6 were waited for; matrix products, arithmetic and copies ran while one was open for 0% of the time, Pallas kernels for 39%

profile of v5, /device:TPU:0, one launch (start us, length us, event | category | flops | bytes accessed | tf_op | source)
XLA Modules:
  0.0 62.8 jit_solution(11006694361407724467)
XLA Ops:
  0.5 2.5 %collective-permute-start.3 = (bf16[4,16,4096]{2,1,0:T(8,128)(2,1)}, bf16[4,16,4096]{2,1,0:T(8,128)(2,1)S(1)}, u32[]{:S(2)}, u32[]{:S(2)}) collective-permute-start(bf16[4,16,4096]{2,1,0:T(8,128)(2,1)} %refs_0_.2), channel_id=1, source_target_pairs={{0,8},{4,12},{8,0},{12,4},{16,24},{20,28},{24,16},{28,20},{1,9},{5... | collective-permute-start | bytes 1572872 | tf_op jit(solution)/shard_map/ppermute | solution.py:243
  3.0 1.5 %collective-permute-start.4 = (bf16[4,16,4096]{2,1,0:T(8,128)(2,1)}, bf16[4,16,4096]{2,1,0:T(8,128)(2,1)S(1)}, u32[]{:S(2)}, u32[]{:S(2)}) collective-permute-start(bf16[4,16,4096]{2,1,0:T(8,128)(2,1)} %refs_0_.2), channel_id=1, source_target_pairs={{0,16},{4,20},{8,24},{12,28},{16,0},{20,4},{24,8},{28,12},{1,17},{... | collective-permute-start | bytes 1572872 | tf_op jit(solution)/shard_map/ppermute | solution.py:243
  4.5 3.6 %shard_map.64 = (bf16[2,4096,512]{2,1,0:T(8,128)(2,1)S(1)}, s32[512,8]{1,0:T(8,128)S(1)}) custom-call(bf16[4096,2048]{1,0:T(8,128)(2,1)} %refs_2_.2, s32[128]{0:T(128)} %request_in.1, s32[64]{0:T(128)} %storage_in.1), custom_call_target="tpu_custom_call" | custom-call | tf_op jit(solution)/shard_map/pallas_call | solution.py:317
  8.1 1.2 %shard_map.65 = bf16[2,128,512]{2,1,0:T(8,128)(2,1)S(1)} custom-call(bf16[4,16,4096]{2,1,0:T(8,128)(2,1)S(1)} %copy-done.1, bf16[4,16,4096]{2,1,0:T(8,128)(2,1)S(1)} %collective-permute-done.refs_1_, bf16[2,4096,512]{2,1,0:T(8,128)(2,1)S(1)} %get-tuple-element.38.refs_2_.refs_4_), custom_call_target="tpu_custom_call" | custom-call | flops 1073741824 | bytes 1048576 | tf_op jit(solution)/shard_map/pallas_call | solution.py:272
  9.4 1.6 %collective-permute-start.1 = (bf16[2,128,512]{2,1,0:T(8,128)(2,1)S(1)}, bf16[2,128,512]{2,1,0:T(8,128)(2,1)S(1)}, u32[]{:S(2)}, u32[]{:S(2)}) collective-permute-start(bf16[2,128,512]{2,1,0:T(8,128)(2,1)S(1)} %shard_map.65), channel_id=1, source_target_pairs={{0,1},{1,0},{2,3},{3,2},{4,5},{5,4},{6,7},{7,6},{8,9},{9,8},{10,11... | collective-permute-start | bytes 786440 | tf_op jit(solution)/shard_map/ppermute | solution.py:246
  11.0 4.8 %shard_map.66 = (f32[128,512]{1,0:T(8,128)S(1)}, f32[128,512]{1,0:T(8,128)S(1)}, bf16[2,4096,512]{2,1,0:T(8,128)(2,1)S(1)}) custom-call(bf16[4,16,4096]{2,1,0:T(8,128)(2,1)S(1)} %copy-done.1, bf16[4,16,4096]{2,1,0:T(8,128)(2,1)S(1)} %collective-permute-done.refs_1_, bf16[4096,2048]{1,0:T(8,128)(2,1)} %refs_2_.2), custom_call_target="tpu_custom_call" | custom-call | flops 1073741824 | bytes 1048576 | tf_op jit(solution)/shard_map/pallas_call | solution.py:285
  15.8 1.8 %collective-permute-done.1.refs_1_ = bf16[2,128,512]{2,1,0:T(8,128)(2,1)S(1)} collective-permute-done((bf16[2,128,512]{2,1,0:T(8,128)(2,1)S(1)}, bf16[2,128,512]{2,1,0:T(8,128)(2,1)S(1)}, u32[]{:S(2)}, u32[]{:S(2)}) %collective-permute-start.1) | collective-permute-done | bytes 262176 | tf_op jit(solution)/shard_map/ppermute | solution.py:246
  18.2 2.6 %collective-permute-start.2 = (bf16[128,512]{1,0:T(8,128)(2,1)S(1)}, bf16[128,512]{1,0:T(8,128)(2,1)S(1)}, u32[]{:S(2)}, u32[]{:S(2)}) collective-permute-start(bf16[128,512]{1,0:T(8,128)(2,1)S(1)} %fusion.3), channel_id=1, source_target_pairs={{0,2},{1,3},{2,0},{3,1},{4,6},{5,7},{6,4},{7,5},{8,10},{9,11},{10,... | collective-permute-start | bytes 393224 | tf_op jit(solution)/shard_map/ppermute | solution.py:246
  22.5 1.2 %shard_map.67 = bf16[2,128,512]{2,1,0:T(8,128)(2,1)S(1)} custom-call(bf16[4,16,4096]{2,1,0:T(8,128)(2,1)S(1)} %collective-permute-done.3.refs_0_.refs_2_, bf16[4,16,4096]{2,1,0:T(8,128)(2,1)S(1)} %collective-permute-done.5.refs_1_.refs_3_, bf16[2,4096,512]{2,1,0:T(8,128)(2,1)S(1)} %get-tuple-element.38.refs_2_.refs_4_), custom_call_target="tpu_custom_call" | custom-call | flops 1073741824 | bytes 1048576 | tf_op jit(solution)/shard_map/pallas_call | solution.py:272
  23.7 1.6 %collective-permute-start.7 = (bf16[2,128,512]{2,1,0:T(8,128)(2,1)S(1)}, bf16[2,128,512]{2,1,0:T(8,128)(2,1)S(1)}, u32[]{:S(2)}, u32[]{:S(2)}) collective-permute-start(bf16[2,128,512]{2,1,0:T(8,128)(2,1)S(1)} %shard_map.67), channel_id=1, source_target_pairs={{0,1},{1,0},{2,3},{3,2},{4,5},{5,4},{6,7},{7,6},{8,9},{9,8},{10,11... | collective-permute-start | bytes 786440 | tf_op jit(solution)/shard_map/ppermute | solution.py:246
  25.4 1.2 %shard_map.68 = bf16[2,128,512]{2,1,0:T(8,128)(2,1)S(1)} custom-call(bf16[4,16,4096]{2,1,0:T(8,128)(2,1)S(1)} %collective-permute-done.4.refs_0_.refs_4_, bf16[4,16,4096]{2,1,0:T(8,128)(2,1)S(1)} %collective-permute-done.6.refs_1_.refs_5_, bf16[2,4096,512]{2,1,0:T(8,128)(2,1)S(1)} %get-tuple-element.38.refs_2_.refs_4_), custom_call_target="tpu_custom_call" | custom-call | flops 1073741824 | bytes 1048576 | tf_op jit(solution)/shard_map/pallas_call | solution.py:272
  27.2 1.2 %shard_map.69 = (f32[128,512]{1,0:T(8,128)S(1)}, f32[128,512]{1,0:T(8,128)S(1)}) custom-call(bf16[4,16,4096]{2,1,0:T(8,128)(2,1)S(1)} %collective-permute-done.3.refs_0_.refs_2_, bf16[4,16,4096]{2,1,0:T(8,128)(2,1)S(1)} %collective-permute-done.5.refs_1_.refs_3_, bf16[2,4096,512]{2,1,0:T(8,128)(2,1)S(1)} %get-tuple-element.48.refs_2_.refs_4_), custom_call_target="tpu_custom_call" | custom-call | flops 1073741824 | bytes 1048576 | tf_op jit(solution)/shard_map/pallas_call | solution.py:285
  28.4 1.2 %shard_map.70 = (f32[128,512]{1,0:T(8,128)S(1)}, f32[128,512]{1,0:T(8,128)S(1)}) custom-call(bf16[4,16,4096]{2,1,0:T(8,128)(2,1)S(1)} %collective-permute-done.4.refs_0_.refs_4_, bf16[4,16,4096]{2,1,0:T(8,128)(2,1)S(1)} %collective-permute-done.6.refs_1_.refs_5_, bf16[2,4096,512]{2,1,0:T(8,128)(2,1)S(1)} %get-tuple-element.48.refs_2_.refs_4_), custom_call_target="tpu_custom_call" | custom-call | flops 1073741824 | bytes 1048576 | tf_op jit(solution)/shard_map/pallas_call | solution.py:285
  30.3 2.8 %collective-permute-done.7.refs_4_ = bf16[2,128,512]{2,1,0:T(8,128)(2,1)S(1)} collective-permute-done((bf16[2,128,512]{2,1,0:T(8,128)(2,1)S(1)}, bf16[2,128,512]{2,1,0:T(8,128)(2,1)S(1)}, u32[]{:S(2)}, u32[]{:S(2)}) %collective-permute-start.7) | collective-permute-done | bytes 262176 | tf_op jit(solution)/shard_map/ppermute | solution.py:246
  33.1 1.7 %collective-permute-start.10 = (bf16[128,512]{1,0:T(8,128)(2,1)S(1)}, bf16[128,512]{1,0:T(8,128)(2,1)S(1)}, u32[]{:S(2)}, u32[]{:S(2)}) collective-permute-start(bf16[128,512]{1,0:T(8,128)(2,1)S(1)} %fusion.2), channel_id=1, source_target_pairs={{0,2},{1,3},{2,0},{3,1},{4,6},{5,7},{6,4},{7,5},{8,10},{9,11},{10,... | collective-permute-start | bytes 393224 | tf_op jit(solution)/shard_map/ppermute | solution.py:246
  34.8 3.4 %shard_map.71 = f32[96,128]{1,0:T(8,128)S(1)} custom-call(bf16[4,16,4096]{2,1,0:T(8,128)(2,1)S(1)} %copy-done.1, bf16[4,16,4096]{2,1,0:T(8,128)(2,1)S(1)} %collective-permute-done.refs_1_, bf16[4,16,4096]{2,1,0:T(8,128)(2,1)S(1)} %collective-permute-done.3.refs_0_.refs_2_, bf16[4,16,4096]{2,1,0:T(8,128)(2,1)S(1)} %collective-permute-done.5.refs_1_.refs_3_, ...), custom_call_target="tpu_custom_call" | custom-call | tf_op jit(solution)/shard_map/pallas_call | solution.py:301
  38.3 2.5 %collective-permute-start.15 = (f32[96,128]{1,0:T(8,128)S(1)}, f32[96,128]{1,0:T(8,128)S(1)}, u32[]{:S(2)}, u32[]{:S(2)}) collective-permute-start(f32[96,128]{1,0:T(8,128)S(1)} %shard_map.71), channel_id=1, source_target_pairs={{0,1},{1,0},{2,3},{3,2},{4,5},{5,4},{6,7},{7,6},{8,9},{9,8},{10,11... | collective-permute-start | bytes 147464 | tf_op jit(solution)/shard_map/ppermute | solution.py:246
  40.8 1.2 %shard_map.72 = bf16[2,128,512]{2,1,0:T(8,128)(2,1)S(1)} custom-call(bf16[2,16,4096]{2,1,0:T(8,128)(2,1)S(1)} %collective-permute-done.8.refs_6_.refs_0_, bf16[2,16,4096]{2,1,0:T(8,128)(2,1)S(1)} %collective-permute-done.9.refs_7_.refs_1_, bf16[2,16,4096]{2,1,0:T(8,128)(2,1)S(1)} %collective-permute-done.12.refs_8_.refs_2_, ...), custom_call_target="tpu_custom_call" | custom-call | flops 1073741824 | bytes 1048576 | tf_op jit(solution)/shard_map/pallas_call | solution.py:272
  42.2 1.2 %collective-permute-done.15 = f32[96,128]{1,0:T(8,128)S(1)} collective-permute-done((f32[96,128]{1,0:T(8,128)S(1)}, f32[96,128]{1,0:T(8,128)S(1)}, u32[]{:S(2)}, u32[]{:S(2)}) %collective-permute-start.15) | collective-permute-done | bytes 49184 | tf_op jit(solution)/shard_map/ppermute | solution.py:246
  44.3 2.1 %collective-permute-start.14 = (bf16[128,512]{1,0:T(8,128)(2,1)S(1)}, bf16[128,512]{1,0:T(8,128)(2,1)S(1)}, u32[]{:S(2)}, u32[]{:S(2)}) collective-permute-start(bf16[128,512]{1,0:T(8,128)(2,1)S(1)} %fusion.1), channel_id=1, source_target_pairs={{0,2},{1,3},{2,0},{3,1},{4,6},{5,7},{6,4},{7,5},{8,10},{9,11},{10,... | collective-permute-start | bytes 393224 | tf_op jit(solution)/shard_map/ppermute | solution.py:246
  46.4 1.4 %shard_map.73 = (f32[128,512]{1,0:T(8,128)S(1)}, f32[128,512]{1,0:T(8,128)S(1)}) custom-call(bf16[2,16,4096]{2,1,0:T(8,128)(2,1)S(1)} %collective-permute-done.8.refs_6_.refs_0_, bf16[2,16,4096]{2,1,0:T(8,128)(2,1)S(1)} %collective-permute-done.9.refs_7_.refs_1_, bf16[2,16,4096]{2,1,0:T(8,128)(2,1)S(1)} %collective-permute-done.12.refs_8_.refs_2_, ...), custom_call_target="tpu_custom_call" | custom-call | flops 1073741824 | bytes 1048576 | tf_op jit(solution)/shard_map/pallas_call | solution.py:285
  47.8 3.8 %collective-permute-done.16.refs_10_ = bf16[2,128,512]{2,1,0:T(8,128)(2,1)S(1)} collective-permute-done((bf16[2,128,512]{2,1,0:T(8,128)(2,1)S(1)}, bf16[2,128,512]{2,1,0:T(8,128)(2,1)S(1)}, u32[]{:S(2)}, u32[]{:S(2)}) %collective-permute-start.16) | collective-permute-done | bytes 262176 | tf_op jit(solution)/shard_map/ppermute | solution.py:246
  55.4 1.2 %collective-permute-start.20 = (bf16[2,96,128]{2,1,0:T(8,128)(2,1)S(1)}, bf16[2,96,128]{2,1,0:T(8,128)(2,1)S(1)}, u32[]{:S(2)}, u32[]{:S(2)}) collective-permute-start(bf16[2,96,128]{2,1,0:T(8,128)(2,1)S(1)} %pad_maximum_fusion.refs_0_), channel_id=1, source_target_pairs={{0,24},{4,28},{8,16},{12,20},{16,8},{20,12},{24,0},{28,4},{1,25},{... | collective-permute-start | bytes 147464 | tf_op jit(solution)/shard_map/ppermute | solution.py:243
  58.8 1.7 %shard_map.75.refs_3_ = f32[512,512]{1,0:T(8,128)S(1)} custom-call(bf16[2,96,128]{2,1,0:T(8,128)(2,1)S(1)} %collective-permute-done.21.refs_0_, bf16[2,96,128]{2,1,0:T(8,128)(2,1)S(1)} %collective-permute-done.22.refs_1_, bf16[64,64,512]{2,1,0:T(8,128)(2,1)S(1)} %copy-done, s32[512,8]{1,0:T(8,128)S(1)} %get-tuple-element.58.refs_11_.refs_2_.refs_3_, ...), custom_call_target="tpu_custom_call" | custom-call | tf_op jit(solution)/shard_map/pallas_call | solution.py:390
  (51 shorter events, 13.0 us)
Async XLA Ops:
  0.0 8.1 %collective-permute-start = (bf16[4,16,4096]{2,1,0:T(8,128)(2,1)}, bf16[4,16,4096]{2,1,0:T(8,128)(2,1)S(1)}, u32[]{:S(2)}, u32[]{:S(2)}) collective-permute-start(bf16[4,16,4096]{2,1,0:T(8,128)(2,1)} %refs_0_.2), channel_id=1, source_target_pairs={{0,4},{4,0},{8,12},{12,8},{16,20},{20,16},{24,28},{28,24},{1,5},{5... | collective-permute-start | bytes 1572872 | tf_op jit(solution)/shard_map/ppermute | solution.py:243
  0.5 17.1 %collective-permute-start.3 = (bf16[4,16,4096]{2,1,0:T(8,128)(2,1)}, bf16[4,16,4096]{2,1,0:T(8,128)(2,1)S(1)}, u32[]{:S(2)}, u32[]{:S(2)}) collective-permute-start(bf16[4,16,4096]{2,1,0:T(8,128)(2,1)} %refs_0_.2), channel_id=1, source_target_pairs={{0,8},{4,12},{8,0},{12,4},{16,24},{20,28},{24,16},{28,20},{1,9},{5... | collective-permute-start | bytes 1572872 | tf_op jit(solution)/shard_map/ppermute | solution.py:243
  3.0 14.6 %collective-permute-start.4 = (bf16[4,16,4096]{2,1,0:T(8,128)(2,1)}, bf16[4,16,4096]{2,1,0:T(8,128)(2,1)S(1)}, u32[]{:S(2)}, u32[]{:S(2)}) collective-permute-start(bf16[4,16,4096]{2,1,0:T(8,128)(2,1)} %refs_0_.2), channel_id=1, source_target_pairs={{0,16},{4,20},{8,24},{12,28},{16,0},{20,4},{24,8},{28,12},{1,17},{... | collective-permute-start | bytes 1572872 | tf_op jit(solution)/shard_map/ppermute | solution.py:243
  9.4 8.2 %collective-permute-start.1 = (bf16[2,128,512]{2,1,0:T(8,128)(2,1)S(1)}, bf16[2,128,512]{2,1,0:T(8,128)(2,1)S(1)}, u32[]{:S(2)}, u32[]{:S(2)}) collective-permute-start(bf16[2,128,512]{2,1,0:T(8,128)(2,1)S(1)} %shard_map.65), channel_id=1, source_target_pairs={{0,1},{1,0},{2,3},{3,2},{4,5},{5,4},{6,7},{7,6},{8,9},{9,8},{10,11... | collective-permute-start | bytes 786440 | tf_op jit(solution)/shard_map/ppermute | solution.py:246
  17.6 4.9 %collective-permute-start.5 = (bf16[4,16,4096]{2,1,0:T(8,128)(2,1)S(1)}, bf16[4,16,4096]{2,1,0:T(8,128)(2,1)S(1)}, u32[]{:S(2)}, u32[]{:S(2)}) collective-permute-start(bf16[4,16,4096]{2,1,0:T(8,128)(2,1)S(1)} %collective-permute-done.3.refs_0_.refs_2_), channel_id=1, source_target_pairs={{0,4},{4,0},{8,12},{12,8},{16,20},{20,16},{24,28},{28,24},{1,5},{5... | collective-permute-start | bytes 1572872 | tf_op jit(solution)/shard_map/ppermute | solution.py:243
  17.7 7.7 %collective-permute-start.6 = (bf16[4,16,4096]{2,1,0:T(8,128)(2,1)S(1)}, bf16[4,16,4096]{2,1,0:T(8,128)(2,1)S(1)}, u32[]{:S(2)}, u32[]{:S(2)}) collective-permute-start(bf16[4,16,4096]{2,1,0:T(8,128)(2,1)S(1)} %collective-permute-done.4.refs_0_.refs_4_), channel_id=1, source_target_pairs={{0,4},{4,0},{8,12},{12,8},{16,20},{20,16},{24,28},{28,24},{1,5},{5... | collective-permute-start | bytes 1572872 | tf_op jit(solution)/shard_map/ppermute | solution.py:243
  18.2 12.1 %collective-permute-start.2 = (bf16[128,512]{1,0:T(8,128)(2,1)S(1)}, bf16[128,512]{1,0:T(8,128)(2,1)S(1)}, u32[]{:S(2)}, u32[]{:S(2)}) collective-permute-start(bf16[128,512]{1,0:T(8,128)(2,1)S(1)} %fusion.3), channel_id=1, source_target_pairs={{0,2},{1,3},{2,0},{3,1},{4,6},{5,7},{6,4},{7,5},{8,10},{9,11},{10,... | collective-permute-start | bytes 393224 | tf_op jit(solution)/shard_map/ppermute | solution.py:246
  20.8 8.8 %collective-permute-start.9 = (bf16[2,16,4096]{2,1,0:T(8,128)(2,1)S(1)}, bf16[2,16,4096]{2,1,0:T(8,128)(2,1)S(1)}, u32[]{:S(2)}, u32[]{:S(2)}) collective-permute-start(bf16[2,16,4096]{2,1,0:T(8,128)(2,1)S(1)} %slice.20), channel_id=1, source_target_pairs={{0,8},{4,12},{8,0},{12,4},{16,24},{20,28},{24,16},{28,20},{1,9},{5... | collective-permute-start | bytes 786440 | tf_op jit(solution)/shard_map/ppermute | solution.py:243
  21.4 8.3 %collective-permute-start.8 = (bf16[2,16,4096]{2,1,0:T(8,128)(2,1)S(1)}, bf16[2,16,4096]{2,1,0:T(8,128)(2,1)S(1)}, u32[]{:S(2)}, u32[]{:S(2)}) collective-permute-start(bf16[2,16,4096]{2,1,0:T(8,128)(2,1)S(1)} %slice.19), channel_id=1, source_target_pairs={{0,16},{4,20},{8,24},{12,28},{16,0},{20,4},{24,8},{28,12},{1,17},{... | collective-permute-start | bytes 786440 | tf_op jit(solution)/shard_map/ppermute | solution.py:243
  23.7 9.3 %collective-permute-start.7 = (bf16[2,128,512]{2,1,0:T(8,128)(2,1)S(1)}, bf16[2,128,512]{2,1,0:T(8,128)(2,1)S(1)}, u32[]{:S(2)}, u32[]{:S(2)}) collective-permute-start(bf16[2,128,512]{2,1,0:T(8,128)(2,1)S(1)} %shard_map.67), channel_id=1, source_target_pairs={{0,1},{1,0},{2,3},{3,2},{4,5},{5,4},{6,7},{7,6},{8,9},{9,8},{10,11... | collective-permute-start | bytes 786440 | tf_op jit(solution)/shard_map/ppermute | solution.py:246
  26.6 15.5 %collective-permute-start.11 = (bf16[2,128,512]{2,1,0:T(8,128)(2,1)S(1)}, bf16[2,128,512]{2,1,0:T(8,128)(2,1)S(1)}, u32[]{:S(2)}, u32[]{:S(2)}) collective-permute-start(bf16[2,128,512]{2,1,0:T(8,128)(2,1)S(1)} %shard_map.68), channel_id=1, source_target_pairs={{0,1},{1,0},{2,3},{3,2},{4,5},{5,4},{6,7},{7,6},{8,9},{9,8},{10,11... | collective-permute-start | bytes 786440 | tf_op jit(solution)/shard_map/ppermute | solution.py:246
  29.7 5.1 %collective-permute-start.12 = (bf16[2,16,4096]{2,1,0:T(8,128)(2,1)S(1)}, bf16[2,16,4096]{2,1,0:T(8,128)(2,1)S(1)}, u32[]{:S(2)}, u32[]{:S(2)}) collective-permute-start(bf16[2,16,4096]{2,1,0:T(8,128)(2,1)S(1)} %collective-permute-done.8.refs_6_.refs_0_), channel_id=1, source_target_pairs={{0,4},{4,0},{8,12},{12,8},{16,20},{20,16},{24,28},{28,24},{1,5},{5... | collective-permute-start | bytes 786440 | tf_op jit(solution)/shard_map/ppermute | solution.py:243
  29.8 5.1 %collective-permute-start.13 = (bf16[2,16,4096]{2,1,0:T(8,128)(2,1)S(1)}, bf16[2,16,4096]{2,1,0:T(8,128)(2,1)S(1)}, u32[]{:S(2)}, u32[]{:S(2)}) collective-permute-start(bf16[2,16,4096]{2,1,0:T(8,128)(2,1)S(1)} %collective-permute-done.9.refs_7_.refs_1_), channel_id=1, source_target_pairs={{0,4},{4,0},{8,12},{12,8},{16,20},{20,16},{24,28},{28,24},{1,5},{5... | collective-permute-start | bytes 786440 | tf_op jit(solution)/shard_map/ppermute | solution.py:243
  33.1 9.0 %collective-permute-start.10 = (bf16[128,512]{1,0:T(8,128)(2,1)S(1)}, bf16[128,512]{1,0:T(8,128)(2,1)S(1)}, u32[]{:S(2)}, u32[]{:S(2)}) collective-permute-start(bf16[128,512]{1,0:T(8,128)(2,1)S(1)} %fusion.2), channel_id=1, source_target_pairs={{0,2},{1,3},{2,0},{3,1},{4,6},{5,7},{6,4},{7,5},{8,10},{9,11},{10,... | collective-permute-start | bytes 393224 | tf_op jit(solution)/shard_map/ppermute | solution.py:246
  38.2 18.4 %copy-start = (bf16[64,64,512]{2,1,0:T(8,128)(2,1)S(1)}, bf16[64,64,512]{2,1,0:T(8,128)(2,1)}, u32[]{:S(2)}) copy-start(bf16[64,64,512]{2,1,0:T(8,128)(2,1)} %refs_1_.3) | copy-start | bytes 12582916
  38.3 5.1 %collective-permute-start.15 = (f32[96,128]{1,0:T(8,128)S(1)}, f32[96,128]{1,0:T(8,128)S(1)}, u32[]{:S(2)}, u32[]{:S(2)}) collective-permute-start(f32[96,128]{1,0:T(8,128)S(1)} %shard_map.71), channel_id=1, source_target_pairs={{0,1},{1,0},{2,3},{3,2},{4,5},{5,4},{6,7},{7,6},{8,9},{9,8},{10,11... | collective-permute-start | bytes 147464 | tf_op jit(solution)/shard_map/ppermute | solution.py:246
  42.0 9.5 %collective-permute-start.16 = (bf16[2,128,512]{2,1,0:T(8,128)(2,1)S(1)}, bf16[2,128,512]{2,1,0:T(8,128)(2,1)S(1)}, u32[]{:S(2)}, u32[]{:S(2)}) collective-permute-start(bf16[2,128,512]{2,1,0:T(8,128)(2,1)S(1)} %shard_map.72), channel_id=1, source_target_pairs={{0,1},{1,0},{2,3},{3,2},{4,5},{5,4},{6,7},{7,6},{8,9},{9,8},{10,11... | collective-permute-start | bytes 786440 | tf_op jit(solution)/shard_map/ppermute | solution.py:246
  43.4 8.2 %collective-permute-start.18 = (f32[96,128]{1,0:T(8,128)S(1)}, f32[96,128]{1,0:T(8,128)S(1)}, u32[]{:S(2)}, u32[]{:S(2)}) collective-permute-start(f32[96,128]{1,0:T(8,128)S(1)} %add.21), channel_id=1, source_target_pairs={{0,2},{1,3},{2,0},{3,1},{4,6},{5,7},{6,4},{7,5},{8,10},{9,11},{10,... | collective-permute-start | bytes 147464 | tf_op jit(solution)/shard_map/ppermute | solution.py:246
  44.3 8.8 %collective-permute-start.14 = (bf16[128,512]{1,0:T(8,128)(2,1)S(1)}, bf16[128,512]{1,0:T(8,128)(2,1)S(1)}, u32[]{:S(2)}, u32[]{:S(2)}) collective-permute-start(bf16[128,512]{1,0:T(8,128)(2,1)S(1)} %fusion.1), channel_id=1, source_target_pairs={{0,2},{1,3},{2,0},{3,1},{4,6},{5,7},{6,4},{7,5},{8,10},{9,11},{10,... | collective-permute-start | bytes 393224 | tf_op jit(solution)/shard_map/ppermute | solution.py:246
  51.6 1.4 %collective-permute-start.19 = (bf16[1,96,128]{2,1,0:T(8,128)(2,1)S(1)}, bf16[1,96,128]{2,1,0:T(8,128)(2,1)S(1)}, u32[]{:S(2)}, u32[]{:S(2)}) collective-permute-start(bf16[1,96,128]{2,1,0:T(8,128)(2,1)S(1)} %fusion.4), channel_id=1, source_target_pairs={{0,4},{4,0},{8,12},{12,8},{16,20},{20,16},{24,28},{28,24},{1,5},{5... | collective-permute-start | bytes 73736 | tf_op jit(solution)/shard_map/ppermute | solution.py:243
  51.7 10.0 %collective-permute-start.17 = (bf16[128,512]{1,0:T(8,128)(2,1)S(1)}, bf16[128,512]{1,0:T(8,128)(2,1)S(1)}, u32[]{:S(2)}, u32[]{:S(2)}) collective-permute-start(bf16[128,512]{1,0:T(8,128)(2,1)S(1)} %fusion), channel_id=1, source_target_pairs={{0,2},{1,3},{2,0},{3,1},{4,6},{5,7},{6,4},{7,5},{8,10},{9,11},{10,... | collective-permute-start | bytes 393224 | tf_op jit(solution)/shard_map/ppermute | solution.py:246
  53.1 4.7 %collective-permute-start.22 = (bf16[2,96,128]{2,1,0:T(8,128)(2,1)S(1)}, bf16[2,96,128]{2,1,0:T(8,128)(2,1)S(1)}, u32[]{:S(2)}, u32[]{:S(2)}) collective-permute-start(bf16[2,96,128]{2,1,0:T(8,128)(2,1)S(1)} %pad_maximum_fusion.refs_0_), channel_id=1, source_target_pairs={{0,16},{4,20},{8,24},{12,28},{16,0},{20,4},{24,8},{28,12},{1,17},{... | collective-permute-start | bytes 147464 | tf_op jit(solution)/shard_map/ppermute | solution.py:243
  54.3 4.6 %collective-permute-start.21 = (bf16[2,96,128]{2,1,0:T(8,128)(2,1)S(1)}, bf16[2,96,128]{2,1,0:T(8,128)(2,1)S(1)}, u32[]{:S(2)}, u32[]{:S(2)}) collective-permute-start(bf16[2,96,128]{2,1,0:T(8,128)(2,1)S(1)} %pad_maximum_fusion.refs_0_), channel_id=1, source_target_pairs={{0,8},{4,12},{8,0},{12,4},{16,24},{20,28},{24,16},{28,20},{1,9},{5... | collective-permute-start | bytes 147464 | tf_op jit(solution)/shard_map/ppermute | solution.py:243
  55.4 5.2 %collective-permute-start.20 = (bf16[2,96,128]{2,1,0:T(8,128)(2,1)S(1)}, bf16[2,96,128]{2,1,0:T(8,128)(2,1)S(1)}, u32[]{:S(2)}, u32[]{:S(2)}) collective-permute-start(bf16[2,96,128]{2,1,0:T(8,128)(2,1)S(1)} %pad_maximum_fusion.refs_0_), channel_id=1, source_target_pairs={{0,24},{4,28},{8,16},{12,20},{16,8},{20,12},{24,0},{28,4},{1,25},{... | collective-permute-start | bytes 147464 | tf_op jit(solution)/shard_map/ppermute | solution.py:243
  (2 other events, 15.8 us)

commit v6 on v5

--- a/solution.py
+++ b/solution.py
@@ -359,12 +359,14 @@
     wait(x6a, x6b)
     x6a, x6b = tie(x6a, x6b)
     x7a, x7b = swap(x6a, 1), swap(x6b, 1)
+    packed = ranked(p0 + p1 + p2)
+    done(packed)
     wait(near1_in, far0_in)
     far1_out = pass_on(far1, tie(near1_in))
     far1_in = along(far1_out, 2)
     wait(far1_out, x7a, x7b)
     p3 = [(x6a, 6, 0), (x6b, 6, half), (x7a, 7, 0), (x7b, 7, half)]
-    packed = ranked(p0 + p1 + p2 + p3)
+    packed = ranked(p3, packed)
     done(packed)
     packed_in = along(packed, 1)
     near3 = outer(p3, held_out)
@@ -383,8 +385,6 @@
     far3_out = pass_on(far3, tie(near3_in))
     far3_in = along(far3_out, 2)
     wait(far3_out)
-    all_pieces = [p0, p1, p2, p3]
-    arrived = [(own0, near0_in, far0_in), (own1, near1_in, far1_in), (own2, near2_in, far2_in), (own3, near3_in, far3_in)]
 
     def up(first, ranks, *before):
         return pl.pallas_call(
@@ -412,6 +412,8 @@
     wait(got6)
     delta = up(6, [tie(got6)], delta)
 
+    all_pieces = [p0, p1, p2, p3]
+    arrived = [(own0, near0_in, far0_in), (own1, near1_in, far1_in), (own2, near2_in, far2_in), (own3, near3_in, far3_in)]
     pieces = [[(bits, first, part.shape[0]) for part, bits, first in piece] for piece in all_pieces]
     return pl.pallas_call(
         functools.partial(finish_kernel, pieces),

time: 62.9 us -> 62.5 us (level)
  waiting for transfers between devices: 11.6 us -> 10.4 us
  Pallas kernels: 25.7 us -> 26.7 us
    ppermute x10, waiting for transfers between devices: 10.6 us -> 9.45 us  [along(): return lax.ppermute(value, 'tensor', flip(tensors, bits))]
    pallas_call x1 -> x2, Pallas kernels: 3.42 us -> 4.39 us  [ranked(): pl.pallas_call(functools.partial(rank_kernel, blocks, len(before) > 0, le...]
  transfers between devices with their start and end apart: 23 -> 23, of which waited for: 6 -> 8; matrix products, arithmetic and copies ran while one was open for 0% -> 0% of each run, Pallas kernels for 39% -> 41%
where the time goes in v6:
time: 62.5 us; the launch traced here: 62.4 us
  Pallas kernels  26.7 us (43%)
  starting transfers between devices  24.8 us (40%)
  waiting for transfers between devices  10.4 us (17%)
    ppermute x10, starting transfers between devices, along(): return lax.ppermute(value, 'tensor', flip(tensors, bits))  13.8 us
    ppermute x13, starting transfers between devices, swap(): return lax.ppermute(value, 'replica', flip(replicas, bits))  10.9 us
    ppermute x10, waiting for transfers between devices, along(): return lax.ppermute(value, 'tensor', flip(tensors, bits))  9.45 us
    pallas_call x4, Pallas kernels, inside(): pl.pallas_call(functools.partial(first_inner_kernel if first else inner_k...  8.74 us
    pallas_call x4, Pallas kernels, outer(): pl.pallas_call(functools.partial(outer_kernel, len(parts)), out_shape=jax...  4.98 us
    pallas_call x2, Pallas kernels, ranked(): pl.pallas_call(functools.partial(rank_kernel, blocks, len(before) > 0, le...  4.39 us
    pallas_call x3, Pallas kernels, up(): pl.pallas_call(functools.partial(up_kernel, first, len(before)), out_shap...  4.06 us
    pallas_call x1, Pallas kernels, on_device_blocks(): pl.pallas_call(functools.partial(load_kernel, replicas, steps, adapters_h...  3.58 us
  transfers between devices with their start and end apart: 23, of which 8 were waited for; matrix products, arithmetic and copies ran while one was open for 0% of the time, Pallas kernels for 41%

profile of v6, /device:TPU:0, one launch (start us, length us, event | category | flops | bytes accessed | tf_op | source)
XLA Modules:
  0.0 62.4 jit_solution(9757430509557461375)
XLA Ops:
  0.5 2.5 %collective-permute-start.3 = (bf16[4,16,4096]{2,1,0:T(8,128)(2,1)}, bf16[4,16,4096]{2,1,0:T(8,128)(2,1)S(1)}, u32[]{:S(2)}, u32[]{:S(2)}) collective-permute-start(bf16[4,16,4096]{2,1,0:T(8,128)(2,1)} %refs_0_.2), channel_id=1, source_target_pairs={{0,8},{4,12},{8,0},{12,4},{16,24},{20,28},{24,16},{28,20},{1,9},{5... | collective-permute-start | bytes 1572872 | tf_op jit(solution)/shard_map/ppermute | solution.py:243
  3.0 1.5 %collective-permute-start.4 = (bf16[4,16,4096]{2,1,0:T(8,128)(2,1)}, bf16[4,16,4096]{2,1,0:T(8,128)(2,1)S(1)}, u32[]{:S(2)}, u32[]{:S(2)}) collective-permute-start(bf16[4,16,4096]{2,1,0:T(8,128)(2,1)} %refs_0_.2), channel_id=1, source_target_pairs={{0,16},{4,20},{8,24},{12,28},{16,0},{20,4},{24,8},{28,12},{1,17},{... | collective-permute-start | bytes 1572872 | tf_op jit(solution)/shard_map/ppermute | solution.py:243
  4.5 3.6 %shard_map.64 = (bf16[2,4096,512]{2,1,0:T(8,128)(2,1)S(1)}, s32[512,8]{1,0:T(8,128)S(1)}) custom-call(bf16[4096,2048]{1,0:T(8,128)(2,1)} %refs_2_.2, s32[128]{0:T(128)} %request_in.1, s32[64]{0:T(128)} %storage_in.1), custom_call_target="tpu_custom_call" | custom-call | tf_op jit(solution)/shard_map/pallas_call | solution.py:317
  8.1 1.2 %shard_map.65 = bf16[2,128,512]{2,1,0:T(8,128)(2,1)S(1)} custom-call(bf16[4,16,4096]{2,1,0:T(8,128)(2,1)S(1)} %copy-done.2, bf16[4,16,4096]{2,1,0:T(8,128)(2,1)S(1)} %collective-permute-done.refs_1_, bf16[2,4096,512]{2,1,0:T(8,128)(2,1)S(1)} %get-tuple-element.39.refs_2_.refs_4_), custom_call_target="tpu_custom_call" | custom-call | flops 1073741824 | bytes 1048576 | tf_op jit(solution)/shard_map/pallas_call | solution.py:272
  9.4 1.6 %collective-permute-start.1 = (bf16[2,128,512]{2,1,0:T(8,128)(2,1)S(1)}, bf16[2,128,512]{2,1,0:T(8,128)(2,1)S(1)}, u32[]{:S(2)}, u32[]{:S(2)}) collective-permute-start(bf16[2,128,512]{2,1,0:T(8,128)(2,1)S(1)} %shard_map.65), channel_id=1, source_target_pairs={{0,1},{1,0},{2,3},{3,2},{4,5},{5,4},{6,7},{7,6},{8,9},{9,8},{10,11... | collective-permute-start | bytes 786440 | tf_op jit(solution)/shard_map/ppermute | solution.py:246
  11.0 4.8 %shard_map.66 = (f32[128,512]{1,0:T(8,128)S(1)}, f32[128,512]{1,0:T(8,128)S(1)}, bf16[2,4096,512]{2,1,0:T(8,128)(2,1)S(1)}) custom-call(bf16[4,16,4096]{2,1,0:T(8,128)(2,1)S(1)} %copy-done.2, bf16[4,16,4096]{2,1,0:T(8,128)(2,1)S(1)} %collective-permute-done.refs_1_, bf16[4096,2048]{1,0:T(8,128)(2,1)} %refs_2_.2), custom_call_target="tpu_custom_call" | custom-call | flops 1073741824 | bytes 1048576 | tf_op jit(solution)/shard_map/pallas_call | solution.py:285
  15.8 1.8 %collective-permute-done.1.refs_1_ = bf16[2,128,512]{2,1,0:T(8,128)(2,1)S(1)} collective-permute-done((bf16[2,128,512]{2,1,0:T(8,128)(2,1)S(1)}, bf16[2,128,512]{2,1,0:T(8,128)(2,1)S(1)}, u32[]{:S(2)}, u32[]{:S(2)}) %collective-permute-start.1) | collective-permute-done | bytes 262176 | tf_op jit(solution)/shard_map/ppermute | solution.py:246
  18.2 2.6 %collective-permute-start.2 = (bf16[128,512]{1,0:T(8,128)(2,1)S(1)}, bf16[128,512]{1,0:T(8,128)(2,1)S(1)}, u32[]{:S(2)}, u32[]{:S(2)}) collective-permute-start(bf16[128,512]{1,0:T(8,128)(2,1)S(1)} %fusion.3), channel_id=1, source_target_pairs={{0,2},{1,3},{2,0},{3,1},{4,6},{5,7},{6,4},{7,5},{8,10},{9,11},{10,... | collective-permute-start | bytes 393224 | tf_op jit(solution)/shard_map/ppermute | solution.py:246
  22.5 1.2 %shard_map.67 = bf16[2,128,512]{2,1,0:T(8,128)(2,1)S(1)} custom-call(bf16[4,16,4096]{2,1,0:T(8,128)(2,1)S(1)} %collective-permute-done.3.refs_0_.refs_2_, bf16[4,16,4096]{2,1,0:T(8,128)(2,1)S(1)} %collective-permute-done.5.refs_1_.refs_3_, bf16[2,4096,512]{2,1,0:T(8,128)(2,1)S(1)} %get-tuple-element.39.refs_2_.refs_4_), custom_call_target="tpu_custom_call" | custom-call | flops 1073741824 | bytes 1048576 | tf_op jit(solution)/shard_map/pallas_call | solution.py:272
  23.7 1.6 %collective-permute-start.7 = (bf16[2,128,512]{2,1,0:T(8,128)(2,1)S(1)}, bf16[2,128,512]{2,1,0:T(8,128)(2,1)S(1)}, u32[]{:S(2)}, u32[]{:S(2)}) collective-permute-start(bf16[2,128,512]{2,1,0:T(8,128)(2,1)S(1)} %shard_map.67), channel_id=1, source_target_pairs={{0,1},{1,0},{2,3},{3,2},{4,5},{5,4},{6,7},{7,6},{8,9},{9,8},{10,11... | collective-permute-start | bytes 786440 | tf_op jit(solution)/shard_map/ppermute | solution.py:246
  25.4 1.2 %shard_map.68 = bf16[2,128,512]{2,1,0:T(8,128)(2,1)S(1)} custom-call(bf16[4,16,4096]{2,1,0:T(8,128)(2,1)S(1)} %collective-permute-done.4.refs_0_.refs_4_, bf16[4,16,4096]{2,1,0:T(8,128)(2,1)S(1)} %collective-permute-done.6.refs_1_.refs_5_, bf16[2,4096,512]{2,1,0:T(8,128)(2,1)S(1)} %get-tuple-element.39.refs_2_.refs_4_), custom_call_target="tpu_custom_call" | custom-call | flops 1073741824 | bytes 1048576 | tf_op jit(solution)/shard_map/pallas_call | solution.py:272
  27.2 1.2 %shard_map.69 = (f32[128,512]{1,0:T(8,128)S(1)}, f32[128,512]{1,0:T(8,128)S(1)}) custom-call(bf16[4,16,4096]{2,1,0:T(8,128)(2,1)S(1)} %collective-permute-done.3.refs_0_.refs_2_, bf16[4,16,4096]{2,1,0:T(8,128)(2,1)S(1)} %collective-permute-done.5.refs_1_.refs_3_, bf16[2,4096,512]{2,1,0:T(8,128)(2,1)S(1)} %get-tuple-element.49.refs_2_.refs_4_), custom_call_target="tpu_custom_call" | custom-call | flops 1073741824 | bytes 1048576 | tf_op jit(solution)/shard_map/pallas_call | solution.py:285
  28.4 1.2 %shard_map.70 = (f32[128,512]{1,0:T(8,128)S(1)}, f32[128,512]{1,0:T(8,128)S(1)}) custom-call(bf16[4,16,4096]{2,1,0:T(8,128)(2,1)S(1)} %collective-permute-done.4.refs_0_.refs_4_, bf16[4,16,4096]{2,1,0:T(8,128)(2,1)S(1)} %collective-permute-done.6.refs_1_.refs_5_, bf16[2,4096,512]{2,1,0:T(8,128)(2,1)S(1)} %get-tuple-element.49.refs_2_.refs_4_), custom_call_target="tpu_custom_call" | custom-call | flops 1073741824 | bytes 1048576 | tf_op jit(solution)/shard_map/pallas_call | solution.py:285
  30.3 2.5 %shard_map.71.refs_6_ = f32[96,128]{1,0:T(8,128)S(1)} custom-call(bf16[4,16,4096]{2,1,0:T(8,128)(2,1)S(1)} %copy-done.2, bf16[4,16,4096]{2,1,0:T(8,128)(2,1)S(1)} %collective-permute-done.refs_1_, bf16[4,16,4096]{2,1,0:T(8,128)(2,1)S(1)} %collective-permute-done.3.refs_0_.refs_2_, bf16[4,16,4096]{2,1,0:T(8,128)(2,1)S(1)} %collective-permute-done.5.refs_1_.refs_3_, ...), custom_call_target="tpu_custom_call" | custom-call | tf_op jit(solution)/shard_map/pallas_call | solution.py:301
  33.1 1.7 %collective-permute-start.10 = (bf16[128,512]{1,0:T(8,128)(2,1)S(1)}, bf16[128,512]{1,0:T(8,128)(2,1)S(1)}, u32[]{:S(2)}, u32[]{:S(2)}) collective-permute-start(bf16[128,512]{1,0:T(8,128)(2,1)S(1)} %fusion.2), channel_id=1, source_target_pairs={{0,2},{1,3},{2,0},{3,1},{4,6},{5,7},{6,4},{7,5},{8,10},{9,11},{10,... | collective-permute-start | bytes 393224 | tf_op jit(solution)/shard_map/ppermute | solution.py:246
  34.8 1.9 %shard_map.72 = f32[96,128]{1,0:T(8,128)S(1)} custom-call(bf16[2,16,4096]{2,1,0:T(8,128)(2,1)S(1)} %collective-permute-done.8.refs_0_, bf16[2,16,4096]{2,1,0:T(8,128)(2,1)S(1)} %collective-permute-done.9.refs_1_, bf16[2,16,4096]{2,1,0:T(8,128)(2,1)S(1)} %collective-permute-done.12.refs_2_, bf16[2,16,4096]{2,1,0:T(8,128)(2,1)S(1)} %collective-permute-done.13.refs_3_, ...), custom_call_target="tpu_custom_call" | custom-call | tf_op jit(solution)/shard_map/pallas_call | solution.py:301
  36.8 2.6 %collective-permute-start.15 = (f32[96,128]{1,0:T(8,128)S(1)}, f32[96,128]{1,0:T(8,128)S(1)}, u32[]{:S(2)}, u32[]{:S(2)}) collective-permute-start(f32[96,128]{1,0:T(8,128)S(1)} %shard_map.72), channel_id=1, source_target_pairs={{0,1},{1,0},{2,3},{3,2},{4,5},{5,4},{6,7},{7,6},{8,9},{9,8},{10,11... | collective-permute-start | bytes 147464 | tf_op jit(solution)/shard_map/ppermute | solution.py:246
  39.3 1.2 %shard_map.73 = bf16[2,128,512]{2,1,0:T(8,128)(2,1)S(1)} custom-call(bf16[2,16,4096]{2,1,0:T(8,128)(2,1)S(1)} %collective-permute-done.8.refs_0_, bf16[2,16,4096]{2,1,0:T(8,128)(2,1)S(1)} %collective-permute-done.9.refs_1_, bf16[2,16,4096]{2,1,0:T(8,128)(2,1)S(1)} %collective-permute-done.12.refs_2_, ...), custom_call_target="tpu_custom_call" | custom-call | flops 1073741824 | bytes 1048576 | tf_op jit(solution)/shard_map/pallas_call | solution.py:272
  40.7 1.5 %collective-permute-done.10.refs_5_ = bf16[128,512]{1,0:T(8,128)(2,1)S(1)} collective-permute-done((bf16[128,512]{1,0:T(8,128)(2,1)S(1)}, bf16[128,512]{1,0:T(8,128)(2,1)S(1)}, u32[]{:S(2)}, u32[]{:S(2)}) %collective-permute-start.10) | collective-permute-done | bytes 131104 | tf_op jit(solution)/shard_map/ppermute | solution.py:246
  44.2 2.0 %collective-permute-start.14 = (bf16[128,512]{1,0:T(8,128)(2,1)S(1)}, bf16[128,512]{1,0:T(8,128)(2,1)S(1)}, u32[]{:S(2)}, u32[]{:S(2)}) collective-permute-start(bf16[128,512]{1,0:T(8,128)(2,1)S(1)} %fusion.1), channel_id=1, source_target_pairs={{0,2},{1,3},{2,0},{3,1},{4,6},{5,7},{6,4},{7,5},{8,10},{9,11},{10,... | collective-permute-start | bytes 393224 | tf_op jit(solution)/shard_map/ppermute | solution.py:246
  46.2 1.5 %shard_map.74 = (f32[128,512]{1,0:T(8,128)S(1)}, f32[128,512]{1,0:T(8,128)S(1)}) custom-call(bf16[2,16,4096]{2,1,0:T(8,128)(2,1)S(1)} %collective-permute-done.8.refs_0_, bf16[2,16,4096]{2,1,0:T(8,128)(2,1)S(1)} %collective-permute-done.9.refs_1_, bf16[2,16,4096]{2,1,0:T(8,128)(2,1)S(1)} %collective-permute-done.12.refs_2_, ...), custom_call_target="tpu_custom_call" | custom-call | flops 1073741824 | bytes 1048576 | tf_op jit(solution)/shard_map/pallas_call | solution.py:285
  47.6 3.5 %collective-permute-done.16.refs_10_ = bf16[2,128,512]{2,1,0:T(8,128)(2,1)S(1)} collective-permute-done((bf16[2,128,512]{2,1,0:T(8,128)(2,1)S(1)}, bf16[2,128,512]{2,1,0:T(8,128)(2,1)S(1)}, u32[]{:S(2)}, u32[]{:S(2)}) %collective-permute-start.16) | collective-permute-done | bytes 262176 | tf_op jit(solution)/shard_map/ppermute | solution.py:246
  51.5 1.3 %collective-permute-done.14.refs_8_ = bf16[128,512]{1,0:T(8,128)(2,1)S(1)} collective-permute-done((bf16[128,512]{1,0:T(8,128)(2,1)S(1)}, bf16[128,512]{1,0:T(8,128)(2,1)S(1)}, u32[]{:S(2)}, u32[]{:S(2)}) %collective-permute-start.14) | collective-permute-done | bytes 131104 | tf_op jit(solution)/shard_map/ppermute | solution.py:246
  58.2 1.7 %shard_map.76.refs_3_ = f32[512,512]{1,0:T(8,128)S(1)} custom-call(bf16[2,96,128]{2,1,0:T(8,128)(2,1)S(1)} %collective-permute-done.21.refs_0_, bf16[2,96,128]{2,1,0:T(8,128)(2,1)S(1)} %collective-permute-done.22.refs_1_, bf16[64,64,512]{2,1,0:T(8,128)(2,1)S(1)} %copy-done, s32[512,8]{1,0:T(8,128)S(1)} %get-tuple-element.55.refs_7_.refs_5_.refs_2_.refs_3_, ...), custom_call_target="tpu_custom_call" | custom-call | tf_op jit(solution)/shard_map/pallas_call | solution.py:390
  (52 shorter events, 14.4 us)
Async XLA Ops:
  0.0 8.1 %collective-permute-start = (bf16[4,16,4096]{2,1,0:T(8,128)(2,1)}, bf16[4,16,4096]{2,1,0:T(8,128)(2,1)S(1)}, u32[]{:S(2)}, u32[]{:S(2)}) collective-permute-start(bf16[4,16,4096]{2,1,0:T(8,128)(2,1)} %refs_0_.2), channel_id=1, source_target_pairs={{0,4},{4,0},{8,12},{12,8},{16,20},{20,16},{24,28},{28,24},{1,5},{5... | collective-permute-start | bytes 1572872 | tf_op jit(solution)/shard_map/ppermute | solution.py:243
  0.5 17.1 %collective-permute-start.3 = (bf16[4,16,4096]{2,1,0:T(8,128)(2,1)}, bf16[4,16,4096]{2,1,0:T(8,128)(2,1)S(1)}, u32[]{:S(2)}, u32[]{:S(2)}) collective-permute-start(bf16[4,16,4096]{2,1,0:T(8,128)(2,1)} %refs_0_.2), channel_id=1, source_target_pairs={{0,8},{4,12},{8,0},{12,4},{16,24},{20,28},{24,16},{28,20},{1,9},{5... | collective-permute-start | bytes 1572872 | tf_op jit(solution)/shard_map/ppermute | solution.py:243
  3.0 14.6 %collective-permute-start.4 = (bf16[4,16,4096]{2,1,0:T(8,128)(2,1)}, bf16[4,16,4096]{2,1,0:T(8,128)(2,1)S(1)}, u32[]{:S(2)}, u32[]{:S(2)}) collective-permute-start(bf16[4,16,4096]{2,1,0:T(8,128)(2,1)} %refs_0_.2), channel_id=1, source_target_pairs={{0,16},{4,20},{8,24},{12,28},{16,0},{20,4},{24,8},{28,12},{1,17},{... | collective-permute-start | bytes 1572872 | tf_op jit(solution)/shard_map/ppermute | solution.py:243
  9.4 8.2 %collective-permute-start.1 = (bf16[2,128,512]{2,1,0:T(8,128)(2,1)S(1)}, bf16[2,128,512]{2,1,0:T(8,128)(2,1)S(1)}, u32[]{:S(2)}, u32[]{:S(2)}) collective-permute-start(bf16[2,128,512]{2,1,0:T(8,128)(2,1)S(1)} %shard_map.65), channel_id=1, source_target_pairs={{0,1},{1,0},{2,3},{3,2},{4,5},{5,4},{6,7},{7,6},{8,9},{9,8},{10,11... | collective-permute-start | bytes 786440 | tf_op jit(solution)/shard_map/ppermute | solution.py:246
  17.6 4.9 %collective-permute-start.5 = (bf16[4,16,4096]{2,1,0:T(8,128)(2,1)S(1)}, bf16[4,16,4096]{2,1,0:T(8,128)(2,1)S(1)}, u32[]{:S(2)}, u32[]{:S(2)}) collective-permute-start(bf16[4,16,4096]{2,1,0:T(8,128)(2,1)S(1)} %collective-permute-done.3.refs_0_.refs_2_), channel_id=1, source_target_pairs={{0,4},{4,0},{8,12},{12,8},{16,20},{20,16},{24,28},{28,24},{1,5},{5... | collective-permute-start | bytes 1572872 | tf_op jit(solution)/shard_map/ppermute | solution.py:243
  17.7 7.7 %collective-permute-start.6 = (bf16[4,16,4096]{2,1,0:T(8,128)(2,1)S(1)}, bf16[4,16,4096]{2,1,0:T(8,128)(2,1)S(1)}, u32[]{:S(2)}, u32[]{:S(2)}) collective-permute-start(bf16[4,16,4096]{2,1,0:T(8,128)(2,1)S(1)} %collective-permute-done.4.refs_0_.refs_4_), channel_id=1, source_target_pairs={{0,4},{4,0},{8,12},{12,8},{16,20},{20,16},{24,28},{28,24},{1,5},{5... | collective-permute-start | bytes 1572872 | tf_op jit(solution)/shard_map/ppermute | solution.py:243
  18.2 14.5 %collective-permute-start.2 = (bf16[128,512]{1,0:T(8,128)(2,1)S(1)}, bf16[128,512]{1,0:T(8,128)(2,1)S(1)}, u32[]{:S(2)}, u32[]{:S(2)}) collective-permute-start(bf16[128,512]{1,0:T(8,128)(2,1)S(1)} %fusion.3), channel_id=1, source_target_pairs={{0,2},{1,3},{2,0},{3,1},{4,6},{5,7},{6,4},{7,5},{8,10},{9,11},{10,... | collective-permute-start | bytes 393224 | tf_op jit(solution)/shard_map/ppermute | solution.py:246
  20.8 8.8 %collective-permute-start.9 = (bf16[2,16,4096]{2,1,0:T(8,128)(2,1)S(1)}, bf16[2,16,4096]{2,1,0:T(8,128)(2,1)S(1)}, u32[]{:S(2)}, u32[]{:S(2)}) collective-permute-start(bf16[2,16,4096]{2,1,0:T(8,128)(2,1)S(1)} %slice.20), channel_id=1, source_target_pairs={{0,8},{4,12},{8,0},{12,4},{16,24},{20,28},{24,16},{28,20},{1,9},{5... | collective-permute-start | bytes 786440 | tf_op jit(solution)/shard_map/ppermute | solution.py:243
  21.4 8.2 %collective-permute-start.8 = (bf16[2,16,4096]{2,1,0:T(8,128)(2,1)S(1)}, bf16[2,16,4096]{2,1,0:T(8,128)(2,1)S(1)}, u32[]{:S(2)}, u32[]{:S(2)}) collective-permute-start(bf16[2,16,4096]{2,1,0:T(8,128)(2,1)S(1)} %slice.19), channel_id=1, source_target_pairs={{0,16},{4,20},{8,24},{12,28},{16,0},{20,4},{24,8},{28,12},{1,17},{... | collective-permute-start | bytes 786440 | tf_op jit(solution)/shard_map/ppermute | solution.py:243
  23.7 9.3 %collective-permute-start.7 = (bf16[2,128,512]{2,1,0:T(8,128)(2,1)S(1)}, bf16[2,128,512]{2,1,0:T(8,128)(2,1)S(1)}, u32[]{:S(2)}, u32[]{:S(2)}) collective-permute-start(bf16[2,128,512]{2,1,0:T(8,128)(2,1)S(1)} %shard_map.67), channel_id=1, source_target_pairs={{0,1},{1,0},{2,3},{3,2},{4,5},{5,4},{6,7},{7,6},{8,9},{9,8},{10,11... | collective-permute-start | bytes 786440 | tf_op jit(solution)/shard_map/ppermute | solution.py:246
  26.6 14.0 %collective-permute-start.11 = (bf16[2,128,512]{2,1,0:T(8,128)(2,1)S(1)}, bf16[2,128,512]{2,1,0:T(8,128)(2,1)S(1)}, u32[]{:S(2)}, u32[]{:S(2)}) collective-permute-start(bf16[2,128,512]{2,1,0:T(8,128)(2,1)S(1)} %shard_map.68), channel_id=1, source_target_pairs={{0,1},{1,0},{2,3},{3,2},{4,5},{5,4},{6,7},{7,6},{8,9},{9,8},{10,11... | collective-permute-start | bytes 786440 | tf_op jit(solution)/shard_map/ppermute | solution.py:246
  29.7 5.1 %collective-permute-start.12 = (bf16[2,16,4096]{2,1,0:T(8,128)(2,1)S(1)}, bf16[2,16,4096]{2,1,0:T(8,128)(2,1)S(1)}, u32[]{:S(2)}, u32[]{:S(2)}) collective-permute-start(bf16[2,16,4096]{2,1,0:T(8,128)(2,1)S(1)} %collective-permute-done.8.refs_0_), channel_id=1, source_target_pairs={{0,4},{4,0},{8,12},{12,8},{16,20},{20,16},{24,28},{28,24},{1,5},{5... | collective-permute-start | bytes 786440 | tf_op jit(solution)/shard_map/ppermute | solution.py:243
  29.8 5.1 %collective-permute-start.13 = (bf16[2,16,4096]{2,1,0:T(8,128)(2,1)S(1)}, bf16[2,16,4096]{2,1,0:T(8,128)(2,1)S(1)}, u32[]{:S(2)}, u32[]{:S(2)}) collective-permute-start(bf16[2,16,4096]{2,1,0:T(8,128)(2,1)S(1)} %collective-permute-done.9.refs_1_), channel_id=1, source_target_pairs={{0,4},{4,0},{8,12},{12,8},{16,20},{20,16},{24,28},{28,24},{1,5},{5... | collective-permute-start | bytes 786440 | tf_op jit(solution)/shard_map/ppermute | solution.py:243
  33.1 9.1 %collective-permute-start.10 = (bf16[128,512]{1,0:T(8,128)(2,1)S(1)}, bf16[128,512]{1,0:T(8,128)(2,1)S(1)}, u32[]{:S(2)}, u32[]{:S(2)}) collective-permute-start(bf16[128,512]{1,0:T(8,128)(2,1)S(1)} %fusion.2), channel_id=1, source_target_pairs={{0,2},{1,3},{2,0},{3,1},{4,6},{5,7},{6,4},{7,5},{8,10},{9,11},{10,... | collective-permute-start | bytes 393224 | tf_op jit(solution)/shard_map/ppermute | solution.py:246
  36.8 19.6 %copy-start = (bf16[64,64,512]{2,1,0:T(8,128)(2,1)S(1)}, bf16[64,64,512]{2,1,0:T(8,128)(2,1)}, u32[]{:S(2)}) copy-start(bf16[64,64,512]{2,1,0:T(8,128)(2,1)} %refs_1_.3) | copy-start | bytes 12582916
  36.8 6.4 %collective-permute-start.15 = (f32[96,128]{1,0:T(8,128)S(1)}, f32[96,128]{1,0:T(8,128)S(1)}, u32[]{:S(2)}, u32[]{:S(2)}) collective-permute-start(f32[96,128]{1,0:T(8,128)S(1)} %shard_map.72), channel_id=1, source_target_pairs={{0,1},{1,0},{2,3},{3,2},{4,5},{5,4},{6,7},{7,6},{8,9},{9,8},{10,11... | collective-permute-start | bytes 147464 | tf_op jit(solution)/shard_map/ppermute | solution.py:246
  40.6 10.6 %collective-permute-start.16 = (bf16[2,128,512]{2,1,0:T(8,128)(2,1)S(1)}, bf16[2,128,512]{2,1,0:T(8,128)(2,1)S(1)}, u32[]{:S(2)}, u32[]{:S(2)}) collective-permute-start(bf16[2,128,512]{2,1,0:T(8,128)(2,1)S(1)} %shard_map.73), channel_id=1, source_target_pairs={{0,1},{1,0},{2,3},{3,2},{4,5},{5,4},{6,7},{7,6},{8,9},{9,8},{10,11... | collective-permute-start | bytes 786440 | tf_op jit(solution)/shard_map/ppermute | solution.py:246
  43.2 8.0 %collective-permute-start.18 = (f32[96,128]{1,0:T(8,128)S(1)}, f32[96,128]{1,0:T(8,128)S(1)}, u32[]{:S(2)}, u32[]{:S(2)}) collective-permute-start(f32[96,128]{1,0:T(8,128)S(1)} %add.21), channel_id=1, source_target_pairs={{0,2},{1,3},{2,0},{3,1},{4,6},{5,7},{6,4},{7,5},{8,10},{9,11},{10,... | collective-permute-start | bytes 147464 | tf_op jit(solution)/shard_map/ppermute | solution.py:246
  44.2 8.6 %collective-permute-start.14 = (bf16[128,512]{1,0:T(8,128)(2,1)S(1)}, bf16[128,512]{1,0:T(8,128)(2,1)S(1)}, u32[]{:S(2)}, u32[]{:S(2)}) collective-permute-start(bf16[128,512]{1,0:T(8,128)(2,1)S(1)} %fusion.1), channel_id=1, source_target_pairs={{0,2},{1,3},{2,0},{3,1},{4,6},{5,7},{6,4},{7,5},{8,10},{9,11},{10,... | collective-permute-start | bytes 393224 | tf_op jit(solution)/shard_map/ppermute | solution.py:246
  51.2 1.6 %collective-permute-start.19 = (bf16[1,96,128]{2,1,0:T(8,128)(2,1)S(1)}, bf16[1,96,128]{2,1,0:T(8,128)(2,1)S(1)}, u32[]{:S(2)}, u32[]{:S(2)}) collective-permute-start(bf16[1,96,128]{2,1,0:T(8,128)(2,1)S(1)} %fusion.4), channel_id=1, source_target_pairs={{0,4},{4,0},{8,12},{12,8},{16,20},{20,16},{24,28},{28,24},{1,5},{5... | collective-permute-start | bytes 73736 | tf_op jit(solution)/shard_map/ppermute | solution.py:243
  51.3 10.1 %collective-permute-start.17 = (bf16[128,512]{1,0:T(8,128)(2,1)S(1)}, bf16[128,512]{1,0:T(8,128)(2,1)S(1)}, u32[]{:S(2)}, u32[]{:S(2)}) collective-permute-start(bf16[128,512]{1,0:T(8,128)(2,1)S(1)} %fusion), channel_id=1, source_target_pairs={{0,2},{1,3},{2,0},{3,1},{4,6},{5,7},{6,4},{7,5},{8,10},{9,11},{10,... | collective-permute-start | bytes 393224 | tf_op jit(solution)/shard_map/ppermute | solution.py:246
  52.8 4.7 %collective-permute-start.22 = (bf16[2,96,128]{2,1,0:T(8,128)(2,1)S(1)}, bf16[2,96,128]{2,1,0:T(8,128)(2,1)S(1)}, u32[]{:S(2)}, u32[]{:S(2)}) collective-permute-start(bf16[2,96,128]{2,1,0:T(8,128)(2,1)S(1)} %pad_maximum_fusion.refs_0_), channel_id=1, source_target_pairs={{0,16},{4,20},{8,24},{12,28},{16,0},{20,4},{24,8},{28,12},{1,17},{... | collective-permute-start | bytes 147464 | tf_op jit(solution)/shard_map/ppermute | solution.py:243
  54.0 4.2 %collective-permute-start.21 = (bf16[2,96,128]{2,1,0:T(8,128)(2,1)S(1)}, bf16[2,96,128]{2,1,0:T(8,128)(2,1)S(1)}, u32[]{:S(2)}, u32[]{:S(2)}) collective-permute-start(bf16[2,96,128]{2,1,0:T(8,128)(2,1)S(1)} %pad_maximum_fusion.refs_0_), channel_id=1, source_target_pairs={{0,8},{4,12},{8,0},{12,4},{16,24},{20,28},{24,16},{28,20},{1,9},{5... | collective-permute-start | bytes 147464 | tf_op jit(solution)/shard_map/ppermute | solution.py:243
  55.2 5.0 %collective-permute-start.20 = (bf16[2,96,128]{2,1,0:T(8,128)(2,1)S(1)}, bf16[2,96,128]{2,1,0:T(8,128)(2,1)S(1)}, u32[]{:S(2)}, u32[]{:S(2)}) collective-permute-start(bf16[2,96,128]{2,1,0:T(8,128)(2,1)S(1)} %pad_maximum_fusion.refs_0_), channel_id=1, source_target_pairs={{0,24},{4,28},{8,16},{12,20},{16,8},{20,12},{24,0},{28,4},{1,25},{... | collective-permute-start | bytes 147464 | tf_op jit(solution)/shard_map/ppermute | solution.py:243
  (2 other events, 11.2 us)

commit v7 on v6

--- a/solution.py
+++ b/solution.py
@@ -112,9 +112,16 @@
 
 
 def first_inner_kernel(n, *refs):
-    parts, whole, far, own, weight, rows, sems = refs[:n], *refs[n:]
+    parts, whole, down, far, own, weight, turned_down, rows, sems = refs[:n], *refs[n:]
     copies = fetch(whole, weight, sems, (2, 0))
     stack_rows(parts, rows)
+    adapters, rank, feats = down.shape
+    pair = 128 // rank
+    for first in range(0, adapters, pair):
+        for at in range(0, feats, WIDE):
+            some = pl.ds(at, WIDE)
+            block = down[pl.ds(first, pair), :, some].reshape(pair * rank, WIDE)
+            turned_down[some, pl.ds(first * rank, pair * rank)] = block.T
     for copy in copies:
         copy.wait()
     inner_dots(rows, weight, far, own)
@@ -130,7 +137,8 @@
     parts, rest, rows = refs[:n], refs[n:-1], refs[-1]
     down, where, out = rest[0], rest[1], rest[-1]
     me = lax.axis_index("replica")
-    adapters, rank, feats = down.shape
+    rank = out.shape[1] // 2
+    adapters = down.shape[1] // rank
     stack_rows(parts, rows)
     total = rows.shape[0]
     whole = where.shape[0] // lax.axis_size("replica")
@@ -140,12 +148,7 @@
         at = pl.multiple_of((me ^ bits) * whole + first * requests, requests)
         here.append(where[pl.ds(at, steps * requests), :])
     here = jnp.concatenate(here, axis=0)
-    reduced = lax.dot_general(
-        rows[...],
-        down[...].reshape(adapters * rank, feats),
-        (((1,), (1,)), ((), ())),
-        preferred_element_type=jnp.float32,
-    )
+    reduced = jnp.dot(rows[...], down[...], preferred_element_type=jnp.float32)
     local = here[:, 0:1] - me * adapters
     adapter_of = lax.broadcasted_iota(jnp.int32, (total, adapters * rank), 1) // rank
     picked = jnp.where(adapter_of == local, reduced, 0.0)
@@ -279,18 +282,20 @@
             cost_estimate=cost(n, 2 * cols),
         )(*parts, weight)
 
-    def inside(piece, weight, first=False):
+    def inside(piece, weight, *extra):
         parts = held_back(piece)
         n = sum(p.shape[0] * p.shape[1] for p in parts)
+        first = len(extra) > 0
         return pl.pallas_call(
             functools.partial(first_inner_kernel if first else inner_kernel, len(parts)),
-            out_shape=[jax.ShapeDtypeStruct((n, cols), jnp.float32)] * 2 + [held] * first,
-            in_specs=[VMEM] * len(parts) + [HBM if first else VMEM],
-            out_specs=[VMEM] * (2 + first),
+            out_shape=[jax.ShapeDtypeStruct((n, cols), jnp.float32)] * 2
+            + [held, pltpu.VMEM((feats, adapters_here * rank), jnp.bfloat16)] * first,
+            in_specs=[VMEM] * len(parts) + [HBM if first else VMEM] + [VMEM] * first,
+            out_specs=[VMEM] * (2 + 2 * first),
             scratch_shapes=[pltpu.VMEM((n, feats), jnp.bfloat16)] + [copies] * first,
             compiler_params=params(8),
             cost_estimate=cost(n, 2 * cols),
-        )(*parts, weight)
+        )(*parts, weight, *extra)
 
     down = jnp.transpose(adapter_down_weight, (0, 2, 1))
 
@@ -306,7 +311,7 @@
             scratch_shapes=[pltpu.VMEM((n, feats), jnp.bfloat16)],
             compiler_params=params(10),
             cost_estimate=pl.CostEstimate(flops=0, bytes_accessed=0, transcendentals=0),
-        )(*parts, down, where, *before)
+        )(*parts, turned_down, where, *before)
 
     def pass_on(far, near_in):
         return (far + near_in[1].astype(jnp.float32)).astype(jnp.bfloat16)
@@ -331,7 +336,7 @@
     near0 = outer(p0, held_out)
     done(near0)
     near0_in = along(near0, 1)
-    far0, own0, held_in = inside(p0, weight, True)
+    far0, own0, held_in, turned_down = inside(p0, weight, down)
     done(own0)
     wait(near0_in)
     far0_out = pass_on(far0, tie(near0_in))
@@ -372,13 +377,14 @@
     near3 = outer(p3, held_out)
     done(near3)
     near3_in = along(near3, 1)
-    wait(near2_in, far1_in)
-    far2_out = pass_on(far2, tie(near2_in))
-    wait(far2_out, packed_in)
+    wait(packed_in, far1_in)
     packed = packed + tie(packed_in)
     done(packed)
     packed_in = along(packed, 2)
+    wait(near2_in)
+    far2_out = pass_on(far2, tie(near2_in))
     far2_in = along(far2_out, 2)
+    wait(far2_out)
     far3, own3 = inside(p3, held_in)
     done(own3)
     wait(near3_in)

time: 62.5 us -> 62.8 us (level)
  starting transfers between devices: 24.8 us -> 25.6 us
    ppermute x10, starting transfers between devices: 13.8 us -> 14.7 us  [along(): return lax.ppermute(value, 'tensor', flip(tensors, bits))]
    pallas_call x2, Pallas kernels: 4.39 us -> 3.66 us  [ranked(): pl.pallas_call(functools.partial(rank_kernel, blocks, len(before) > 0, le...]
  transfers between devices with their start and end apart: 23 -> 23, of which waited for: 8 -> 7; matrix products, arithmetic and copies ran while one was open for 0% -> 0% of each run, Pallas kernels for 41% -> 40%
where the time goes in v7:
time: 62.8 us; the launch traced here: 62.7 us
  Pallas kernels  26.1 us (42%)
  starting transfers between devices  25.6 us (41%)
  waiting for transfers between devices  10.5 us (17%)
    ppermute x10, starting transfers between devices, along(): return lax.ppermute(value, 'tensor', flip(tensors, bits))  14.7 us
    ppermute x13, starting transfers between devices, swap(): return lax.ppermute(value, 'replica', flip(replicas, bits))  10.9 us
    ppermute x10, waiting for transfers between devices, along(): return lax.ppermute(value, 'tensor', flip(tensors, bits))  9.93 us
    pallas_call x4, Pallas kernels, inside(): pl.pallas_call(functools.partial(first_inner_kernel if first else inner_k...  8.56 us
    pallas_call x4, Pallas kernels, outer(): pl.pallas_call(functools.partial(outer_kernel, len(parts)), out_shape=jax...  5.22 us
    pallas_call x3, Pallas kernels, up(): pl.pallas_call(functools.partial(up_kernel, first, len(before)), out_shap...  4.06 us
    pallas_call x2, Pallas kernels, ranked(): pl.pallas_call(functools.partial(rank_kernel, blocks, len(before) > 0, le...  3.66 us
    pallas_call x1, Pallas kernels, on_device_blocks(): pl.pallas_call(functools.partial(load_kernel, replicas, steps, adapters_h...  3.58 us
  transfers between devices with their start and end apart: 23, of which 7 were waited for; matrix products, arithmetic and copies ran while one was open for 0% of the time, Pallas kernels for 40%

profile of v7, /device:TPU:0, one launch (start us, length us, event | category | flops | bytes accessed | tf_op | source)
XLA Modules:
  0.0 62.7 jit_solution(4803639432797184526)
XLA Ops:
  0.5 2.5 %collective-permute-start.3 = (bf16[4,16,4096]{2,1,0:T(8,128)(2,1)}, bf16[4,16,4096]{2,1,0:T(8,128)(2,1)S(1)}, u32[]{:S(2)}, u32[]{:S(2)}) collective-permute-start(bf16[4,16,4096]{2,1,0:T(8,128)(2,1)} %refs_0_.2), channel_id=1, source_target_pairs={{0,8},{4,12},{8,0},{12,4},{16,24},{20,28},{24,16},{28,20},{1,9},{5... | collective-permute-start | bytes 1572872 | tf_op jit(solution)/shard_map/ppermute | solution.py:246
  3.0 1.5 %collective-permute-start.4 = (bf16[4,16,4096]{2,1,0:T(8,128)(2,1)}, bf16[4,16,4096]{2,1,0:T(8,128)(2,1)S(1)}, u32[]{:S(2)}, u32[]{:S(2)}) collective-permute-start(bf16[4,16,4096]{2,1,0:T(8,128)(2,1)} %refs_0_.2), channel_id=1, source_target_pairs={{0,16},{4,20},{8,24},{12,28},{16,0},{20,4},{24,8},{28,12},{1,17},{... | collective-permute-start | bytes 1572872 | tf_op jit(solution)/shard_map/ppermute | solution.py:246
  4.5 3.6 %shard_map.64 = (bf16[2,4096,512]{2,1,0:T(8,128)(2,1)S(1)}, s32[512,8]{1,0:T(8,128)S(1)}) custom-call(bf16[4096,2048]{1,0:T(8,128)(2,1)} %refs_2_.2, s32[128]{0:T(128)} %request_in.1, s32[64]{0:T(128)} %storage_in.1), custom_call_target="tpu_custom_call" | custom-call | tf_op jit(solution)/shard_map/pallas_call | solution.py:322
  9.4 1.6 %collective-permute-start.1 = (bf16[2,128,512]{2,1,0:T(8,128)(2,1)S(1)}, bf16[2,128,512]{2,1,0:T(8,128)(2,1)S(1)}, u32[]{:S(2)}, u32[]{:S(2)}) collective-permute-start(bf16[2,128,512]{2,1,0:T(8,128)(2,1)S(1)} %shard_map.65), channel_id=1, source_target_pairs={{0,1},{1,0},{2,3},{3,2},{4,5},{5,4},{6,7},{7,6},{8,9},{9,8},{10,11... | collective-permute-start | bytes 786440 | tf_op jit(solution)/shard_map/ppermute | solution.py:249
  11.0 4.8 %shard_map.66 = (f32[128,512]{1,0:T(8,128)S(1)}, f32[128,512]{1,0:T(8,128)S(1)}, bf16[2,4096,512]{2,1,0:T(8,128)(2,1)S(1)}, bf16[4096,512]{1,0:T(8,128)(2,1)S(1)}) custom-call(bf16[4,16,4096]{2,1,0:T(8,128)(2,1)S(1)} %copy-done.1, bf16[4,16,4096]{2,1,0:T(8,128)(2,1)S(1)} %collective-permute-done.refs_1_, bf16[4096,2048]{1,0:T(8,128)(2,1)} %refs_2_.2, ...), custom_call_target="tpu_custom_call" | custom-call | flops 1073741824 | bytes 1048576 | tf_op jit(solution)/shard_map/pallas_call | solution.py:289
  15.8 1.7 %collective-permute-done.1.refs_1_ = bf16[2,128,512]{2,1,0:T(8,128)(2,1)S(1)} collective-permute-done((bf16[2,128,512]{2,1,0:T(8,128)(2,1)S(1)}, bf16[2,128,512]{2,1,0:T(8,128)(2,1)S(1)}, u32[]{:S(2)}, u32[]{:S(2)}) %collective-permute-start.1) | collective-permute-done | bytes 262176 | tf_op jit(solution)/shard_map/ppermute | solution.py:249
  18.2 2.6 %collective-permute-start.2 = (bf16[128,512]{1,0:T(8,128)(2,1)S(1)}, bf16[128,512]{1,0:T(8,128)(2,1)S(1)}, u32[]{:S(2)}, u32[]{:S(2)}) collective-permute-start(bf16[128,512]{1,0:T(8,128)(2,1)S(1)} %fusion.3), channel_id=1, source_target_pairs={{0,2},{1,3},{2,0},{3,1},{4,6},{5,7},{6,4},{7,5},{8,10},{9,11},{10,... | collective-permute-start | bytes 393224 | tf_op jit(solution)/shard_map/ppermute | solution.py:249
  22.5 1.3 %shard_map.67 = bf16[2,128,512]{2,1,0:T(8,128)(2,1)S(1)} custom-call(bf16[4,16,4096]{2,1,0:T(8,128)(2,1)S(1)} %collective-permute-done.3.refs_0_.refs_2_, bf16[4,16,4096]{2,1,0:T(8,128)(2,1)S(1)} %collective-permute-done.5.refs_1_.refs_3_, bf16[2,4096,512]{2,1,0:T(8,128)(2,1)S(1)} %get-tuple-element.40.refs_2_.refs_4_), custom_call_target="tpu_custom_call" | custom-call | flops 1073741824 | bytes 1048576 | tf_op jit(solution)/shard_map/pallas_call | solution.py:275
  23.8 1.6 %collective-permute-start.7 = (bf16[2,128,512]{2,1,0:T(8,128)(2,1)S(1)}, bf16[2,128,512]{2,1,0:T(8,128)(2,1)S(1)}, u32[]{:S(2)}, u32[]{:S(2)}) collective-permute-start(bf16[2,128,512]{2,1,0:T(8,128)(2,1)S(1)} %shard_map.67), channel_id=1, source_target_pairs={{0,1},{1,0},{2,3},{3,2},{4,5},{5,4},{6,7},{7,6},{8,9},{9,8},{10,11... | collective-permute-start | bytes 786440 | tf_op jit(solution)/shard_map/ppermute | solution.py:249
  27.2 1.3 %shard_map.69 = (f32[128,512]{1,0:T(8,128)S(1)}, f32[128,512]{1,0:T(8,128)S(1)}) custom-call(bf16[4,16,4096]{2,1,0:T(8,128)(2,1)S(1)} %collective-permute-done.3.refs_0_.refs_2_, bf16[4,16,4096]{2,1,0:T(8,128)(2,1)S(1)} %collective-permute-done.5.refs_1_.refs_3_, bf16[2,4096,512]{2,1,0:T(8,128)(2,1)S(1)} %get-tuple-element.50.refs_2_.refs_4_), custom_call_target="tpu_custom_call" | custom-call | flops 1073741824 | bytes 1048576 | tf_op jit(solution)/shard_map/pallas_call | solution.py:289
  28.4 1.2 %shard_map.70 = (f32[128,512]{1,0:T(8,128)S(1)}, f32[128,512]{1,0:T(8,128)S(1)}) custom-call(bf16[4,16,4096]{2,1,0:T(8,128)(2,1)S(1)} %collective-permute-done.4.refs_0_.refs_4_, bf16[4,16,4096]{2,1,0:T(8,128)(2,1)S(1)} %collective-permute-done.6.refs_1_.refs_5_, bf16[2,4096,512]{2,1,0:T(8,128)(2,1)S(1)} %get-tuple-element.50.refs_2_.refs_4_), custom_call_target="tpu_custom_call" | custom-call | flops 1073741824 | bytes 1048576 | tf_op jit(solution)/shard_map/pallas_call | solution.py:289
  30.3 2.4 %shard_map.71.refs_6_ = f32[96,128]{1,0:T(8,128)S(1)} custom-call(bf16[4,16,4096]{2,1,0:T(8,128)(2,1)S(1)} %copy-done.1, bf16[4,16,4096]{2,1,0:T(8,128)(2,1)S(1)} %collective-permute-done.refs_1_, bf16[4,16,4096]{2,1,0:T(8,128)(2,1)S(1)} %collective-permute-done.3.refs_0_.refs_2_, bf16[4,16,4096]{2,1,0:T(8,128)(2,1)S(1)} %collective-permute-done.5.refs_1_.refs_3_, ...), custom_call_target="tpu_custom_call" | custom-call | tf_op jit(solution)/shard_map/pallas_call | solution.py:306
  33.1 1.7 %collective-permute-start.10 = (bf16[128,512]{1,0:T(8,128)(2,1)S(1)}, bf16[128,512]{1,0:T(8,128)(2,1)S(1)}, u32[]{:S(2)}, u32[]{:S(2)}) collective-permute-start(bf16[128,512]{1,0:T(8,128)(2,1)S(1)} %fusion.2), channel_id=1, source_target_pairs={{0,2},{1,3},{2,0},{3,1},{4,6},{5,7},{6,4},{7,5},{8,10},{9,11},{10,... | collective-permute-start | bytes 393224 | tf_op jit(solution)/shard_map/ppermute | solution.py:249
  36.1 2.5 %collective-permute-start.14 = (f32[96,128]{1,0:T(8,128)S(1)}, f32[96,128]{1,0:T(8,128)S(1)}, u32[]{:S(2)}, u32[]{:S(2)}) collective-permute-start(f32[96,128]{1,0:T(8,128)S(1)} %shard_map.72), channel_id=1, source_target_pairs={{0,1},{1,0},{2,3},{3,2},{4,5},{5,4},{6,7},{7,6},{8,9},{9,8},{10,11... | collective-permute-start | bytes 147464 | tf_op jit(solution)/shard_map/ppermute | solution.py:249
  38.6 1.5 %shard_map.73 = bf16[2,128,512]{2,1,0:T(8,128)(2,1)S(1)} custom-call(bf16[2,16,4096]{2,1,0:T(8,128)(2,1)S(1)} %collective-permute-done.8.refs_0_, bf16[2,16,4096]{2,1,0:T(8,128)(2,1)S(1)} %collective-permute-done.9.refs_1_, bf16[2,16,4096]{2,1,0:T(8,128)(2,1)S(1)} %collective-permute-done.12.refs_2_, ...), custom_call_target="tpu_custom_call" | custom-call | flops 1073741824 | bytes 1048576 | tf_op jit(solution)/shard_map/pallas_call | solution.py:275
  40.2 2.4 %collective-permute-done.14 = f32[96,128]{1,0:T(8,128)S(1)} collective-permute-done((f32[96,128]{1,0:T(8,128)S(1)}, f32[96,128]{1,0:T(8,128)S(1)}, u32[]{:S(2)}, u32[]{:S(2)}) %collective-permute-start.14) | collective-permute-done | bytes 49184 | tf_op jit(solution)/shard_map/ppermute | solution.py:249
  42.6 1.7 %collective-permute-start.18 = (f32[96,128]{1,0:T(8,128)S(1)}, f32[96,128]{1,0:T(8,128)S(1)}, u32[]{:S(2)}, u32[]{:S(2)}) collective-permute-start(f32[96,128]{1,0:T(8,128)S(1)} %add.20), channel_id=1, source_target_pairs={{0,2},{1,3},{2,0},{3,1},{4,6},{5,7},{6,4},{7,5},{8,10},{9,11},{10,... | collective-permute-start | bytes 147464 | tf_op jit(solution)/shard_map/ppermute | solution.py:249
  44.3 1.4 %collective-permute-start.15 = (bf16[128,512]{1,0:T(8,128)(2,1)S(1)}, bf16[128,512]{1,0:T(8,128)(2,1)S(1)}, u32[]{:S(2)}, u32[]{:S(2)}) collective-permute-start(bf16[128,512]{1,0:T(8,128)(2,1)S(1)} %fusion.1), channel_id=1, source_target_pairs={{0,2},{1,3},{2,0},{3,1},{4,6},{5,7},{6,4},{7,5},{8,10},{9,11},{10,... | collective-permute-start | bytes 393224 | tf_op jit(solution)/shard_map/ppermute | solution.py:249
  45.7 1.3 %shard_map.74 = (f32[128,512]{1,0:T(8,128)S(1)}, f32[128,512]{1,0:T(8,128)S(1)}) custom-call(bf16[2,16,4096]{2,1,0:T(8,128)(2,1)S(1)} %collective-permute-done.8.refs_0_, bf16[2,16,4096]{2,1,0:T(8,128)(2,1)S(1)} %collective-permute-done.9.refs_1_, bf16[2,16,4096]{2,1,0:T(8,128)(2,1)S(1)} %collective-permute-done.12.refs_2_, ...), custom_call_target="tpu_custom_call" | custom-call | flops 1073741824 | bytes 1048576 | tf_op jit(solution)/shard_map/pallas_call | solution.py:289
  46.9 2.8 %collective-permute-done.16.refs_10_ = bf16[2,128,512]{2,1,0:T(8,128)(2,1)S(1)} collective-permute-done((bf16[2,128,512]{2,1,0:T(8,128)(2,1)S(1)}, bf16[2,128,512]{2,1,0:T(8,128)(2,1)S(1)}, u32[]{:S(2)}, u32[]{:S(2)}) %collective-permute-start.16) | collective-permute-done | bytes 262176 | tf_op jit(solution)/shard_map/ppermute | solution.py:249
  51.2 2.3 %collective-permute-done.15.refs_8_ = bf16[128,512]{1,0:T(8,128)(2,1)S(1)} collective-permute-done((bf16[128,512]{1,0:T(8,128)(2,1)S(1)}, bf16[128,512]{1,0:T(8,128)(2,1)S(1)}, u32[]{:S(2)}, u32[]{:S(2)}) %collective-permute-start.15) | collective-permute-done | bytes 131104 | tf_op jit(solution)/shard_map/ppermute | solution.py:249
  53.8 1.7 %collective-permute-start.21 = (bf16[2,96,128]{2,1,0:T(8,128)(2,1)S(1)}, bf16[2,96,128]{2,1,0:T(8,128)(2,1)S(1)}, u32[]{:S(2)}, u32[]{:S(2)}) collective-permute-start(bf16[2,96,128]{2,1,0:T(8,128)(2,1)S(1)} %pad_maximum_fusion.refs_0_), channel_id=1, source_target_pairs={{0,8},{4,12},{8,0},{12,4},{16,24},{20,28},{24,16},{28,20},{1,9},{5... | collective-permute-start | bytes 147464 | tf_op jit(solution)/shard_map/ppermute | solution.py:246
  55.5 1.5 %collective-permute-start.20 = (bf16[2,96,128]{2,1,0:T(8,128)(2,1)S(1)}, bf16[2,96,128]{2,1,0:T(8,128)(2,1)S(1)}, u32[]{:S(2)}, u32[]{:S(2)}) collective-permute-start(bf16[2,96,128]{2,1,0:T(8,128)(2,1)S(1)} %pad_maximum_fusion.refs_0_), channel_id=1, source_target_pairs={{0,24},{4,28},{8,16},{12,20},{16,8},{20,12},{24,0},{28,4},{1,25},{... | collective-permute-start | bytes 147464 | tf_op jit(solution)/shard_map/ppermute | solution.py:246
  58.2 1.7 %shard_map.76.refs_3_ = f32[512,512]{1,0:T(8,128)S(1)} custom-call(bf16[2,96,128]{2,1,0:T(8,128)(2,1)S(1)} %collective-permute-done.21.refs_0_, bf16[2,96,128]{2,1,0:T(8,128)(2,1)S(1)} %collective-permute-done.22.refs_1_, bf16[64,64,512]{2,1,0:T(8,128)(2,1)S(1)} %copy-done, s32[512,8]{1,0:T(8,128)S(1)} %get-tuple-element.57.refs_7_.refs_5_.refs_2_.refs_3_, ...), custom_call_target="tpu_custom_call" | custom-call | tf_op jit(solution)/shard_map/pallas_call | solution.py:396
  (52 shorter events, 13.7 us)
Async XLA Ops:
  0.0 8.1 %collective-permute-start = (bf16[4,16,4096]{2,1,0:T(8,128)(2,1)}, bf16[4,16,4096]{2,1,0:T(8,128)(2,1)S(1)}, u32[]{:S(2)}, u32[]{:S(2)}) collective-permute-start(bf16[4,16,4096]{2,1,0:T(8,128)(2,1)} %refs_0_.2), channel_id=1, source_target_pairs={{0,4},{4,0},{8,12},{12,8},{16,20},{20,16},{24,28},{28,24},{1,5},{5... | collective-permute-start | bytes 1572872 | tf_op jit(solution)/shard_map/ppermute | solution.py:246
  0.5 17.1 %collective-permute-start.3 = (bf16[4,16,4096]{2,1,0:T(8,128)(2,1)}, bf16[4,16,4096]{2,1,0:T(8,128)(2,1)S(1)}, u32[]{:S(2)}, u32[]{:S(2)}) collective-permute-start(bf16[4,16,4096]{2,1,0:T(8,128)(2,1)} %refs_0_.2), channel_id=1, source_target_pairs={{0,8},{4,12},{8,0},{12,4},{16,24},{20,28},{24,16},{28,20},{1,9},{5... | collective-permute-start | bytes 1572872 | tf_op jit(solution)/shard_map/ppermute | solution.py:246
  3.0 14.6 %collective-permute-start.4 = (bf16[4,16,4096]{2,1,0:T(8,128)(2,1)}, bf16[4,16,4096]{2,1,0:T(8,128)(2,1)S(1)}, u32[]{:S(2)}, u32[]{:S(2)}) collective-permute-start(bf16[4,16,4096]{2,1,0:T(8,128)(2,1)} %refs_0_.2), channel_id=1, source_target_pairs={{0,16},{4,20},{8,24},{12,28},{16,0},{20,4},{24,8},{28,12},{1,17},{... | collective-permute-start | bytes 1572872 | tf_op jit(solution)/shard_map/ppermute | solution.py:246
  9.4 8.2 %collective-permute-start.1 = (bf16[2,128,512]{2,1,0:T(8,128)(2,1)S(1)}, bf16[2,128,512]{2,1,0:T(8,128)(2,1)S(1)}, u32[]{:S(2)}, u32[]{:S(2)}) collective-permute-start(bf16[2,128,512]{2,1,0:T(8,128)(2,1)S(1)} %shard_map.65), channel_id=1, source_target_pairs={{0,1},{1,0},{2,3},{3,2},{4,5},{5,4},{6,7},{7,6},{8,9},{9,8},{10,11... | collective-permute-start | bytes 786440 | tf_op jit(solution)/shard_map/ppermute | solution.py:249
  17.6 4.9 %collective-permute-start.5 = (bf16[4,16,4096]{2,1,0:T(8,128)(2,1)S(1)}, bf16[4,16,4096]{2,1,0:T(8,128)(2,1)S(1)}, u32[]{:S(2)}, u32[]{:S(2)}) collective-permute-start(bf16[4,16,4096]{2,1,0:T(8,128)(2,1)S(1)} %collective-permute-done.3.refs_0_.refs_2_), channel_id=1, source_target_pairs={{0,4},{4,0},{8,12},{12,8},{16,20},{20,16},{24,28},{28,24},{1,5},{5... | collective-permute-start | bytes 1572872 | tf_op jit(solution)/shard_map/ppermute | solution.py:246
  17.7 7.7 %collective-permute-start.6 = (bf16[4,16,4096]{2,1,0:T(8,128)(2,1)S(1)}, bf16[4,16,4096]{2,1,0:T(8,128)(2,1)S(1)}, u32[]{:S(2)}, u32[]{:S(2)}) collective-permute-start(bf16[4,16,4096]{2,1,0:T(8,128)(2,1)S(1)} %collective-permute-done.4.refs_0_.refs_4_), channel_id=1, source_target_pairs={{0,4},{4,0},{8,12},{12,8},{16,20},{20,16},{24,28},{28,24},{1,5},{5... | collective-permute-start | bytes 1572872 | tf_op jit(solution)/shard_map/ppermute | solution.py:246
  18.2 14.5 %collective-permute-start.2 = (bf16[128,512]{1,0:T(8,128)(2,1)S(1)}, bf16[128,512]{1,0:T(8,128)(2,1)S(1)}, u32[]{:S(2)}, u32[]{:S(2)}) collective-permute-start(bf16[128,512]{1,0:T(8,128)(2,1)S(1)} %fusion.3), channel_id=1, source_target_pairs={{0,2},{1,3},{2,0},{3,1},{4,6},{5,7},{6,4},{7,5},{8,10},{9,11},{10,... | collective-permute-start | bytes 393224 | tf_op jit(solution)/shard_map/ppermute | solution.py:249
  20.8 8.9 %collective-permute-start.9 = (bf16[2,16,4096]{2,1,0:T(8,128)(2,1)S(1)}, bf16[2,16,4096]{2,1,0:T(8,128)(2,1)S(1)}, u32[]{:S(2)}, u32[]{:S(2)}) collective-permute-start(bf16[2,16,4096]{2,1,0:T(8,128)(2,1)S(1)} %slice.20), channel_id=1, source_target_pairs={{0,8},{4,12},{8,0},{12,4},{16,24},{20,28},{24,16},{28,20},{1,9},{5... | collective-permute-start | bytes 786440 | tf_op jit(solution)/shard_map/ppermute | solution.py:246
  21.4 8.3 %collective-permute-start.8 = (bf16[2,16,4096]{2,1,0:T(8,128)(2,1)S(1)}, bf16[2,16,4096]{2,1,0:T(8,128)(2,1)S(1)}, u32[]{:S(2)}, u32[]{:S(2)}) collective-permute-start(bf16[2,16,4096]{2,1,0:T(8,128)(2,1)S(1)} %slice.19), channel_id=1, source_target_pairs={{0,16},{4,20},{8,24},{12,28},{16,0},{20,4},{24,8},{28,12},{1,17},{... | collective-permute-start | bytes 786440 | tf_op jit(solution)/shard_map/ppermute | solution.py:246
  23.8 9.3 %collective-permute-start.7 = (bf16[2,128,512]{2,1,0:T(8,128)(2,1)S(1)}, bf16[2,128,512]{2,1,0:T(8,128)(2,1)S(1)}, u32[]{:S(2)}, u32[]{:S(2)}) collective-permute-start(bf16[2,128,512]{2,1,0:T(8,128)(2,1)S(1)} %shard_map.67), channel_id=1, source_target_pairs={{0,1},{1,0},{2,3},{3,2},{4,5},{5,4},{6,7},{7,6},{8,9},{9,8},{10,11... | collective-permute-start | bytes 786440 | tf_op jit(solution)/shard_map/ppermute | solution.py:249
  26.7 17.6 %collective-permute-start.11 = (bf16[2,128,512]{2,1,0:T(8,128)(2,1)S(1)}, bf16[2,128,512]{2,1,0:T(8,128)(2,1)S(1)}, u32[]{:S(2)}, u32[]{:S(2)}) collective-permute-start(bf16[2,128,512]{2,1,0:T(8,128)(2,1)S(1)} %shard_map.68), channel_id=1, source_target_pairs={{0,1},{1,0},{2,3},{3,2},{4,5},{5,4},{6,7},{7,6},{8,9},{9,8},{10,11... | collective-permute-start | bytes 786440 | tf_op jit(solution)/shard_map/ppermute | solution.py:249
  29.7 5.1 %collective-permute-start.12 = (bf16[2,16,4096]{2,1,0:T(8,128)(2,1)S(1)}, bf16[2,16,4096]{2,1,0:T(8,128)(2,1)S(1)}, u32[]{:S(2)}, u32[]{:S(2)}) collective-permute-start(bf16[2,16,4096]{2,1,0:T(8,128)(2,1)S(1)} %collective-permute-done.8.refs_0_), channel_id=1, source_target_pairs={{0,4},{4,0},{8,12},{12,8},{16,20},{20,16},{24,28},{28,24},{1,5},{5... | collective-permute-start | bytes 786440 | tf_op jit(solution)/shard_map/ppermute | solution.py:246
  29.8 5.0 %collective-permute-start.13 = (bf16[2,16,4096]{2,1,0:T(8,128)(2,1)S(1)}, bf16[2,16,4096]{2,1,0:T(8,128)(2,1)S(1)}, u32[]{:S(2)}, u32[]{:S(2)}) collective-permute-start(bf16[2,16,4096]{2,1,0:T(8,128)(2,1)S(1)} %collective-permute-done.9.refs_1_), channel_id=1, source_target_pairs={{0,4},{4,0},{8,12},{12,8},{16,20},{20,16},{24,28},{28,24},{1,5},{5... | collective-permute-start | bytes 786440 | tf_op jit(solution)/shard_map/ppermute | solution.py:246
  33.1 9.5 %collective-permute-start.10 = (bf16[128,512]{1,0:T(8,128)(2,1)S(1)}, bf16[128,512]{1,0:T(8,128)(2,1)S(1)}, u32[]{:S(2)}, u32[]{:S(2)}) collective-permute-start(bf16[128,512]{1,0:T(8,128)(2,1)S(1)} %fusion.2), channel_id=1, source_target_pairs={{0,2},{1,3},{2,0},{3,1},{4,6},{5,7},{6,4},{7,5},{8,10},{9,11},{10,... | collective-permute-start | bytes 393224 | tf_op jit(solution)/shard_map/ppermute | solution.py:249
  36.1 21.0 %copy-start = (bf16[64,64,512]{2,1,0:T(8,128)(2,1)S(1)}, bf16[64,64,512]{2,1,0:T(8,128)(2,1)}, u32[]{:S(2)}) copy-start(bf16[64,64,512]{2,1,0:T(8,128)(2,1)} %refs_1_.3) | copy-start | bytes 12582916
  36.1 6.5 %collective-permute-start.14 = (f32[96,128]{1,0:T(8,128)S(1)}, f32[96,128]{1,0:T(8,128)S(1)}, u32[]{:S(2)}, u32[]{:S(2)}) collective-permute-start(f32[96,128]{1,0:T(8,128)S(1)} %shard_map.72), channel_id=1, source_target_pairs={{0,1},{1,0},{2,3},{3,2},{4,5},{5,4},{6,7},{7,6},{8,9},{9,8},{10,11... | collective-permute-start | bytes 147464 | tf_op jit(solution)/shard_map/ppermute | solution.py:249
  40.1 9.7 %collective-permute-start.16 = (bf16[2,128,512]{2,1,0:T(8,128)(2,1)S(1)}, bf16[2,128,512]{2,1,0:T(8,128)(2,1)S(1)}, u32[]{:S(2)}, u32[]{:S(2)}) collective-permute-start(bf16[2,128,512]{2,1,0:T(8,128)(2,1)S(1)} %shard_map.73), channel_id=1, source_target_pairs={{0,1},{1,0},{2,3},{3,2},{4,5},{5,4},{6,7},{7,6},{8,9},{9,8},{10,11... | collective-permute-start | bytes 786440 | tf_op jit(solution)/shard_map/ppermute | solution.py:249
  42.6 7.5 %collective-permute-start.18 = (f32[96,128]{1,0:T(8,128)S(1)}, f32[96,128]{1,0:T(8,128)S(1)}, u32[]{:S(2)}, u32[]{:S(2)}) collective-permute-start(f32[96,128]{1,0:T(8,128)S(1)} %add.20), channel_id=1, source_target_pairs={{0,2},{1,3},{2,0},{3,1},{4,6},{5,7},{6,4},{7,5},{8,10},{9,11},{10,... | collective-permute-start | bytes 147464 | tf_op jit(solution)/shard_map/ppermute | solution.py:249
  44.3 9.1 %collective-permute-start.15 = (bf16[128,512]{1,0:T(8,128)(2,1)S(1)}, bf16[128,512]{1,0:T(8,128)(2,1)S(1)}, u32[]{:S(2)}, u32[]{:S(2)}) collective-permute-start(bf16[128,512]{1,0:T(8,128)(2,1)S(1)} %fusion.1), channel_id=1, source_target_pairs={{0,2},{1,3},{2,0},{3,1},{4,6},{5,7},{6,4},{7,5},{8,10},{9,11},{10,... | collective-permute-start | bytes 393224 | tf_op jit(solution)/shard_map/ppermute | solution.py:249
  50.1 3.3 %collective-permute-start.19 = (bf16[1,96,128]{2,1,0:T(8,128)(2,1)S(1)}, bf16[1,96,128]{2,1,0:T(8,128)(2,1)S(1)}, u32[]{:S(2)}, u32[]{:S(2)}) collective-permute-start(bf16[1,96,128]{2,1,0:T(8,128)(2,1)S(1)} %fusion.4), channel_id=1, source_target_pairs={{0,4},{4,0},{8,12},{12,8},{16,20},{20,16},{24,28},{28,24},{1,5},{5... | collective-permute-start | bytes 73736 | tf_op jit(solution)/shard_map/ppermute | solution.py:246
  50.2 11.5 %collective-permute-start.17 = (bf16[128,512]{1,0:T(8,128)(2,1)S(1)}, bf16[128,512]{1,0:T(8,128)(2,1)S(1)}, u32[]{:S(2)}, u32[]{:S(2)}) collective-permute-start(bf16[128,512]{1,0:T(8,128)(2,1)S(1)} %fusion), channel_id=1, source_target_pairs={{0,2},{1,3},{2,0},{3,1},{4,6},{5,7},{6,4},{7,5},{8,10},{9,11},{10,... | collective-permute-start | bytes 393224 | tf_op jit(solution)/shard_map/ppermute | solution.py:249
  53.5 4.7 %collective-permute-start.22 = (bf16[2,96,128]{2,1,0:T(8,128)(2,1)S(1)}, bf16[2,96,128]{2,1,0:T(8,128)(2,1)S(1)}, u32[]{:S(2)}, u32[]{:S(2)}) collective-permute-start(bf16[2,96,128]{2,1,0:T(8,128)(2,1)S(1)} %pad_maximum_fusion.refs_0_), channel_id=1, source_target_pairs={{0,16},{4,20},{8,24},{12,28},{16,0},{20,4},{24,8},{28,12},{1,17},{... | collective-permute-start | bytes 147464 | tf_op jit(solution)/shard_map/ppermute | solution.py:246
  53.8 4.4 %collective-permute-start.21 = (bf16[2,96,128]{2,1,0:T(8,128)(2,1)S(1)}, bf16[2,96,128]{2,1,0:T(8,128)(2,1)S(1)}, u32[]{:S(2)}, u32[]{:S(2)}) collective-permute-start(bf16[2,96,128]{2,1,0:T(8,128)(2,1)S(1)} %pad_maximum_fusion.refs_0_), channel_id=1, source_target_pairs={{0,8},{4,12},{8,0},{12,4},{16,24},{20,28},{24,16},{28,20},{1,9},{5... | collective-permute-start | bytes 147464 | tf_op jit(solution)/shard_map/ppermute | solution.py:246
  55.5 5.0 %collective-permute-start.20 = (bf16[2,96,128]{2,1,0:T(8,128)(2,1)S(1)}, bf16[2,96,128]{2,1,0:T(8,128)(2,1)S(1)}, u32[]{:S(2)}, u32[]{:S(2)}) collective-permute-start(bf16[2,96,128]{2,1,0:T(8,128)(2,1)S(1)} %pad_maximum_fusion.refs_0_), channel_id=1, source_target_pairs={{0,24},{4,28},{8,16},{12,20},{16,8},{20,12},{24,0},{28,4},{1,25},{... | collective-permute-start | bytes 147464 | tf_op jit(solution)/shard_map/ppermute | solution.py:246
  (2 other events, 11.0 us)
